TPU v7x, 256 devices: a whole 4x4x8 slice. The times are simulated.
256 devices in a mesh: space: 32 (over x, y, z_lo), chan: 8 (over z_hi, core).
Axes of the slice: x: 4, y: 4, z: 8 (z_hi: 4, z_lo: 2; z = z_hi * 2 + z_lo), core: 2. Of those that a mesh axis runs over, the one named last changes fastest.
Arguments:
- volume: bfloat16 [128, 128, 1024], P('chan', 'space'), may hold values from -6 to 6
- conv_in: bfloat16 [27, 256, 128], P(None, 'chan'), may hold values from -0.109375 to 0.109375
- conv_group: bfloat16 [27, 256, 8], P(None, 'chan'), may hold values from -0.4375 to 0.4375
- cotangent: bfloat16 [256, 64, 256], P('chan', 'space'), may hold values from -6 to 6
Outputs:
- mixed_out: bfloat16 [256, 64, 256], P('chan', 'space')
- input_grad: float32 [128, 128, 1024], P('chan', 'space')
- filter_grad: float32 [27, 256, 128], P(None, 'chan')
- group_grad: float32 [27, 256, 8], P(None, 'chan')
All inputs are finite; a program needn't handle non-finite values.
Results may differ from a plain program's by a relative error of at most 0.005.
Values may be sent and summed in bfloat16 or wider, within the bound.
No kernel may reach another device: no remote copies, remote signals or barrier semaphores. Data moves between devices by JAX's collectives and lax.ppermute only.
A program may use at most 64 MiB of HBM per device.

v0:
```python
import math

import jax
import jax.numpy as jnp
from jax import lax
from jax.sharding import PartitionSpec as P

OFFSETS = [
    (first, second, third) for first in (-1, 0, 1) for second in (-1, 0, 1) for third in (-1, 0, 1)
]


def passed_along(block, axis, distance):
    devices = range(lax.axis_size(axis))
    route = [((i - distance) % len(devices), i) for i in devices]
    return lax.ppermute(block, axis, route)


def padded(block, sides, width):
    for axis, dim in sides:
        count = lax.axis_size(axis)
        forward = [(i, i + 1) for i in range(count - 1)]
        forward.append((count - 1, 0))
        backward = [(target, source) for source, target in forward]
        low = lax.ppermute(
            lax.slice_in_dim(block, block.shape[dim] - width, None, axis=dim), axis, forward
        )
        high = lax.ppermute(lax.slice_in_dim(block, 0, width, axis=dim), axis, backward)
        block = jnp.concatenate([low, block, high], axis=dim)
    return block


def roll_cells(flat, row_k, col_k, side):
    moved = flat
    if row_k != 0:
        moved = jnp.roll(moved, -row_k * side, moved.ndim - 1)
    if col_k != 0:
        inside = jnp.roll(moved, -col_k, moved.ndim - 1)
        wrapped = jnp.roll(moved, col_k * (side - 1), moved.ndim - 1)
        column = lax.broadcasted_iota(jnp.int32, (moved.shape[-1],), 0) % side
        edge = column == (side - 1 if col_k > 0 else 0)
        moved = jnp.where(edge, wrapped, inside)
    return moved


def pick_slice(values, dim_index, offset, count):
    return lax.slice_in_dim(values, offset + 1, offset + 2 * count, 2, dim_index)


def phase_of(offset):
    return 0 if offset == 0 else 1


def pad_block(contrib, dim_index, offset):
    lower_pad = (offset + 1) // 2
    widths = [(0, 0)] * contrib.ndim
    widths[dim_index] = (lower_pad, 1 - lower_pad)
    return (jnp.pad(contrib, widths), (offset + 1) % 2)


def alternate(phase_sums):
    depth_parts = []
    for depth_phase in (0, 1):
        depth_parts.append(
            jnp.concatenate(
                [
                    phase_sums[depth_phase, row_phase, col_phase]
                    for row_phase in (0, 1)
                    for col_phase in (0, 1)
                ],
                2,
            )
        )
    stacked = jnp.stack(depth_parts, 2)
    shape = stacked.shape
    return stacked.reshape(shape[0], 2 * shape[1], shape[3])


def silu_grad(hidden):
    sigmoid_val = jax.nn.sigmoid(hidden)
    return sigmoid_val * (1.0 + hidden * (1.0 - sigmoid_val))


def contract_last(left, right):
    return lax.dot_general(
        left, right, (((1,), (1,)), ((), ())), preferred_element_type=jnp.float32
    )


def contract_first(left, right):
    return lax.dot_general(
        left, right, (((0,), (0,)), ((), ())), preferred_element_type=jnp.float32
    )


def strided_view(source, depth_k, row_k, col_k, planes, channels, side_out):
    square = side_out * side_out
    picked = pick_slice(source, 1, depth_k, planes)
    segment = (2 * phase_of(row_k) + phase_of(col_k)) * square
    picked = lax.slice_in_dim(picked, segment, segment + square, 1, 2)
    picked = roll_cells(picked, min(row_k, 0), min(col_k, 0), side_out)
    return picked.reshape(channels, planes * square)


def body(volume, conv_in, conv_group, cotangent):
    in_chan, in_planes, flat_in = volume.shape
    side_in = math.isqrt(flat_in)
    planes = in_planes // 2
    side_out = side_in // 2
    square = side_out * side_out
    cell_count = planes * square
    out_chan = conv_in.shape[1]
    all_in = conv_in.shape[2]
    group_width = conv_group.shape[2]
    groups_here = out_chan // group_width
    columns = lax.all_to_all(conv_in, "chan", split_axis=2, concat_axis=1, tiled=True)
    neighbour = passed_along(volume[:, in_planes - 1 :], "space", 1)
    extended = jnp.concatenate([neighbour, volume], 1)
    gathered = lax.all_gather(extended, "chan", axis=0, tiled=True)

    def slab_view(depth_k, row_k, col_k):
        return strided_view(gathered, depth_k, row_k, col_k, planes, all_in, side_out)

    hidden = jnp.zeros((out_chan, cell_count), jnp.float32)
    for tap_index, offsets in enumerate(OFFSETS):
        hidden = hidden + jnp.dot(
            conv_in[tap_index], slab_view(*offsets), preferred_element_type=jnp.float32
        )
    active = (hidden * jax.nn.sigmoid(hidden)).astype(jnp.bfloat16)
    shaped = active.reshape(out_chan, planes, square)
    act_rim = padded(shaped, (("space", 1),), 1)
    up_rim = padded(cotangent, (("space", 1),), 1)
    flat_up = cotangent.reshape(groups_here, group_width, cell_count)

    def unit_tap(rimmed, depth_k, row_k, col_k, direction):
        shifted = lax.slice_in_dim(
            rimmed, 1 + direction * depth_k, 1 + direction * depth_k + planes, 1, 1
        )
        shifted = roll_cells(shifted, direction * row_k, direction * col_k, side_out)
        return shifted.reshape(groups_here, group_width, cell_count)

    mixed = jnp.zeros((groups_here, group_width, cell_count), jnp.float32)
    act_grad = jnp.zeros((groups_here, group_width, cell_count), jnp.float32)
    group_terms = []
    for tap_index, (depth_k, row_k, col_k) in enumerate(OFFSETS):
        weights = conv_group[tap_index].reshape(groups_here, group_width, group_width)
        shifted = unit_tap(act_rim, depth_k, row_k, col_k, 1)
        mixed = mixed + jnp.einsum(
            "goi,gic->goc", weights, shifted, preferred_element_type=jnp.float32
        )
        backward_view = unit_tap(up_rim, depth_k, row_k, col_k, -1)
        act_grad = act_grad + jnp.einsum(
            "goi,goc->gic", weights, backward_view, preferred_element_type=jnp.float32
        )
        group_terms.append(
            jnp.einsum(
                "goc,gic->goi", flat_up, shifted, preferred_element_type=jnp.float32
            ).reshape(out_chan, group_width)
        )
    mixed_out = mixed.reshape(out_chan, planes, square).astype(jnp.bfloat16)
    hidden_grad = (act_grad.reshape(out_chan, cell_count) * silu_grad(hidden)).astype(jnp.bfloat16)
    grad_all = lax.all_gather(hidden_grad, "chan", axis=0, tiled=True)
    filter_terms = []
    phase_sums = {}
    for tap_index, (depth_k, row_k, col_k) in enumerate(OFFSETS):
        filter_terms.append(contract_last(hidden_grad, slab_view(depth_k, row_k, col_k)))
        contrib = contract_first(columns[tap_index], grad_all).reshape(in_chan, planes, square)
        contrib, depth_phase = pad_block(contrib, 1, depth_k)
        contrib = roll_cells(contrib, 1 if row_k < 0 else 0, 1 if col_k < 0 else 0, side_out)
        slot_key = (depth_phase, phase_of(row_k), phase_of(col_k))
        phase_sums[slot_key] = phase_sums[slot_key] + contrib if slot_key in phase_sums else contrib
    framed_grad = alternate(phase_sums)[:, : in_planes + 1]
    returned = passed_along(framed_grad[:, :1].astype(jnp.bfloat16), "space", -1).astype(
        jnp.float32
    )
    input_grad = framed_grad[:, 1:].at[:, in_planes - 1 :].add(returned)
    filter_part = jnp.stack(filter_terms)
    filter_sum, group_sum = lax.psum((filter_part, jnp.stack(group_terms)), "space")
    inverse_root = 1.0 / math.sqrt(lax.axis_size("space") * cell_count)
    return (mixed_out, input_grad, filter_sum * inverse_root, group_sum * inverse_root)


def solution(mesh):
    return jax.shard_map(
        body,
        mesh=mesh,
        in_specs=(
            P("chan", "space", None),
            P(None, "chan", None),
            P(None, "chan", None),
            P("chan", "space", None),
        ),
        out_specs=(
            P("chan", "space", None),
            P("chan", "space", None),
            P(None, "chan", None),
            P(None, "chan", None),
        ),
        check_vma=False,
    )
```

profile of v0, /device:TPU:62, one launch (start us, length us, event | category | flops | bytes accessed | tf_op | source)
XLA Modules:
  0.0 520.8 jit_solution(12840757592983608004)
XLA Ops:
  8.1 1.5 collective-permute-start.4
  11.1 5.7 %collective-permute-start = (bf16[16,1,1024]{2,0,1:T(8,128)(2,1)S(1)}, bf16[16,1,1024]{2,0,1:T(8,128)(2,1)S(1)}, u32[]{:S(2)}, u32[]{:S(2)}) collective-permute-start(bf16[16,1,1024]{2,0,1:T(8,128)(2,1)S(1)} %slice.2030), channel_id=1, source_target_pairs={{248,0},{0,8},{8,16},{16,24},{24,32},{32,40},{40,48},{48,56},{56,6... | collective-permute-start | bytes 98312 | tf_op jit(solution)/shard_map/ppermute | solution.py:16
  16.9 2.3 copy.262
  19.2 1.4 reshape.860
  20.6 6.7 %all-to-all-start = ((bf16[8,2,6912]{2,1,0:T(2,128)(2,1)}), bf16[8,2,6912]{2,1,0:T(2,128)(2,1)S(1)}, u32[]{:S(2)}, u32[]{:S(2)}) async-start(bf16[8,2,6912]{2,1,0:T(2,128)(2,1)} %reshape.860), calls=%async_computation | async-start | bytes 442368 | tf_op jit(solution)/shard_map/all_to_all | solution.py:116
  68.0 10.5 %all-gather.2.cloned.1.call-done = bf16[128,5,1024]{2,0,1:T(8,128)(2,1)} async-done(((bf16[16,5,1024]{2,0,1:T(8,128)(2,1)}), bf16[128,5,1024]{2,0,1:T(8,128)(2,1)}) %all-gather.2.cloned.1.call-update) | async-done | bytes 1310736 | tf_op jit(solution)/shard_map/all_gather | solution.py:119
  78.4 1.5 fusion.344
  93.1 1.6 copy.379
  97.5 1.5 copy.389
  99.0 1.5 copy.383
  100.7 1.6 copy.417
  102.2 1.5 copy.398
  103.7 1.6 copy.380
  105.4 1.7 broadcast_select_fusion.8
  110.0 1.1 copy.385
  116.8 1.5 copy.427
  118.3 1.5 copy.421
  119.8 1.5 copy.416
  121.3 1.5 copy.397
  122.8 1.5 copy.402
  124.3 1.5 copy.408
  127.3 1.7 copy.425
  129.0 1.7 copy.419
  130.6 1.7 copy.400
  139.0 2.6 broadcast_select_fusion
  143.2 1.4 broadcast_select_fusion.1
  148.1 14.8 %all_gather.7 = bf16[256,512]{1,0:T(8,128)(2,1)S(1)} all-gather(bf16[32,512]{1,0:T(8,128)(2,1)S(1)} %fusion.39), channel_id=1, replica_groups=mesh['space'=32,'chan'=8] {'chan'}, dimensions={0}, use_global_device_ids=true | all-gather | bytes 294912 | tf_op jit(solution)/shard_map/all_gather | solution.py:162
  196.9 1.1 collective-permute-start.2
  198.0 5.1 collective-permute-start.1
  234.2 153.0 %psum.15 = f32[27,32,8]{1,2,0:T(8,128)S(1)} all-reduce(f32[27,32,8]{1,2,0:T(8,128)S(1)} %constant_dynamic-update-slice_fusion), channel_id=1, replica_groups=mesh['space'=32,'chan'=8] {'space'}, use_global_device_ids=true, to_apply=%region_1.2 | all-reduce | flops 6912 | bytes 55296 | tf_op jit(solution)/shard_map/psum | solution.py:178
  389.5 122.5 %all-reduce.29.cloned.1.call-done = f32[27,32,128]{2,1,0:T(8,128)} async-done(((f32[27,32,128]{2,1,0:T(8,128)}), f32[27,32,128]{2,1,0:T(8,128)}) %all-reduce.29.cloned.1.call-update) | async-done | bytes 442384 | tf_op jit(solution)/shard_map/psum | solution.py:178
  512.0 1.8 broadcast_multiply_fusion
  (1055 shorter events, 144.8 us)
Async XLA Ops:
  8.1 22.8 %collective-permute-start.4 = (bf16[32,1,256]{2,1,0:T(2,128)(2,1)S(1)}, bf16[32,1,256]{2,1,0:T(2,128)(2,1)S(1)}, u32[]{:S(2)}, u32[]{:S(2)}) collective-permute-start(bf16[32,1,256]{2,1,0:T(2,128)(2,1)S(1)} %get-tuple-element.324), channel_id=1, source_target_pairs={{0,8},{8,16},{16,24},{24,32},{32,40},{40,48},{48,56},{56,64},{64,7... | collective-permute-start | bytes 49160 | tf_op jit(solution)/shard_map/ppermute | solution.py:25
  9.6 21.3 %collective-permute-start.3 = (bf16[32,1,256]{2,1,0:T(2,128)(2,1)S(1)}, bf16[32,1,256]{2,1,0:T(2,128)(2,1)S(1)}, u32[]{:S(2)}, u32[]{:S(2)}) collective-permute-start(bf16[32,1,256]{2,1,0:T(2,128)(2,1)S(1)} %get-tuple-element.325), channel_id=1, source_target_pairs={{8,0},{16,8},{24,16},{32,24},{40,32},{48,40},{56,48},{64,56},{72,6... | collective-permute-start | bytes 49160 | tf_op jit(solution)/shard_map/ppermute | solution.py:28
  11.1 34.3 %collective-permute-start = (bf16[16,1,1024]{2,0,1:T(8,128)(2,1)S(1)}, bf16[16,1,1024]{2,0,1:T(8,128)(2,1)S(1)}, u32[]{:S(2)}, u32[]{:S(2)}) collective-permute-start(bf16[16,1,1024]{2,0,1:T(8,128)(2,1)S(1)} %slice.2030), channel_id=1, source_target_pairs={{248,0},{0,8},{8,16},{16,24},{24,32},{32,40},{40,48},{48,56},{56,6... | collective-permute-start | bytes 98312 | tf_op jit(solution)/shard_map/ppermute | solution.py:16
  20.6 28.3 %all-to-all-start = ((bf16[8,2,6912]{2,1,0:T(2,128)(2,1)}), bf16[8,2,6912]{2,1,0:T(2,128)(2,1)S(1)}, u32[]{:S(2)}, u32[]{:S(2)}) async-start(bf16[8,2,6912]{2,1,0:T(2,128)(2,1)} %reshape.860), calls=%async_computation | async-start | bytes 442368 | tf_op jit(solution)/shard_map/all_to_all | solution.py:116
  27.3 51.1 %all-gather.2.cloned.1.call-start = ((), (), s32[]{:S(2)}) async-start(), calls=%async_computation.1 | async-start | bytes 1474560 | tf_op jit(solution)/shard_map/all_gather | solution.py:119
  27.7 77.7 %copy-start.167 = (pred[256]{0:T(512)(128)(4,1)}, pred[256]{0:T(512)(128)(4,1)S(1)}, u32[]{:S(2)}) copy-start(pred[256]{0:T(512)(128)(4,1)S(1)} %broadcast_compare_fusion) | copy-start | bytes 772
  46.2 465.7 %all-reduce.29.cloned.1.call-start = ((), (), s32[]{:S(2)}) async-start(), calls=%async_computation.2 | async-start | bytes 884736 | tf_op jit(solution)/shard_map/psum | solution.py:178
  109.9 22.4 %copy-start.13 = (bf16[128,2,241]{2,0,1:T(8,128)(2,1)S(1)}, bf16[128,2,241]{2,0,1:T(8,128)(2,1)}, u32[]{:S(2)}) copy-start(bf16[128,2,241]{2,0,1:T(8,128)(2,1)} %get-tuple-element.394) | copy-start | bytes 370180
  111.0 22.0 %copy-start.12 = (bf16[128,2,255]{2,0,1:T(8,128)(2,1)S(1)}, bf16[128,2,255]{2,0,1:T(8,128)(2,1)}, u32[]{:S(2)}) copy-start(bf16[128,2,255]{2,0,1:T(8,128)(2,1)} %get-tuple-element.93) | copy-start | bytes 391684
  147.8 20.8 %copy-start.159 = (bf16[256,16]{0,1:T(8,128)(2,1)S(1)}, bf16[256,16]{0,1:T(8,128)(2,1)}, u32[]{:S(2)}) copy-start(bf16[256,16]{0,1:T(8,128)(2,1)} %squeeze.214) | copy-start | bytes 24580
  182.6 20.5 %copy-start.14 = (bf16[128,2,256]{0,2,1:T(8,128)(2,1)S(1)}, bf16[128,2,256]{0,2,1:T(8,128)(2,1)}, u32[]{:S(2)}) copy-start(bf16[128,2,256]{0,2,1:T(8,128)(2,1)} %get-tuple-element.25) | copy-start | bytes 393220
  182.6 20.5 %copy-start.15 = (bf16[128,2,256]{0,2,1:T(8,128)(2,1)S(1)}, bf16[128,2,256]{0,2,1:T(8,128)(2,1)}, u32[]{:S(2)}) copy-start(bf16[128,2,256]{0,2,1:T(8,128)(2,1)} %get-tuple-element.26) | copy-start | bytes 393220
  182.6 20.5 %copy-start.16 = (bf16[128,2,256]{0,2,1:T(8,128)(2,1)S(1)}, bf16[128,2,256]{0,2,1:T(8,128)(2,1)}, u32[]{:S(2)}) copy-start(bf16[128,2,256]{0,2,1:T(8,128)(2,1)} %get-tuple-element.370) | copy-start | bytes 393220
  182.6 20.5 %copy-start.17 = (bf16[128,2,256]{0,2,1:T(8,128)(2,1)S(1)}, bf16[128,2,256]{0,2,1:T(8,128)(2,1)}, u32[]{:S(2)}) copy-start(bf16[128,2,256]{0,2,1:T(8,128)(2,1)} %get-tuple-element.371) | copy-start | bytes 393220
  182.6 20.5 %copy-start.18 = (bf16[128,2,256]{0,2,1:T(8,128)(2,1)S(1)}, bf16[128,2,256]{0,2,1:T(8,128)(2,1)}, u32[]{:S(2)}) copy-start(bf16[128,2,256]{0,2,1:T(8,128)(2,1)} %get-tuple-element.373) | copy-start | bytes 393220
  182.6 20.5 %copy-start.19 = (bf16[128,2,256]{0,2,1:T(8,128)(2,1)S(1)}, bf16[128,2,256]{0,2,1:T(8,128)(2,1)}, u32[]{:S(2)}) copy-start(bf16[128,2,256]{0,2,1:T(8,128)(2,1)} %get-tuple-element.374) | copy-start | bytes 393220
  182.7 20.5 %copy-start.20 = (bf16[128,2,256]{0,2,1:T(8,128)(2,1)S(1)}, bf16[128,2,256]{0,2,1:T(8,128)(2,1)}, u32[]{:S(2)}) copy-start(bf16[128,2,256]{0,2,1:T(8,128)(2,1)} %get-tuple-element.376) | copy-start | bytes 393220
  182.7 20.5 %copy-start.21 = (bf16[128,2,256]{0,2,1:T(8,128)(2,1)S(1)}, bf16[128,2,256]{0,2,1:T(8,128)(2,1)}, u32[]{:S(2)}) copy-start(bf16[128,2,256]{0,2,1:T(8,128)(2,1)} %get-tuple-element.377) | copy-start | bytes 393220
  182.7 20.5 %copy-start.22 = (bf16[128,2,256]{0,2,1:T(8,128)(2,1)S(1)}, bf16[128,2,256]{0,2,1:T(8,128)(2,1)}, u32[]{:S(2)}) copy-start(bf16[128,2,256]{0,2,1:T(8,128)(2,1)} %get-tuple-element.28) | copy-start | bytes 393220
  182.7 20.5 %copy-start.23 = (bf16[128,2,256]{0,2,1:T(8,128)(2,1)S(1)}, bf16[128,2,256]{0,2,1:T(8,128)(2,1)}, u32[]{:S(2)}) copy-start(bf16[128,2,256]{0,2,1:T(8,128)(2,1)} %get-tuple-element.29) | copy-start | bytes 393220
  182.7 20.5 %copy-start.24 = (bf16[128,2,256]{0,2,1:T(8,128)(2,1)S(1)}, bf16[128,2,256]{0,2,1:T(8,128)(2,1)}, u32[]{:S(2)}) copy-start(bf16[128,2,256]{0,2,1:T(8,128)(2,1)} %get-tuple-element.379) | copy-start | bytes 393220
  182.7 20.5 %copy-start.25 = (bf16[128,2,256]{0,2,1:T(8,128)(2,1)S(1)}, bf16[128,2,256]{0,2,1:T(8,128)(2,1)}, u32[]{:S(2)}) copy-start(bf16[128,2,256]{0,2,1:T(8,128)(2,1)} %get-tuple-element.380) | copy-start | bytes 393220
  182.7 20.5 %copy-start.26 = (bf16[128,2,256]{0,2,1:T(8,128)(2,1)S(1)}, bf16[128,2,256]{0,2,1:T(8,128)(2,1)}, u32[]{:S(2)}) copy-start(bf16[128,2,256]{0,2,1:T(8,128)(2,1)} %get-tuple-element.382) | copy-start | bytes 393220
  182.7 20.5 %copy-start.27 = (bf16[128,2,256]{0,2,1:T(8,128)(2,1)S(1)}, bf16[128,2,256]{0,2,1:T(8,128)(2,1)}, u32[]{:S(2)}) copy-start(bf16[128,2,256]{0,2,1:T(8,128)(2,1)} %get-tuple-element.383) | copy-start | bytes 393220
  182.7 20.5 %copy-start.28 = (bf16[128,2,256]{0,2,1:T(8,128)(2,1)S(1)}, bf16[128,2,256]{0,2,1:T(8,128)(2,1)}, u32[]{:S(2)}) copy-start(bf16[128,2,256]{0,2,1:T(8,128)(2,1)} %get-tuple-element.385) | copy-start | bytes 393220
  182.8 20.5 %copy-start.29 = (bf16[128,2,256]{0,2,1:T(8,128)(2,1)S(1)}, bf16[128,2,256]{0,2,1:T(8,128)(2,1)}, u32[]{:S(2)}) copy-start(bf16[128,2,256]{0,2,1:T(8,128)(2,1)} %get-tuple-element.386) | copy-start | bytes 393220
  182.8 20.5 %copy-start.30 = (bf16[128,2,256]{0,2,1:T(8,128)(2,1)S(1)}, bf16[128,2,256]{0,2,1:T(8,128)(2,1)}, u32[]{:S(2)}) copy-start(bf16[128,2,256]{0,2,1:T(8,128)(2,1)} %get-tuple-element.49) | copy-start | bytes 393220
  182.8 20.5 %copy-start.31 = (bf16[128,2,256]{0,2,1:T(8,128)(2,1)S(1)}, bf16[128,2,256]{0,2,1:T(8,128)(2,1)}, u32[]{:S(2)}) copy-start(bf16[128,2,256]{0,2,1:T(8,128)(2,1)} %get-tuple-element.50) | copy-start | bytes 393220
  196.9 16.8 %collective-permute-start.2 = (bf16[32,1,256]{2,1,0:T(2,128)(2,1)}, bf16[32,1,256]{2,1,0:T(2,128)(2,1)S(1)}, u32[]{:S(2)}, u32[]{:S(2)}) collective-permute-start(bf16[32,1,256]{2,1,0:T(2,128)(2,1)} %get-tuple-element.356), channel_id=1, source_target_pairs={{8,0},{16,8},{24,16},{32,24},{40,32},{48,40},{56,48},{64,56},{72,6... | collective-permute-start | bytes 49160 | tf_op jit(solution)/shard_map/ppermute | solution.py:28
  198.0 15.7 %collective-permute-start.1 = (bf16[32,1,256]{2,1,0:T(2,128)(2,1)}, bf16[32,1,256]{2,1,0:T(2,128)(2,1)S(1)}, u32[]{:S(2)}, u32[]{:S(2)}) collective-permute-start(bf16[32,1,256]{2,1,0:T(2,128)(2,1)} %get-tuple-element.357), channel_id=1, source_target_pairs={{0,8},{8,16},{16,24},{24,32},{32,40},{40,48},{48,56},{56,64},{64,7... | collective-permute-start | bytes 49160 | tf_op jit(solution)/shard_map/ppermute | solution.py:25
  213.4 175.2 %collective-permute-start.5 = (bf16[16,1,1024]{2,0,1:T(8,128)(2,1)S(1)}, bf16[16,1,1024]{2,0,1:T(8,128)(2,1)S(1)}, u32[]{:S(2)}, u32[]{:S(2)}) collective-permute-start(bf16[16,1,1024]{2,0,1:T(8,128)(2,1)S(1)} %slice.3177), channel_id=1, source_target_pairs={{8,0},{16,8},{24,16},{32,24},{40,32},{48,40},{56,48},{64,56},{72,6... | collective-permute-start | bytes 98312 | tf_op jit(solution)/shard_map/ppermute | solution.py:16
  232.1 155.7 %copy-start.164 = (bf16[1,32,8]{2,1,0:T(8,128)(2,1)S(1)}, bf16[1,32,8]{2,1,0:T(8,128)(2,1)}, u32[]{:S(2)}) copy-start(bf16[1,32,8]{2,1,0:T(8,128)(2,1)} %copy.234) | copy-start | bytes 1540
  (150 other events, 850.3 us)
Sparse Core Ops, SparseCore 0:
  46.3 32.0 all-gather.1
  213.5 298.3 all-reduce.28
where the time goes:
time: 528 us; the launch traced here: 521 us
  blocking collectives  168 us (32%)
  waiting for transfers between devices  133 us (25%)
  local copies, waits for them, and re-layouts  120 us (23%)
  other arithmetic  34.8 us (7%)
  matrix products  25.6 us (5%)
  starting transfers between devices  21.7 us (4%)
  between operations  17.9 us (3%)
    psum x1, blocking collectives, body(): lax.psum((filter_part, jnp.stack(group_terms)), 'space')  153 us
    psum x1, waiting for transfers between devices, body(): lax.psum((filter_part, jnp.stack(group_terms)), 'space')  123 us
    unnamed x431, local copies, waits for them, and re-layouts  48.3 us
    squeeze x27, local copies, waits for them, and re-layouts, body(): columns[tap_index]  17.4 us
    all_gather x1, blocking collectives, body(): grad_all = lax.all_gather(hidden_grad, 'chan', axis=0, tiled=True)  14.8 us
    slice x22, local copies, waits for them, and re-layouts, roll_cells(): moved = jnp.roll(moved, -row_k * side, moved.ndim - 1)  14.1 us
    slice x19, local copies, waits for them, and re-layouts, roll_cells(): wrapped = jnp.roll(moved, col_k * (side - 1), moved.ndim - 1)  13.1 us
    slice x19, local copies, waits for them, and re-layouts, roll_cells(): inside = jnp.roll(moved, -col_k, moved.ndim - 1)  12.5 us
  transfers between devices with their start and end apart: 9, of which 2 were waited for; matrix products, arithmetic and copies ran while one was open for 14% of the time, Pallas kernels for 0%

commit v1 on v0

v1 whole, which is shorter than its diff:
```python
import math

import jax
import jax.numpy as jnp
from jax import lax
from jax.experimental import pallas as pl
from jax.experimental.pallas import tpu as pltpu
from jax.sharding import PartitionSpec as P

OFFSETS = [
    (first, second, third) for first in (-1, 0, 1) for second in (-1, 0, 1) for third in (-1, 0, 1)
]
TAPS = len(OFFSETS)
BF16 = jnp.bfloat16
F32 = jnp.float32
VMEM_LIMIT = 48 * 1024 * 1024


def phase_of(row_k, col_k):
    return 2 * (row_k != 0) + (col_k != 0)


def roll_class(row_k, col_k):
    return 2 * (row_k < 0) + (col_k < 0)


def shift_cells(plane, row_k, col_k, side):
    square = side * side
    moved = plane
    if col_k:
        inside = pltpu.roll(moved, (-col_k) % square, 1)
        wrapped = pltpu.roll(moved, (col_k * (side - 1)) % square, 1)
        column = lax.broadcasted_iota(jnp.int32, moved.shape, 1) % side
        moved = jnp.where(column == (side - 1 if col_k > 0 else 0), wrapped, inside)
    if row_k:
        moved = pltpu.roll(moved, (-row_k * side) % square, 1)
    return moved


def call(kernel, outs, *args, scratch=(), flops=0, moved=0):
    whole = pl.BlockSpec(memory_space=pltpu.VMEM)
    single = not isinstance(outs, (tuple, list))
    return pl.pallas_call(
        kernel,
        out_shape=outs,
        in_specs=[
            pl.BlockSpec(memory_space=pltpu.SMEM) if arg.dtype == jnp.int32 else whole
            for arg in args
        ],
        out_specs=whole if single else [whole] * len(outs),
        scratch_shapes=list(scratch),
        compiler_params=pltpu.CompilerParams(vmem_limit_bytes=VMEM_LIMIT),
        cost_estimate=pl.CostEstimate(flops=flops, bytes_accessed=moved, transcendentals=0),
    )(*args)


def split_filter(conv_in, pieces):
    taps, outputs, inputs = conv_in.shape
    width = inputs // pieces

    def kernel(src, dst):
        for piece in range(pieces):
            dst[piece] = jnp.concatenate(
                [src[tap, :, piece * width : (piece + 1) * width] for tap in range(taps)], axis=1
            )

    return call(kernel, jax.ShapeDtypeStruct((pieces, outputs, taps * width), BF16), conv_in)


def fill_windows(planes, store, direction, side):
    count = len(planes) - 2
    for index, plane in enumerate(planes):
        plane = plane.astype(F32)
        for row_k in (-1, 0, 1):
            for col_k in (-1, 0, 1):
                window = shift_cells(plane, direction * row_k, direction * col_k, side).astype(BF16)
                for depth_k in (-1, 0, 1):
                    inner = index - 1 - direction * depth_k
                    if 0 <= inner < count:
                        tap = 9 * (depth_k + 1) + 3 * (row_k + 1) + col_k + 1
                        store(tap, inner, window)


def block_diagonal(values, width, outputs):
    rows = values.shape[0]
    tiled = jnp.concatenate([values] * (outputs // width), axis=1)
    row = lax.broadcasted_iota(jnp.int32, tiled.shape, 0) % outputs
    column = lax.broadcasted_iota(jnp.int32, tiled.shape, 1)
    return jnp.where(row // width == column // width, tiled, jnp.zeros_like(tiled))


def upstream_part(low, cotangent, high, conv_group, side):
    planes, outputs, square = cotangent.shape
    taps, _, width = conv_group.shape
    cells = planes * square

    def kernel(low_ref, mid_ref, high_ref, group_ref, grad_ref, windows_ref):
        def store(tap, inner, window):
            windows_ref[
                tap * outputs : (tap + 1) * outputs, inner * square : (inner + 1) * square
            ] = window

        fill_windows(
            [low_ref[...]] + [mid_ref[z] for z in range(planes)] + [high_ref[...]], store, -1, side
        )
        weights = block_diagonal(group_ref[...].astype(F32), width, outputs).astype(BF16)
        grad_ref[...] = lax.dot_general(
            weights, windows_ref[...], (((0,), (0,)), ((), ())), preferred_element_type=F32
        )

    return call(
        kernel,
        (
            jax.ShapeDtypeStruct((outputs, cells), F32),
            jax.ShapeDtypeStruct((taps * outputs, cells), BF16),
        ),
        low,
        cotangent,
        high,
        conv_group.reshape(taps * outputs, width),
    )


def mix_part(low, active, high, conv_group, side):
    outputs, cells = active.shape
    square = side * side
    planes = cells // square
    taps, _, width = conv_group.shape

    def kernel(low_ref, mid_ref, high_ref, group_ref, out_ref, windows_ref):
        def store(tap, inner, window):
            windows_ref[
                tap * outputs : (tap + 1) * outputs, inner * square : (inner + 1) * square
            ] = window

        middle = [mid_ref[:, z * square : (z + 1) * square] for z in range(planes)]
        fill_windows([low_ref[...]] + middle + [high_ref[...]], store, 1, side)
        weights = block_diagonal(group_ref[...].astype(F32), width, outputs).astype(BF16)
        weights = jnp.concatenate(
            [weights[tap * outputs : (tap + 1) * outputs] for tap in range(taps)], axis=1
        )
        mixed = jnp.dot(weights, windows_ref[...], preferred_element_type=F32).astype(BF16)
        for z in range(planes):
            out_ref[z] = mixed[:, z * square : (z + 1) * square]

    return call(
        kernel,
        jax.ShapeDtypeStruct((planes, outputs, square), BF16),
        low,
        active,
        high,
        conv_group.reshape(taps * outputs, width),
        scratch=[pltpu.VMEM((taps * outputs, cells), BF16)],
    )


def main_part(place, pieces, conv_in, act_grad, windows, width, rows, side):
    taps, outputs, inputs = conv_in.shape
    square = side * side
    cells = act_grad.shape[1]
    planes = cells // square
    frames = 2 * planes + 1
    depth = 12 * inputs
    filter_rows = taps * outputs
    group_rows = -(-filter_rows // 128) * width

    def kernel(*refs):
        place_ref, conv_ref, grad_ref, windows_ref = refs[:4]
        piece_refs = refs[4 : 4 + len(pieces)]
        active_ref, hidden_grad_ref, terms_ref, field, filters = refs[4 + len(pieces) :]
        for index, (ref, (_, parts)) in enumerate(zip(piece_refs, pieces)):
            base = pl.multiple_of(place_ref[index], 16)
            for source, frame, phase, lanes in parts:
                start = (frame * 4 + phase) * inputs
                field[pl.ds(start + base, 16), :] = ref[source, :, lanes : lanes + square]
        filters[...] = jnp.zeros_like(filters)
        places = []
        for tap, (depth_k, row_k, col_k) in enumerate(OFFSETS):
            top = roll_class(row_k, col_k) * outputs
            left = ((depth_k + 1) * 4 + phase_of(row_k, col_k)) * inputs
            places.append((slice(top, top + outputs), slice(left, left + inputs)))
            filters[places[-1]] = conv_ref[tap]
        terms = jnp.zeros((4 * outputs, depth), F32)
        actives = []
        for z in range(planes):
            view = field[8 * inputs * z : 8 * inputs * z + depth, :]
            sums = jnp.dot(filters[...], view, preferred_element_type=F32)
            hidden = sums[:outputs]
            for kind, (row_k, col_k) in ((1, (0, -1)), (2, (-1, 0)), (3, (-1, -1))):
                part = sums[kind * outputs : (kind + 1) * outputs]
                hidden = hidden + shift_cells(part, row_k, col_k, side)
            sigmoid = 1.0 / (1.0 + jnp.exp(-hidden))
            active = (hidden * sigmoid).astype(BF16)
            at = slice(z * square, (z + 1) * square)
            slope = sigmoid * (1.0 + hidden * (1.0 - sigmoid))
            grad = grad_ref[:, at] * slope
            active_ref[:, at] = active
            actives.append(active)
            rounded = grad.astype(BF16)
            hidden_grad_ref[:, at] = rounded
            grad = rounded.astype(F32)
            shifted = jnp.concatenate(
                [shift_cells(grad, row_k, col_k, side) for row_k in (0, 1) for col_k in (0, 1)],
                axis=0,
            ).astype(BF16)
            terms = terms + lax.dot_general(
                shifted, view, (((1,), (1,)), ((), ())), preferred_element_type=F32
            )
        for tap, at in enumerate(places):
            terms_ref[tap * outputs : (tap + 1) * outputs, :] = terms[at].astype(BF16)
        pairs = lax.dot_general(
            jnp.concatenate(actives, axis=1),
            windows_ref[...],
            (((1,), (1,)), ((), ())),
            preferred_element_type=F32,
        )
        group = lax.broadcasted_iota(jnp.int32, (width, filter_rows), 1) % outputs // width
        kept = jnp.zeros((width, filter_rows), F32)
        for index in range(outputs // width):
            block = pairs[index * width : (index + 1) * width]
            kept = kept + jnp.where(group == index, block, 0.0)
        short = group_rows // width * 128 - filter_rows
        kept = jnp.concatenate([kept, jnp.zeros((width, short), F32)], axis=1)
        tail = [kept[:, 128 * i : 128 * (i + 1)] for i in range(group_rows // width)]
        tail.append(jnp.zeros((rows - filter_rows - group_rows, 128), F32))
        terms_ref[filter_rows:, :] = jnp.concatenate(tail, axis=0).astype(BF16)

    arrays = [piece for piece, _ in pieces]
    return call(
        kernel,
        (
            jax.ShapeDtypeStruct((outputs, cells), BF16),
            jax.ShapeDtypeStruct((outputs, cells), BF16),
            jax.ShapeDtypeStruct((rows, 128), BF16),
        ),
        place,
        conv_in,
        act_grad,
        windows,
        *arrays,
        scratch=[
            pltpu.VMEM((frames * 4 * inputs, square), BF16),
            pltpu.VMEM((4 * outputs, depth), BF16),
        ],
    )


def input_part(columns, grad_all, width, side):
    square = side * side
    cells = grad_all.shape[1]
    planes = cells // square

    def kernel(columns_ref, grad_ref, out_ref, below_ref):
        terms = lax.dot_general(
            columns_ref[...], grad_ref[...], (((0,), (0,)), ((), ())), preferred_element_type=F32
        )
        sums = {}
        for tap, (depth_k, row_k, col_k) in enumerate(OFFSETS):
            for z in range(planes):
                key = (2 * z + depth_k, phase_of(row_k, col_k), roll_class(row_k, col_k))
                part = terms[tap * width : (tap + 1) * width, z * square : (z + 1) * square]
                sums[key] = sums[key] + part if key in sums else part
        total = {}
        for (frame, phase, kind), part in sums.items():
            part = shift_cells(part, kind // 2, kind % 2, side)
            key = (frame, phase)
            total[key] = total[key] + part if key in total else part
        for (frame, phase), part in total.items():
            at = slice(phase * square, (phase + 1) * square)
            if frame < 0:
                below_ref[:, at] = part.astype(BF16)
            else:
                out_ref[frame, :, at] = part

    return call(
        kernel,
        (
            jax.ShapeDtypeStruct((2 * planes, width, 4 * square), F32),
            jax.ShapeDtypeStruct((width, 4 * square), BF16),
        ),
        columns,
        grad_all,
    )


def sum_part(received, scale):
    devices, rows, lanes = received.shape

    def kernel(src, dst):
        total = src[0].astype(F32)
        for index in range(1, devices):
            total = total + src[index].astype(F32)
        total = total * scale
        for index in range(devices):
            dst[index] = total

    return call(kernel, jax.ShapeDtypeStruct(received.shape, F32), received)


def final_part(gathered, taps, outputs, width):
    rows = taps * outputs
    blocks = -(-rows // 128)

    def kernel(src, filter_ref, group_ref):
        filter_ref[...] = src[:rows, :].reshape(taps, outputs, 128)
        for index in range(blocks):
            block = src[rows + index * width : rows + (index + 1) * width, :]
            block = jnp.concatenate([block] * (128 // width), axis=0).T
            low = index * 128
            count = min(128, rows - low)
            group_ref[low : low + count, :] = block[:count, :width]

    return call(
        kernel,
        (
            jax.ShapeDtypeStruct((taps, outputs, 128), F32),
            jax.ShapeDtypeStruct((rows, width), F32),
        ),
        gathered,
    )


def body(volume, conv_in, conv_group, cotangent):
    in_chan, in_planes, flat_in = volume.shape
    side = math.isqrt(flat_in) // 2
    square = side * side
    planes = in_planes // 2
    cells = planes * square
    taps, outputs, inputs = conv_in.shape
    width = conv_group.shape[2]
    slabs = lax.axis_size("space")
    blocks = lax.axis_size("chan")

    def along_space(block, step):
        return lax.ppermute(block, "space", [(i, (i + step) % slabs) for i in range(slabs)])

    def along_chips(block, step):
        return lax.ppermute(
            block, "chan", [(i, (i + 2 * step) % blocks) for i in range(blocks)]
        )

    def other_core(block):
        return lax.ppermute(block, "chan", [(i, i ^ 1) for i in range(blocks)])

    framed = jnp.transpose(volume, (1, 0, 2))
    below = along_space(framed[in_planes - 1 :], 1)
    own = jnp.concatenate([below, framed], axis=0)
    from_low = along_chips(own, 1)
    from_high = along_chips(own, -1)
    half = flat_in // 2
    far_left = along_chips(from_low[:, :, :half], 1)
    far_right = along_chips(from_high[:, :, half:], -1)

    upstream = jnp.transpose(cotangent, (1, 0, 2))
    up_low = along_space(upstream[planes - 1], 1)
    up_high = along_space(upstream[0], -1)
    act_grad, windows = upstream_part(up_low, upstream, up_high, conv_group, side)

    columns = lax.all_to_all(
        split_filter(conv_in, blocks), "chan", split_axis=0, concat_axis=0, tiled=True
    ).reshape(blocks * outputs, taps * in_chan)

    frames = in_planes + 1
    all_parts = [(f, f, p, p * square) for f in range(frames) for p in range(4)]
    left_parts = [(f, f, p, p * square) for f in range(frames) for p in (0, 1)]
    right_parts = [(f, f, p, (p - 2) * square) for f in range(frames) for p in (2, 3)]
    same = [
        (own, all_parts, 0),
        (from_low, all_parts, -1),
        (from_high, all_parts, 1),
        (far_left, left_parts, 2),
        (far_right, right_parts, 2),
    ]
    me = lax.axis_index("chan")
    pieces, place = [], []
    for block, parts, step in same:
        owner = (me + 2 * step) % blocks
        pieces += [(block, parts), (other_core(block), parts)]
        place += [owner * in_chan, (owner ^ 1) * in_chan]
    place = jnp.stack(place).astype(jnp.int32)

    rows = -(-(taps * outputs + 64) // (slabs * 32)) * slabs * 32
    active, hidden_grad, terms = main_part(
        place, pieces, conv_in, act_grad, windows, width, rows, side
    )
    received = lax.all_to_all(
        terms.reshape(slabs, rows // slabs, 128), "space", split_axis=0, concat_axis=0, tiled=True
    )
    scale = 1.0 / math.sqrt(slabs * cells)
    gathered = lax.all_to_all(
        sum_part(received, scale), "space", split_axis=0, concat_axis=0, tiled=True
    )
    filter_grad, group_grad = final_part(gathered.reshape(rows, 128), taps, outputs, width)

    grad_all = lax.all_gather(hidden_grad, "chan", axis=0, tiled=True)
    framed_grad, grad_below = input_part(columns, grad_all, in_chan, side)
    returned = along_space(grad_below, -1).astype(F32)
    framed_grad = framed_grad.at[in_planes - 1].add(returned)
    input_grad = jnp.transpose(framed_grad, (1, 0, 2))

    act_low = along_space(active[:, cells - square :], 1)
    act_high = along_space(active[:, :square], -1)
    mixed = mix_part(act_low, active, act_high, conv_group, side)
    mixed_out = jnp.transpose(mixed, (1, 0, 2))
    return (mixed_out, input_grad, filter_grad, group_grad.reshape(taps, outputs, width))


def solution(mesh):
    return jax.shard_map(
        body,
        mesh=mesh,
        in_specs=(
            P("chan", "space", None),
            P(None, "chan", None),
            P(None, "chan", None),
            P("chan", "space", None),
        ),
        out_specs=(
            P("chan", "space", None),
            P("chan", "space", None),
            P(None, "chan", None),
            P(None, "chan", None),
        ),
        check_vma=False,
    )
```

time: 528 us -> 108 us (0.20); the launches traced: 521 us -> 107 us
  blocking collectives: 168 us -> 16.2 us
  local copies, waits for them, and re-layouts: 120 us -> 4.4 us
  waiting for transfers between devices: 133 us -> 33.3 us
  other arithmetic: 34.8 us -> 0.03 us
  matrix products: 25.6 us -> 0 us
  starting transfers between devices: 21.7 us -> 43.8 us
  between operations: 17.9 us -> 0.79 us
  Pallas kernels: 0 us -> 8.39 us
    psum x1 -> x0, blocking collectives: 153 us -> none  [body(): lax.psum((filter_part, jnp.stack(group_terms)), 'space')]
    psum x1 -> x0, waiting for transfers between devices: 123 us -> none  [body(): lax.psum((filter_part, jnp.stack(group_terms)), 'space')]
    slice x126 -> x4, local copies, waits for them, and re-layouts: 47.2 us -> 0.02 us  [the longest x1 0.01 us: body(): far_left = along_chips(from_low[:, :, :half], 1)]
    unnamed x431 -> x12, local copies, waits for them, and re-layouts: 48.3 us -> 4.29 us
    dot_general x162 -> x0, matrix products: 25.6 us -> none  [the longest x27 5.81 us: body(): jnp.einsum('goi,goc->gic', weights, backward_view, preferred_element_type...]
    concatenate x123 -> x1, other arithmetic: 23.7 us -> 0.02 us  [body(): own = jnp.concatenate([below, framed], axis=0)]
    squeeze x27 -> x1, local copies, waits for them, and re-layouts: 17.4 us -> 0.01 us  [body(): up_high = along_space(upstream[0], -1)]
    ppermute x6 -> x15, waiting for transfers between devices: 0.02 us -> 17.1 us  [the longest x6 12.9 us: along_space(): lax.ppermute(block, 'space', [(i, (i + step) % slabs) for i in range(slab...]
  transfers between devices with their start and end apart: 9 -> 18, of which waited for: 2 -> 9; matrix products, arithmetic and copies ran while one was open for 14% -> 2% of each run, Pallas kernels for 0% -> 4%
where the time goes in v1:
time: 108 us; the launch traced here: 107 us
  starting transfers between devices  43.8 us (41%)
  waiting for transfers between devices  33.3 us (31%)
  blocking collectives  16.2 us (15%)
  Pallas kernels  8.39 us (8%)
  local copies, waits for them, and re-layouts  4.4 us (4%)
    all_gather x1, blocking collectives, body(): grad_all = lax.all_gather(hidden_grad, 'chan', axis=0, tiled=True)  16.2 us
    ppermute x6, waiting for transfers between devices, along_space(): lax.ppermute(block, 'space', [(i, (i + step) % slabs) for i in range(slab...  12.9 us
    ppermute x6, starting transfers between devices, along_space(): lax.ppermute(block, 'space', [(i, (i + step) % slabs) for i in range(slab...  12.6 us
    all_to_all x1, waiting for transfers between devices, body(): lax.all_to_all(split_filter(conv_in, blocks), 'chan', split_axis=0, conca...  11.2 us
    ppermute x4, starting transfers between devices, along_chips(): lax.ppermute(block, 'chan', [(i, (i + 2 * step) % blocks) for i in range(...  10.2 us
    all_to_all x1, starting transfers between devices, body(): lax.all_to_all(terms.reshape(slabs, rows // slabs, 128), 'space', split_a...  9.08 us
    pallas_call x7, Pallas kernels, call(): pl.pallas_call(kernel, out_shape=outs, in_specs=[pl.BlockSpec(memory_spac...  8.39 us
    all_to_all x1, starting transfers between devices, body(): lax.all_to_all(sum_part(received, scale), 'space', split_axis=0, concat_a...  8.02 us
  transfers between devices with their start and end apart: 18, of which 9 were waited for; matrix products, arithmetic and copies ran while one was open for 2% of the time, Pallas kernels for 4%

profile of v1, /device:TPU:62, one launch (start us, length us, event | category | flops | bytes accessed | tf_op | source)
XLA Modules:
  0.0 106.9 jit_solution(7414829736127487988)
XLA Ops:
  0.6 0.9 copy.16
  1.6 1.5 %collective-permute-start.2 = (bf16[1,16,1024]{2,1,0:T(8,128)(2,1)S(1)}, bf16[1,16,1024]{2,1,0:T(8,128)(2,1)S(1)}, u32[]{:S(2)}, u32[]{:S(2)}) collective-permute-start(bf16[1,16,1024]{2,1,0:T(8,128)(2,1)S(1)} %slice.53), channel_id=1, source_target_pairs={{0,8},{8,16},{16,24},{24,32},{32,40},{40,48},{48,56},{56,64},{64,7... | collective-permute-start | bytes 98312 | tf_op jit(solution)/shard_map/ppermute | solution.py:335
  3.1 2.5 %collective-permute-done.2 = bf16[1,16,1024]{2,1,0:T(8,128)(2,1)S(1)} collective-permute-done((bf16[1,16,1024]{2,1,0:T(8,128)(2,1)S(1)}, bf16[1,16,1024]{2,1,0:T(8,128)(2,1)S(1)}, u32[]{:S(2)}, u32[]{:S(2)}) %collective-permute-start.2) | collective-permute-done | bytes 32800 | tf_op jit(solution)/shard_map/ppermute | solution.py:335
  5.6 5.5 %collective-permute-start.6 = (bf16[5,16,1024]{2,1,0:T(8,128)(2,1)S(1)}, bf16[5,16,1024]{2,1,0:T(8,128)(2,1)S(1)}, u32[]{:S(2)}, u32[]{:S(2)}) collective-permute-start(bf16[5,16,1024]{2,1,0:T(8,128)(2,1)S(1)} %pad_maximum_fusion.refs_4_), channel_id=1, source_target_pairs={{0,6},{1,7},{2,0},{3,1},{4,2},{5,3},{6,4},{7,5},{8,14},{9,15},{10,... | collective-permute-start | bytes 491528 | tf_op jit(solution)/shard_map/ppermute | solution.py:338
  11.1 4.8 %collective-permute-start = (bf16[32,256]{1,0:T(8,128)(2,1)S(1)}, bf16[32,256]{1,0:T(8,128)(2,1)S(1)}, u32[]{:S(2)}, u32[]{:S(2)}) collective-permute-start(bf16[32,256]{1,0:T(8,128)(2,1)S(1)} %get-tuple-element.41), channel_id=1, source_target_pairs={{0,8},{8,16},{16,24},{24,32},{32,40},{40,48},{48,56},{56,64},{64,7... | collective-permute-start | bytes 49160 | tf_op jit(solution)/shard_map/ppermute | solution.py:335
  15.9 0.6 collective-permute-done.6.refs_8_
  16.6 4.6 %collective-permute-start.10 = (bf16[5,16,512]{2,1,0:T(8,128)(2,1)S(1)}, bf16[5,16,512]{2,1,0:T(8,128)(2,1)S(1)}, u32[]{:S(2)}, u32[]{:S(2)}) collective-permute-start(bf16[5,16,512]{2,1,0:T(8,128)(2,1)S(1)} %slice.55), channel_id=1, source_target_pairs={{0,6},{1,7},{2,0},{3,1},{4,2},{5,3},{6,4},{7,5},{8,14},{9,15},{10,... | collective-permute-start | bytes 245768 | tf_op jit(solution)/shard_map/ppermute | solution.py:338
  21.4 2.5 %collective-permute-done.1.high_ref = bf16[32,256]{1,0:T(8,128)(2,1)S(1)} collective-permute-done((bf16[32,256]{1,0:T(8,128)(2,1)S(1)}, bf16[32,256]{1,0:T(8,128)(2,1)S(1)}, u32[]{:S(2)}, u32[]{:S(2)}) %collective-permute-start.1) | collective-permute-done | bytes 16416 | tf_op jit(solution)/shard_map/ppermute | solution.py:335
  24.0 0.4 collective-permute-start.11
  24.4 3.4 %collective-permute-done.8.refs_10_ = bf16[5,16,512]{2,1,0:T(8,128)(2,1)S(1)} collective-permute-done((bf16[5,16,512]{2,1,0:T(8,128)(2,1)S(1)}, bf16[5,16,512]{2,1,0:T(8,128)(2,1)S(1)}, u32[]{:S(2)}, u32[]{:S(2)}) %collective-permute-start.8) | collective-permute-done | bytes 81952 | tf_op jit(solution)/shard_map/ppermute | solution.py:338
  27.8 0.8 copy-done.1
  28.6 0.2 copy.9
  28.9 1.0 shard_map.75
  30.0 3.0 %shard_map.76 = (bf16[32,512]{1,0:T(8,128)(2,1)S(1)}, bf16[32,512]{1,0:T(8,128)(2,1)S(1)}, bf16[1024,128]{1,0:T(8,128)(2,1)}) custom-call(s32[10]{0:T(128)S(1)} %stack.37.refs_0_, bf16[27,32,128]{2,1,0:T(8,128)(2,1)S(1)} %copy-done, f32[32,512]{1,0:T(8,128)S(1)} %get-tuple-element.25.refs_2_, bf16[864,512]{1,0:T(8,128)(2,1)S(1)} %get-tuple-element.26.refs_3_, ...), custom_call_target="tpu_custom_call" | custom-call | tf_op jit(solution)/shard_map/pallas_call | solution.py:43
  33.0 9.1 %all-to-all-start.1 = ((bf16[32,32,128]{2,1,0:T(8,128)(2,1)}), bf16[32,32,128]{2,1,0:T(8,128)(2,1)S(1)}, u32[]{:S(2)}, u32[]{:S(2)}) async-start(bf16[32,32,128]{2,1,0:T(8,128)(2,1)} %bitcast.17), calls=%async_computation.1 | async-start | bytes 524288 | tf_op jit(solution)/shard_map/all_to_all | solution.py:386
  42.0 1.2 %shard_map.78 = bf16[8,32,432]{2,1,0:T(8,128)(2,1)} custom-call(bf16[27,32,128]{2,1,0:T(8,128)(2,1)S(1)} %copy-done), custom_call_target="tpu_custom_call" | custom-call | tf_op jit(solution)/shard_map/pallas_call | solution.py:43
  43.2 4.9 %all-to-all-done.1.src = bf16[32,32,128]{2,1,0:T(8,128)(2,1)S(1)} async-done(((bf16[32,32,128]{2,1,0:T(8,128)(2,1)}), bf16[32,32,128]{2,1,0:T(8,128)(2,1)S(1)}, u32[]{:S(2)}, u32[]{:S(2)}) %all-to-all-start.1) | async-done | bytes 262176 | tf_op jit(solution)/shard_map/all_to_all | solution.py:386
  48.2 3.4 %all-to-all-start = ((bf16[8,32,432]{2,1,0:T(8,128)(2,1)}), bf16[8,32,432]{2,1,0:T(8,128)(2,1)S(1)}, u32[]{:S(2)}, u32[]{:S(2)}) async-start(bf16[8,32,432]{2,1,0:T(8,128)(2,1)} %shard_map.78), calls=%async_computation | async-start | bytes 524288 | tf_op jit(solution)/shard_map/all_to_all | solution.py:359
  51.6 0.9 shard_map.80
  52.5 11.2 %all-to-all-done = bf16[8,32,432]{2,1,0:T(8,128)(2,1)S(1)} async-done(((bf16[8,32,432]{2,1,0:T(8,128)(2,1)}), bf16[8,32,432]{2,1,0:T(8,128)(2,1)S(1)}, u32[]{:S(2)}, u32[]{:S(2)}) %all-to-all-start) | async-done | bytes 221216 | tf_op jit(solution)/shard_map/all_to_all | solution.py:359
  63.7 8.0 %all-to-all-start.2 = ((f32[32,32,128]{2,1,0:T(8,128)}), f32[32,32,128]{2,1,0:T(8,128)S(1)}, u32[]{:S(2)}, u32[]{:S(2)}) async-start(f32[32,32,128]{2,1,0:T(8,128)} %shard_map.80), calls=%async_computation.2 | async-start | bytes 1048576 | tf_op jit(solution)/shard_map/all_to_all | solution.py:390
  71.7 16.2 %all_gather.3.grad_ref = bf16[256,512]{1,0:T(8,128)(2,1)S(1)} all-gather(bf16[32,512]{1,0:T(8,128)(2,1)S(1)} %get-tuple-element.28), channel_id=1, replica_groups=mesh['space'=32,'chan'=8] {'chan'}, dimensions={0}, use_global_device_ids=true | all-gather | bytes 294912 | tf_op jit(solution)/shard_map/all_gather | solution.py:395
  87.9 0.5 shard_map.79
  88.4 0.6 collective-permute-start.14
  88.9 5.8 %collective-permute-start.12 = (bf16[32,256]{1,0:T(8,128)(2,1)S(1)}, bf16[32,256]{1,0:T(8,128)(2,1)S(1)}, u32[]{:S(2)}, u32[]{:S(2)}) collective-permute-start(bf16[32,256]{1,0:T(8,128)(2,1)S(1)} %get-tuple-element.39), channel_id=1, source_target_pairs={{0,8},{8,16},{16,24},{24,32},{32,40},{40,48},{48,56},{56,64},{64,7... | collective-permute-start | bytes 49160 | tf_op jit(solution)/shard_map/ppermute | solution.py:335
  94.7 1.4 %collective-permute-done.12.low_ref = bf16[32,256]{1,0:T(8,128)(2,1)S(1)} collective-permute-done((bf16[32,256]{1,0:T(8,128)(2,1)S(1)}, bf16[32,256]{1,0:T(8,128)(2,1)S(1)}, u32[]{:S(2)}, u32[]{:S(2)}) %collective-permute-start.12) | collective-permute-done | bytes 16416 | tf_op jit(solution)/shard_map/ppermute | solution.py:335
  96.1 6.5 %collective-permute-done.13.high_ref = bf16[32,256]{1,0:T(8,128)(2,1)S(1)} collective-permute-done((bf16[32,256]{1,0:T(8,128)(2,1)S(1)}, bf16[32,256]{1,0:T(8,128)(2,1)S(1)}, u32[]{:S(2)}, u32[]{:S(2)}) %collective-permute-start.13) | collective-permute-done | bytes 16416 | tf_op jit(solution)/shard_map/ppermute | solution.py:335
  102.7 1.0 shard_map.77
  103.6 0.7 copy.11
  104.3 0.9 copy.12
  105.2 0.9 shard_map.81
  106.1 0.8 copy.13
  (32 shorter events, 0.5 us)
Async XLA Ops:
  1.6 1.5 %copy-start.2 = (bf16[32,2,256]{2,1,0:T(2,128)(2,1)S(1)}, bf16[32,2,256]{2,1,0:T(2,128)(2,1)}, u32[]{:S(2)}) copy-start(bf16[32,2,256]{2,1,0:T(2,128)(2,1)} %param.9) | copy-start | bytes 98308
  1.6 4.0 %collective-permute-start.2 = (bf16[1,16,1024]{2,1,0:T(8,128)(2,1)S(1)}, bf16[1,16,1024]{2,1,0:T(8,128)(2,1)S(1)}, u32[]{:S(2)}, u32[]{:S(2)}) collective-permute-start(bf16[1,16,1024]{2,1,0:T(8,128)(2,1)S(1)} %slice.53), channel_id=1, source_target_pairs={{0,8},{8,16},{16,24},{24,32},{32,40},{40,48},{48,56},{56,64},{64,7... | collective-permute-start | bytes 98312 | tf_op jit(solution)/shard_map/ppermute | solution.py:335
  5.6 10.9 %collective-permute-start.6 = (bf16[5,16,1024]{2,1,0:T(8,128)(2,1)S(1)}, bf16[5,16,1024]{2,1,0:T(8,128)(2,1)S(1)}, u32[]{:S(2)}, u32[]{:S(2)}) collective-permute-start(bf16[5,16,1024]{2,1,0:T(8,128)(2,1)S(1)} %pad_maximum_fusion.refs_4_), channel_id=1, source_target_pairs={{0,6},{1,7},{2,0},{3,1},{4,2},{5,3},{6,4},{7,5},{8,14},{9,15},{10,... | collective-permute-start | bytes 491528 | tf_op jit(solution)/shard_map/ppermute | solution.py:338
  11.1 10.1 %collective-permute-start.4 = (bf16[5,16,1024]{2,1,0:T(8,128)(2,1)S(1)}, bf16[5,16,1024]{2,1,0:T(8,128)(2,1)S(1)}, u32[]{:S(2)}, u32[]{:S(2)}) collective-permute-start(bf16[5,16,1024]{2,1,0:T(8,128)(2,1)S(1)} %pad_maximum_fusion.refs_4_), channel_id=1, source_target_pairs={{0,2},{1,3},{2,4},{3,5},{4,6},{5,7},{6,0},{7,1},{8,10},{9,11},{10,... | collective-permute-start | bytes 491528 | tf_op jit(solution)/shard_map/ppermute | solution.py:338
  11.1 10.2 %collective-permute-start = (bf16[32,256]{1,0:T(8,128)(2,1)S(1)}, bf16[32,256]{1,0:T(8,128)(2,1)S(1)}, u32[]{:S(2)}, u32[]{:S(2)}) collective-permute-start(bf16[32,256]{1,0:T(8,128)(2,1)S(1)} %get-tuple-element.41), channel_id=1, source_target_pairs={{0,8},{8,16},{16,24},{24,32},{32,40},{40,48},{48,56},{56,64},{64,7... | collective-permute-start | bytes 49160 | tf_op jit(solution)/shard_map/ppermute | solution.py:335
  15.9 8.0 %collective-permute-start.1 = (bf16[32,256]{1,0:T(8,128)(2,1)S(1)}, bf16[32,256]{1,0:T(8,128)(2,1)S(1)}, u32[]{:S(2)}, u32[]{:S(2)}) collective-permute-start(bf16[32,256]{1,0:T(8,128)(2,1)S(1)} %get-tuple-element.40), channel_id=1, source_target_pairs={{0,248},{8,0},{16,8},{24,16},{32,24},{40,32},{48,40},{56,48},{64,5... | collective-permute-start | bytes 49160 | tf_op jit(solution)/shard_map/ppermute | solution.py:335
  15.9 14.0 %collective-permute-start.3 = (bf16[5,16,1024]{2,1,0:T(8,128)(2,1)S(1)}, bf16[5,16,1024]{2,1,0:T(8,128)(2,1)S(1)}, u32[]{:S(2)}, u32[]{:S(2)}) collective-permute-start(bf16[5,16,1024]{2,1,0:T(8,128)(2,1)S(1)} %pad_maximum_fusion.refs_4_), channel_id=1, source_target_pairs={{0,1},{1,0},{2,3},{3,2},{4,5},{5,4},{6,7},{7,6},{8,9},{9,8},{10,11... | collective-permute-start | bytes 491528 | tf_op jit(solution)/shard_map/ppermute | solution.py:343
  16.6 7.4 %collective-permute-start.10 = (bf16[5,16,512]{2,1,0:T(8,128)(2,1)S(1)}, bf16[5,16,512]{2,1,0:T(8,128)(2,1)S(1)}, u32[]{:S(2)}, u32[]{:S(2)}) collective-permute-start(bf16[5,16,512]{2,1,0:T(8,128)(2,1)S(1)} %slice.55), channel_id=1, source_target_pairs={{0,6},{1,7},{2,0},{3,1},{4,2},{5,3},{6,4},{7,5},{8,14},{9,15},{10,... | collective-permute-start | bytes 245768 | tf_op jit(solution)/shard_map/ppermute | solution.py:338
  21.2 6.6 %collective-permute-start.8 = (bf16[5,16,512]{2,1,0:T(8,128)(2,1)S(1)}, bf16[5,16,512]{2,1,0:T(8,128)(2,1)S(1)}, u32[]{:S(2)}, u32[]{:S(2)}) collective-permute-start(bf16[5,16,512]{2,1,0:T(8,128)(2,1)S(1)} %slice.54), channel_id=1, source_target_pairs={{0,2},{1,3},{2,4},{3,5},{4,6},{5,7},{6,0},{7,1},{8,10},{9,11},{10,... | collective-permute-start | bytes 245768 | tf_op jit(solution)/shard_map/ppermute | solution.py:338
  21.3 8.7 %collective-permute-start.5 = (bf16[5,16,1024]{2,1,0:T(8,128)(2,1)S(1)}, bf16[5,16,1024]{2,1,0:T(8,128)(2,1)S(1)}, u32[]{:S(2)}, u32[]{:S(2)}) collective-permute-start(bf16[5,16,1024]{2,1,0:T(8,128)(2,1)S(1)} %collective-permute-done.4.refs_6_), channel_id=1, source_target_pairs={{0,1},{1,0},{2,3},{3,2},{4,5},{5,4},{6,7},{7,6},{8,9},{9,8},{10,11... | collective-permute-start | bytes 491528 | tf_op jit(solution)/shard_map/ppermute | solution.py:343
  23.9 6.1 %collective-permute-start.7 = (bf16[5,16,1024]{2,1,0:T(8,128)(2,1)S(1)}, bf16[5,16,1024]{2,1,0:T(8,128)(2,1)S(1)}, u32[]{:S(2)}, u32[]{:S(2)}) collective-permute-start(bf16[5,16,1024]{2,1,0:T(8,128)(2,1)S(1)} %collective-permute-done.6.refs_8_), channel_id=1, source_target_pairs={{0,1},{1,0},{2,3},{3,2},{4,5},{5,4},{6,7},{7,6},{8,9},{9,8},{10,11... | collective-permute-start | bytes 491528 | tf_op jit(solution)/shard_map/ppermute | solution.py:343
  24.0 6.0 %collective-permute-start.11 = (bf16[5,16,512]{2,1,0:T(8,128)(2,1)S(1)}, bf16[5,16,512]{2,1,0:T(8,128)(2,1)S(1)}, u32[]{:S(2)}, u32[]{:S(2)}) collective-permute-start(bf16[5,16,512]{2,1,0:T(8,128)(2,1)S(1)} %collective-permute-done.10.refs_12_), channel_id=1, source_target_pairs={{0,1},{1,0},{2,3},{3,2},{4,5},{5,4},{6,7},{7,6},{8,9},{9,8},{10,11... | collective-permute-start | bytes 245768 | tf_op jit(solution)/shard_map/ppermute | solution.py:343
  27.8 2.1 %collective-permute-start.9 = (bf16[5,16,512]{2,1,0:T(8,128)(2,1)S(1)}, bf16[5,16,512]{2,1,0:T(8,128)(2,1)S(1)}, u32[]{:S(2)}, u32[]{:S(2)}) collective-permute-start(bf16[5,16,512]{2,1,0:T(8,128)(2,1)S(1)} %collective-permute-done.8.refs_10_), channel_id=1, source_target_pairs={{0,1},{1,0},{2,3},{3,2},{4,5},{5,4},{6,7},{7,6},{8,9},{9,8},{10,11... | collective-permute-start | bytes 245768 | tf_op jit(solution)/shard_map/ppermute | solution.py:343
  27.8 0.8 copy-start.1
  28.8 1.2 %copy-start = (bf16[27,32,128]{2,1,0:T(8,128)(2,1)S(1)}, bf16[27,32,128]{2,1,0:T(8,128)(2,1)}, u32[]{:S(2)}) copy-start(bf16[27,32,128]{2,1,0:T(8,128)(2,1)} %src.1) | copy-start | bytes 663556
  33.0 15.2 %all-to-all-start.1 = ((bf16[32,32,128]{2,1,0:T(8,128)(2,1)}), bf16[32,32,128]{2,1,0:T(8,128)(2,1)S(1)}, u32[]{:S(2)}, u32[]{:S(2)}) async-start(bf16[32,32,128]{2,1,0:T(8,128)(2,1)} %bitcast.17), calls=%async_computation.1 | async-start | bytes 524288 | tf_op jit(solution)/shard_map/all_to_all | solution.py:386
  48.2 15.6 %all-to-all-start = ((bf16[8,32,432]{2,1,0:T(8,128)(2,1)}), bf16[8,32,432]{2,1,0:T(8,128)(2,1)S(1)}, u32[]{:S(2)}, u32[]{:S(2)}) async-start(bf16[8,32,432]{2,1,0:T(8,128)(2,1)} %shard_map.78), calls=%async_computation | async-start | bytes 524288 | tf_op jit(solution)/shard_map/all_to_all | solution.py:359
  63.7 41.5 %all-to-all-start.2 = ((f32[32,32,128]{2,1,0:T(8,128)}), f32[32,32,128]{2,1,0:T(8,128)S(1)}, u32[]{:S(2)}, u32[]{:S(2)}) async-start(f32[32,32,128]{2,1,0:T(8,128)} %shard_map.80), calls=%async_computation.2 | async-start | bytes 1048576 | tf_op jit(solution)/shard_map/all_to_all | solution.py:390
  88.4 15.9 %collective-permute-start.14 = (bf16[16,1024]{1,0:T(8,128)(2,1)S(1)}, bf16[16,1024]{1,0:T(8,128)(2,1)S(1)}, u32[]{:S(2)}, u32[]{:S(2)}) collective-permute-start(bf16[16,1024]{1,0:T(8,128)(2,1)S(1)} %get-tuple-element.30), channel_id=1, source_target_pairs={{0,248},{8,0},{16,8},{24,16},{32,24},{40,32},{48,40},{56,48},{64,5... | collective-permute-start | bytes 98312 | tf_op jit(solution)/shard_map/ppermute | solution.py:335
  88.9 7.2 %collective-permute-start.12 = (bf16[32,256]{1,0:T(8,128)(2,1)S(1)}, bf16[32,256]{1,0:T(8,128)(2,1)S(1)}, u32[]{:S(2)}, u32[]{:S(2)}) collective-permute-start(bf16[32,256]{1,0:T(8,128)(2,1)S(1)} %get-tuple-element.39), channel_id=1, source_target_pairs={{0,8},{8,16},{16,24},{24,32},{32,40},{40,48},{48,56},{56,64},{64,7... | collective-permute-start | bytes 49160 | tf_op jit(solution)/shard_map/ppermute | solution.py:335
  94.7 8.0 %collective-permute-start.13 = (bf16[32,256]{1,0:T(8,128)(2,1)S(1)}, bf16[32,256]{1,0:T(8,128)(2,1)S(1)}, u32[]{:S(2)}, u32[]{:S(2)}) collective-permute-start(bf16[32,256]{1,0:T(8,128)(2,1)S(1)} %get-tuple-element.38), channel_id=1, source_target_pairs={{0,248},{8,0},{16,8},{24,16},{32,24},{40,32},{48,40},{56,48},{64,5... | collective-permute-start | bytes 49160 | tf_op jit(solution)/shard_map/ppermute | solution.py:335

commit v2 on v1

v2 whole, which is shorter than its diff:
```python
import math

import jax
import jax.numpy as jnp
from jax import lax
from jax.experimental import pallas as pl
from jax.experimental.pallas import tpu as pltpu
from jax.sharding import PartitionSpec as P

OFFSETS = [
    (first, second, third) for first in (-1, 0, 1) for second in (-1, 0, 1) for third in (-1, 0, 1)
]
TAPS = len(OFFSETS)
BF16 = jnp.bfloat16
F32 = jnp.float32
VMEM_LIMIT = 48 * 1024 * 1024


def phase_of(row_k, col_k):
    return 2 * (row_k != 0) + (col_k != 0)


def roll_class(row_k, col_k):
    return 2 * (row_k < 0) + (col_k < 0)


def shift_cells(plane, row_k, col_k, side):
    square = side * side
    moved = plane
    if col_k:
        inside = pltpu.roll(moved, (-col_k) % square, 1)
        wrapped = pltpu.roll(moved, (col_k * (side - 1)) % square, 1)
        column = lax.broadcasted_iota(jnp.int32, moved.shape, 1) % side
        moved = jnp.where(column == (side - 1 if col_k > 0 else 0), wrapped, inside)
    if row_k:
        moved = pltpu.roll(moved, (-row_k * side) % square, 1)
    return moved


def call(kernel, outs, *args, scratch=(), flops=0, moved=0):
    whole = pl.BlockSpec(memory_space=pltpu.VMEM)
    single = not isinstance(outs, (tuple, list))
    return pl.pallas_call(
        kernel,
        out_shape=outs,
        in_specs=[whole] * len(args),
        out_specs=whole if single else [whole] * len(outs),
        scratch_shapes=list(scratch),
        compiler_params=pltpu.CompilerParams(vmem_limit_bytes=VMEM_LIMIT),
        cost_estimate=pl.CostEstimate(flops=flops, bytes_accessed=moved, transcendentals=0),
    )(*args)


def prep_part(volume, cotangent):
    in_chan, in_planes, flat_in = volume.shape
    outputs, planes, square = cotangent.shape

    def kernel(vol_ref, cot_ref, own_ref, packed_ref, cells_ref):
        for frame in range(in_planes):
            for phase in range(4):
                low = (frame * 4 + phase) * in_chan
                part = vol_ref[frame, :, phase * square : (phase + 1) * square]
                own_ref[low : low + in_chan, :] = part
                if frame == in_planes - 1:
                    packed_ref[phase * in_chan : (phase + 1) * in_chan, :] = part
        for z in range(planes):
            cells_ref[z * outputs : (z + 1) * outputs, :] = cot_ref[z]
        packed_ref[4 * in_chan :, :] = cot_ref[planes - 1]

    return call(
        kernel,
        (
            jax.ShapeDtypeStruct((in_planes * 4 * in_chan, square), BF16),
            jax.ShapeDtypeStruct((4 * in_chan + outputs, square), BF16),
            jax.ShapeDtypeStruct((planes * outputs, square), BF16),
        ),
        jnp.transpose(volume, (1, 0, 2)),
        jnp.transpose(cotangent, (1, 0, 2)),
    )


def split_filter(conv_in, in_chan, square):
    taps, outputs, inputs = conv_in.shape
    count = inputs // in_chan
    block_rows = 2 * outputs
    short = 2 * square - taps * in_chan

    def kernel(conv_ref, here_ref, up_ref, down_ref, far_ref, blocks):
        me = lax.axis_index("chan")
        for owner in range(count):
            steps = lax.rem(owner // 2 + count // 2 - me // 2, count // 2)
            crossed = lax.rem(owner + me, 2)
            wide = [conv_ref[tap, :, owner * in_chan : (owner + 1) * in_chan] for tap in range(taps)]
            wide = jnp.concatenate(wide + [jnp.zeros((outputs, short), BF16)], axis=1)
            blocks[2 * steps + crossed, :outputs, :] = wide[:, :square]
            blocks[2 * steps + crossed, outputs:, :] = wide[:, square:]
        for ref, order in ((here_ref, (1, 0)), (up_ref, (2, 3)), (down_ref, (6, 7)), (far_ref, (4, 5))):
            for index, block in enumerate(order):
                ref[index * block_rows : (index + 1) * block_rows, :] = blocks[block]

    return call(
        kernel,
        [jax.ShapeDtypeStruct((2 * block_rows, square), BF16)] * 4,
        conv_in,
        scratch=[pltpu.VMEM((count, block_rows, square), BF16)],
    )


def fill_windows(planes, store, direction, side):
    count = len(planes) - 2
    for index, plane in enumerate(planes):
        plane = plane.astype(F32)
        for row_k in (-1, 0, 1):
            for col_k in (-1, 0, 1):
                window = shift_cells(plane, direction * row_k, direction * col_k, side).astype(BF16)
                for depth_k in (-1, 0, 1):
                    inner = index - 1 - direction * depth_k
                    if 0 <= inner < count:
                        tap = 9 * (depth_k + 1) + 3 * (row_k + 1) + col_k + 1
                        store(tap, inner, window)


def block_diagonal(values, outputs):
    width, columns = values.shape
    tiled = jnp.concatenate([values] * (outputs // width), axis=0)
    row = lax.broadcasted_iota(jnp.int32, tiled.shape, 0)
    column = lax.broadcasted_iota(jnp.int32, tiled.shape, 1) % outputs
    return jnp.where(row // width == column // width, tiled, jnp.zeros_like(tiled))


def upstream_part(packed, cotangent, high, group_filter, side):
    square = side * side
    taps, width, outputs = group_filter.shape
    planes = cotangent.shape[0] // outputs
    cells = planes * square
    skipped = packed.shape[0] - outputs

    def kernel(low_ref, mid_ref, high_ref, group_ref, grad_ref, windows_ref):
        def store(tap, inner, window):
            windows_ref[
                tap * outputs : (tap + 1) * outputs, inner * square : (inner + 1) * square
            ] = window

        middle = [mid_ref[z * outputs : (z + 1) * outputs, :] for z in range(planes)]
        fill_windows([low_ref[skipped:, :]] + middle + [high_ref[...]], store, -1, side)
        flat = jnp.concatenate([group_ref[tap].astype(F32) for tap in range(taps)], axis=1)
        weights = block_diagonal(flat, outputs).astype(BF16)
        grad_ref[...] = jnp.dot(weights, windows_ref[...], preferred_element_type=F32)

    return call(
        kernel,
        (
            jax.ShapeDtypeStruct((outputs, cells), F32),
            jax.ShapeDtypeStruct((taps * outputs, cells), BF16),
        ),
        packed,
        cotangent,
        high,
        group_filter,
    )


def owner_row(step, other, rows):
    me = lax.axis_index("chan")
    count = lax.axis_size("chan")
    owner = lax.rem(me + (2 * step) % count, count)
    if other:
        owner = owner + 1 - 2 * lax.rem(owner, 2)
    return pl.multiple_of(owner * rows, rows)


def main_part(pieces, conv_in, act_grad, windows, width, rows, side):
    taps, outputs, inputs = conv_in.shape
    square = side * side
    cells = act_grad.shape[1]
    planes = cells // square
    frames = 2 * planes + 1
    depth = 12 * inputs
    in_chan = inputs // lax.axis_size("chan")
    filter_rows = taps * outputs
    group_rows = -(-filter_rows // 128) * width

    def kernel(*refs):
        conv_ref, grad_ref, windows_ref = refs[:3]
        piece_refs = refs[3 : 3 + len(pieces)]
        active_ref, hidden_grad_ref, terms_ref, field, filters = refs[3 + len(pieces) :]
        for ref, (_, parts) in zip(piece_refs, pieces):
            for first, slots, step, other in parts:
                base = owner_row(step, other, in_chan)
                for index, slot in enumerate(slots):
                    low = first + index * in_chan
                    field[pl.ds(slot * inputs + base, in_chan), :] = ref[low : low + in_chan, :]
        filters[...] = jnp.zeros_like(filters)
        places = []
        for tap, (depth_k, row_k, col_k) in enumerate(OFFSETS):
            top = roll_class(row_k, col_k) * outputs
            left = ((depth_k + 1) * 4 + phase_of(row_k, col_k)) * inputs
            places.append((slice(top, top + outputs), slice(left, left + inputs)))
            filters[places[-1]] = conv_ref[tap]
        terms = jnp.zeros((4 * outputs, depth), F32)
        actives = []
        for z in range(planes):
            view = field[8 * inputs * z : 8 * inputs * z + depth, :]
            sums = jnp.dot(filters[...], view, preferred_element_type=F32)
            hidden = sums[:outputs]
            for kind, (row_k, col_k) in ((1, (0, -1)), (2, (-1, 0)), (3, (-1, -1))):
                part = sums[kind * outputs : (kind + 1) * outputs]
                hidden = hidden + shift_cells(part, row_k, col_k, side)
            sigmoid = 1.0 / (1.0 + jnp.exp(-hidden))
            active = (hidden * sigmoid).astype(BF16)
            at = slice(z * square, (z + 1) * square)
            slope = sigmoid * (1.0 + hidden * (1.0 - sigmoid))
            grad = grad_ref[:, at] * slope
            active_ref[:, at] = active
            actives.append(active)
            rounded = grad.astype(BF16)
            hidden_grad_ref[z * outputs : (z + 1) * outputs, :] = rounded
            grad = rounded.astype(F32)
            shifted = jnp.concatenate(
                [shift_cells(grad, row_k, col_k, side) for row_k in (0, 1) for col_k in (0, 1)],
                axis=0,
            ).astype(BF16)
            terms = terms + lax.dot_general(
                shifted, view, (((1,), (1,)), ((), ())), preferred_element_type=F32
            )
        for tap, at in enumerate(places):
            terms_ref[tap * outputs : (tap + 1) * outputs, :] = terms[at].astype(BF16)
        pairs = lax.dot_general(
            jnp.concatenate(actives, axis=1),
            windows_ref[...],
            (((1,), (1,)), ((), ())),
            preferred_element_type=F32,
        )
        group = lax.broadcasted_iota(jnp.int32, (width, filter_rows), 1) % outputs // width
        kept = jnp.zeros((width, filter_rows), F32)
        for index in range(outputs // width):
            block = pairs[index * width : (index + 1) * width]
            kept = kept + jnp.where(group == index, block, 0.0)
        short = group_rows // width * 128 - filter_rows
        kept = jnp.concatenate([kept, jnp.zeros((width, short), F32)], axis=1)
        tail = [kept[:, 128 * i : 128 * (i + 1)] for i in range(group_rows // width)]
        tail.append(jnp.zeros((rows - filter_rows - group_rows, 128), F32))
        terms_ref[filter_rows:, :] = jnp.concatenate(tail, axis=0).astype(BF16)

    return call(
        kernel,
        (
            jax.ShapeDtypeStruct((outputs, cells), BF16),
            jax.ShapeDtypeStruct((planes * outputs, square), BF16),
            jax.ShapeDtypeStruct((rows, 128), BF16),
        ),
        conv_in,
        act_grad,
        windows,
        *[piece for piece, _ in pieces],
        scratch=[
            pltpu.VMEM((frames * 4 * inputs, square), BF16),
            pltpu.VMEM((4 * outputs, depth), BF16),
        ],
    )


def input_part(pieces, active, width, side):
    square = side * side
    outputs, cells = active.shape
    planes = cells // square
    devices = lax.axis_size("chan")

    def kernel(active_ref, *refs):
        piece_refs = refs[: len(pieces)]
        out_ref, down_ref, grads, filters = refs[len(pieces) :]
        for ref, (_, parts) in zip(piece_refs, pieces):
            for first, is_filter, step, other in parts:
                at = pl.ds(owner_row(step, other, outputs), outputs)
                target = filters if is_filter else grads
                for z in range(target.shape[1] // square):
                    low = first + z * outputs
                    target[at, z * square : (z + 1) * square] = ref[low : low + outputs, :]
        terms = lax.dot_general(
            filters[...], grads[...], (((0,), (0,)), ((), ())), preferred_element_type=F32
        )
        sums = {}
        for tap, (depth_k, row_k, col_k) in enumerate(OFFSETS):
            for z in range(planes):
                key = (2 * z + depth_k, phase_of(row_k, col_k), roll_class(row_k, col_k))
                part = terms[tap * width : (tap + 1) * width, z * square : (z + 1) * square]
                sums[key] = sums[key] + part if key in sums else part
        total = {}
        for (frame, phase, kind), part in sums.items():
            part = shift_cells(part, kind // 2, kind % 2, side)
            key = (frame, phase)
            total[key] = total[key] + part if key in total else part
        for (frame, phase), part in total.items():
            if frame < 0:
                down_ref[phase * width : (phase + 1) * width, :] = part.astype(BF16)
            else:
                out_ref[frame, :, phase * square : (phase + 1) * square] = part
        down_ref[4 * width :, :] = active_ref[:, :square]

    return call(
        kernel,
        (
            jax.ShapeDtypeStruct((2 * planes, width, 4 * square), F32),
            jax.ShapeDtypeStruct((4 * width + outputs, square), BF16),
        ),
        active,
        *[piece for piece, _ in pieces],
        scratch=[
            pltpu.VMEM((devices * outputs, cells), BF16),
            pltpu.VMEM((devices * outputs, 2 * square), BF16),
        ],
    )


def mix_part(low, active, packed, framed_grad, group_filter, side):
    outputs, cells = active.shape
    square = side * side
    planes = cells // square
    taps, width, _ = group_filter.shape
    in_planes, in_chan, _ = framed_grad.shape

    def kernel(low_ref, mid_ref, packed_ref, grad_ref, group_ref, out_ref, sum_ref, windows_ref):
        def store(tap, inner, window):
            windows_ref[
                tap * outputs : (tap + 1) * outputs, inner * square : (inner + 1) * square
            ] = window

        middle = [mid_ref[:, z * square : (z + 1) * square] for z in range(planes)]
        fill_windows([low_ref[...]] + middle + [packed_ref[4 * in_chan :, :]], store, 1, side)
        weights = jnp.concatenate(
            [block_diagonal(group_ref[tap].astype(F32), outputs) for tap in range(taps)], axis=0
        ).astype(BF16)
        mixed = lax.dot_general(
            weights, windows_ref[...], (((0,), (0,)), ((), ())), preferred_element_type=F32
        ).astype(BF16)
        for z in range(planes):
            out_ref[z] = mixed[:, z * square : (z + 1) * square]
        for frame in range(in_planes - 1):
            sum_ref[frame] = grad_ref[frame]
        for phase in range(4):
            at = slice(phase * square, (phase + 1) * square)
            from_above = packed_ref[phase * in_chan : (phase + 1) * in_chan, :].astype(F32)
            sum_ref[in_planes - 1, :, at] = grad_ref[in_planes - 1, :, at] + from_above

    return call(
        kernel,
        (
            jax.ShapeDtypeStruct((planes, outputs, square), BF16),
            jax.ShapeDtypeStruct(framed_grad.shape, F32),
        ),
        low,
        active,
        packed,
        framed_grad,
        group_filter,
        scratch=[pltpu.VMEM((taps * outputs, cells), BF16)],
    )


def sum_part(received, scale):
    devices, rows, lanes = received.shape

    def kernel(src, dst):
        total = src[0].astype(F32)
        for index in range(1, devices):
            total = total + src[index].astype(F32)
        total = total * scale
        total = total.astype(BF16)
        for index in range(devices):
            dst[index] = total

    return call(kernel, jax.ShapeDtypeStruct(received.shape, BF16), received)


def final_part(gathered, taps, outputs, width):
    rows = taps * outputs
    blocks = -(-rows // 128)

    def kernel(src, filter_ref, group_ref):
        filter_ref[...] = src[:rows, :].astype(F32).reshape(taps, outputs, 128)
        tail = src[rows:, :].astype(F32)
        flat = jnp.concatenate(
            [tail[i * width : (i + 1) * width, :] for i in range(blocks)], axis=1
        )
        for tap in range(taps):
            group_ref[tap] = flat[:, tap * outputs : (tap + 1) * outputs]

    return call(
        kernel,
        (
            jax.ShapeDtypeStruct((taps, outputs, 128), F32),
            jax.ShapeDtypeStruct((taps, width, outputs), F32),
        ),
        gathered,
    )


def body(volume, conv_in, conv_group, cotangent):
    in_chan, in_planes, flat_in = volume.shape
    side = math.isqrt(flat_in) // 2
    square = side * side
    planes = in_planes // 2
    cells = planes * square
    taps, outputs, inputs = conv_in.shape
    width = conv_group.shape[2]
    slabs = lax.axis_size("space")
    blocks = lax.axis_size("chan")

    def along_space(block, step):
        return lax.ppermute(block, "space", [(i, (i + step) % slabs) for i in range(slabs)])

    def along_chips(block, step):
        return lax.ppermute(
            block, "chan", [(i, (i + 2 * step) % blocks) for i in range(blocks)]
        )

    def other_core(block):
        return lax.ppermute(block, "chan", [(i, i ^ 1) for i in range(blocks)])

    def joined(*parts):
        return jnp.concatenate(parts, axis=0)

    own, packed, upstream = prep_part(volume, cotangent)
    frame = 4 * in_chan
    packed = along_space(packed, 1)
    up_high = along_space(upstream[:outputs], -1)
    group_filter = jnp.transpose(conv_group, (0, 2, 1))
    act_grad, windows = upstream_part(packed, upstream, up_high, group_filter, side)
    sent = split_filter(conv_in, in_chan, square)

    slots = list(range(4 * (in_planes + 1)))
    length = len(slots) * in_chan
    cut = len(slots) // 2
    own, up_high = lax.optimization_barrier((own, up_high))
    framed = joined(packed[:frame], own)
    from_low = along_chips(framed, 1)
    from_high = along_chips(framed, -1)
    from_low, act_grad, sent = lax.optimization_barrier((from_low, act_grad, sent))
    far_low = along_chips(from_low[: cut * in_chan], 1)
    far_high = along_chips(from_high[cut * in_chan :], -1)
    near_other = other_core(joined(from_low, from_high))
    far_other = other_core(joined(far_low, far_high))
    pieces = [
        (framed, [(0, slots, 0, False)]),
        (other_core(framed), [(0, slots, 0, True)]),
        (from_low, [(0, slots, -1, False)]),
        (from_high, [(0, slots, 1, False)]),
        (near_other, [(0, slots, -1, True), (length, slots, 1, True)]),
        (far_low, [(0, slots[:cut], 2, False)]),
        (far_high, [(0, slots[cut:], 2, False)]),
        (far_other, [(0, slots, 2, True)]),
    ]

    rows = -(-(taps * outputs + 64) // (slabs * 32)) * slabs * 32
    active, hidden_grad, terms = main_part(
        pieces, conv_in, act_grad, windows, width, rows, side
    )
    received = lax.all_to_all(
        terms.reshape(slabs, rows // slabs, 128), "space", split_axis=0, concat_axis=0, tiled=True
    )
    here, up, down, far = sent
    act_low = along_space(active[:, cells - square :], 1)
    up = along_chips(joined(hidden_grad, up), 1)
    down = along_chips(joined(hidden_grad, down), -1)
    far = along_chips(joined(hidden_grad, far), 2)
    block = 2 * outputs
    near = other_core(joined(hidden_grad, here[:block]))
    up, near, act_low = lax.optimization_barrier((up, near, act_low))
    crossed = other_core(
        joined(*[part for ring in (up, down, far) for part in (ring[:block], ring[2 * block :])])
    )
    steps = (-1, 1, 2)
    grads = [
        (hidden_grad, [(0, False, 0, False)]),
        (here, [(block, True, 0, False)]),
        (near, [(0, False, 0, True), (block, True, 0, True)]),
        (crossed, [(i * 2 * block, False, step, True) for i, step in enumerate(steps)]
         + [((2 * i + 1) * block, True, step, True) for i, step in enumerate(steps)]),
    ]
    for ring, step in zip((up, down, far), steps):
        grads.append((ring, [(0, False, step, False), (block, True, step, False)]))
    framed_grad, lowest = input_part(grads, active, in_chan, side)
    received, lowest = lax.optimization_barrier((received, lowest))
    scale = 1.0 / math.sqrt(slabs * cells)
    gathered = lax.all_to_all(
        sum_part(received, scale), "space", split_axis=0, concat_axis=0, tiled=True
    )
    filter_grad, group_grad = final_part(gathered.reshape(rows, 128), taps, outputs, width)

    mixed, input_grad = mix_part(
        act_low, active, along_space(lowest, -1), framed_grad, group_filter, side
    )
    return (
        jnp.transpose(mixed, (1, 0, 2)),
        jnp.transpose(input_grad, (1, 0, 2)),
        filter_grad,
        jnp.transpose(group_grad, (0, 2, 1)),
    )


def solution(mesh):
    return jax.shard_map(
        body,
        mesh=mesh,
        in_specs=(
            P("chan", "space", None),
            P(None, "chan", None),
            P(None, "chan", None),
            P("chan", "space", None),
        ),
        out_specs=(
            P("chan", "space", None),
            P("chan", "space", None),
            P(None, "chan", None),
            P(None, "chan", None),
        ),
        check_vma=False,
    )
```

time: 108 us -> 76.8 us (0.71)
  blocking collectives: 16.2 us -> 0 us
  waiting for transfers between devices: 33.3 us -> 28.2 us
  starting transfers between devices: 43.8 us -> 38.8 us
  Pallas kernels: 8.39 us -> 6.05 us
  local copies, waits for them, and re-layouts: 4.4 us -> 2.58 us
    all_gather x1 -> x0, blocking collectives: 16.2 us -> none  [body(): grad_all = lax.all_gather(hidden_grad, 'chan', axis=0, tiled=True)]
    all_to_all x1 -> x0, waiting for transfers between devices: 11.2 us -> none  [body(): lax.all_to_all(split_filter(conv_in, blocks), 'chan', split_axis=0, conca...]
    ppermute x6 -> x4, starting transfers between devices: 12.6 us -> 3.53 us  [along_space(): lax.ppermute(block, 'space', [(i, (i + step) % slabs) for i in range(slab...]
    ppermute x4 -> x7, starting transfers between devices: 10.2 us -> 16.1 us  [along_chips(): lax.ppermute(block, 'chan', [(i, (i + 2 * step) % blocks) for i in range(...]
    all_to_all x1 -> x0, starting transfers between devices: 3.41 us -> none  [body(): lax.all_to_all(split_filter(conv_in, blocks), 'chan', split_axis=0, conca...]
    ppermute x4 -> x7, waiting for transfers between devices: 4.17 us -> 7.41 us  [along_chips(): lax.ppermute(block, 'chan', [(i, (i + 2 * step) % blocks) for i in range(...]
    ppermute x5, waiting for transfers between devices: 0.03 us -> 2.8 us  [other_core(): return lax.ppermute(block, 'chan', [(i, i ^ 1) for i in range(blocks)])]
    pallas_call x7 -> x8, Pallas kernels: 8.39 us -> 6.05 us  [call(): pl.pallas_call(kernel, out_shape=outs, in_specs=[whole] * len(args), out_...]
  transfers between devices with their start and end apart: 18 -> 18, of which waited for: 9 -> 9; matrix products, arithmetic and copies ran while one was open for 2% -> 2% of each run, Pallas kernels for 4% -> 3%
where the time goes in v2:
time: 76.8 us; the launch traced here: 76.5 us
  starting transfers between devices  38.8 us (51%)
  waiting for transfers between devices  28.2 us (37%)
  Pallas kernels  6.05 us (8%)
  local copies, waits for them, and re-layouts  2.58 us (3%)
  between operations  0.9 us (1%)
    ppermute x7, starting transfers between devices, along_chips(): lax.ppermute(block, 'chan', [(i, (i + 2 * step) % blocks) for i in range(...  16.1 us
    ppermute x4, waiting for transfers between devices, along_space(): lax.ppermute(block, 'space', [(i, (i + step) % slabs) for i in range(slab...  15.1 us
    all_to_all x1, starting transfers between devices, body(): lax.all_to_all(terms.reshape(slabs, rows // slabs, 128), 'space', split_a...  10.1 us
    all_to_all x1, starting transfers between devices, body(): lax.all_to_all(sum_part(received, scale), 'space', split_axis=0, concat_a...  8.09 us
    ppermute x7, waiting for transfers between devices, along_chips(): lax.ppermute(block, 'chan', [(i, (i + 2 * step) % blocks) for i in range(...  7.41 us
    pallas_call x8, Pallas kernels, call(): pl.pallas_call(kernel, out_shape=outs, in_specs=[whole] * len(args), out_...  6.05 us
    ppermute x4, starting transfers between devices, along_space(): lax.ppermute(block, 'space', [(i, (i + step) % slabs) for i in range(slab...  3.53 us
    all_to_all x1, waiting for transfers between devices, body(): lax.all_to_all(terms.reshape(slabs, rows // slabs, 128), 'space', split_a...  2.88 us
  transfers between devices with their start and end apart: 18, of which 9 were waited for; matrix products, arithmetic and copies ran while one was open for 2% of the time, Pallas kernels for 3%

profile of v2, /device:TPU:62, one launch (start us, length us, event | category | flops | bytes accessed | tf_op | source)
XLA Modules:
  0.0 76.5 jit_solution(1379456701172999485)
XLA Ops:
  0.6 1.0 %copy.14 = bf16[16,4,1024]{2,0,1:T(8,128)(2,1)S(1)} copy(bf16[16,4,1024]{2,1,0:T(4,128)(2,1)} %param.4) | data formatting | bytes 262144 | tf_op args[0]
  1.7 1.5 %collective-permute-start = (bf16[96,256]{1,0:T(8,128)(2,1)S(1)}, bf16[96,256]{1,0:T(8,128)(2,1)S(1)}, u32[]{:S(2)}, u32[]{:S(2)}) collective-permute-start(bf16[96,256]{1,0:T(8,128)(2,1)S(1)} %get-tuple-element.34), channel_id=1, source_target_pairs={{0,8},{8,16},{16,24},{24,32},{32,40},{40,48},{48,56},{56,64},{64,7... | collective-permute-start | bytes 147464 | tf_op jit(solution)/shard_map/ppermute | solution.py:410
  3.2 0.6 collective-permute-start.1
  3.8 7.4 %collective-permute-done.1.high_ref = bf16[32,256]{1,0:T(8,128)(2,1)S(1)} collective-permute-done((bf16[32,256]{1,0:T(8,128)(2,1)S(1)}, bf16[32,256]{1,0:T(8,128)(2,1)S(1)}, u32[]{:S(2)}, u32[]{:S(2)}) %collective-permute-start.1) | collective-permute-done | bytes 16416 | tf_op jit(solution)/shard_map/ppermute | solution.py:410
  11.2 3.2 %collective-permute-start.2 = (bf16[320,256]{1,0:T(8,128)(2,1)S(1)}, bf16[320,256]{1,0:T(8,128)(2,1)S(1)}, u32[]{:S(2)}, u32[]{:S(2)}) collective-permute-start(bf16[320,256]{1,0:T(8,128)(2,1)S(1)} %pad_maximum_fusion.1.refs_3_), channel_id=1, source_target_pairs={{0,2},{1,3},{2,4},{3,5},{4,6},{5,7},{6,0},{7,1},{8,10},{9,11},{10,... | collective-permute-start | bytes 491528 | tf_op jit(solution)/shard_map/ppermute | solution.py:413
  14.4 3.3 %collective-permute-start.4 = (bf16[320,256]{1,0:T(8,128)(2,1)S(1)}, bf16[320,256]{1,0:T(8,128)(2,1)S(1)}, u32[]{:S(2)}, u32[]{:S(2)}) collective-permute-start(bf16[320,256]{1,0:T(8,128)(2,1)S(1)} %pad_maximum_fusion.1.refs_3_), channel_id=1, source_target_pairs={{0,6},{1,7},{2,0},{3,1},{4,2},{5,3},{6,4},{7,5},{8,14},{9,15},{10,... | collective-permute-start | bytes 491528 | tf_op jit(solution)/shard_map/ppermute | solution.py:413
  17.7 0.5 shard_map.77
  18.2 0.5 shard_map.76
  18.7 3.0 %collective-permute-done.2.refs_5_ = bf16[320,256]{1,0:T(8,128)(2,1)S(1)} collective-permute-done((bf16[320,256]{1,0:T(8,128)(2,1)S(1)}, bf16[320,256]{1,0:T(8,128)(2,1)S(1)}, u32[]{:S(2)}, u32[]{:S(2)}) %collective-permute-start.2) | collective-permute-done | bytes 163872 | tf_op jit(solution)/shard_map/ppermute | solution.py:413
  21.8 1.9 %collective-permute-done.4.refs_6_ = bf16[320,256]{1,0:T(8,128)(2,1)S(1)} collective-permute-done((bf16[320,256]{1,0:T(8,128)(2,1)S(1)}, bf16[320,256]{1,0:T(8,128)(2,1)S(1)}, u32[]{:S(2)}, u32[]{:S(2)}) %collective-permute-start.4) | collective-permute-done | bytes 163872 | tf_op jit(solution)/shard_map/ppermute | solution.py:413
  23.7 2.3 %collective-permute-start.7 = (bf16[160,256]{1,0:T(8,128)(2,1)S(1)}, bf16[160,256]{1,0:T(8,128)(2,1)S(1)}, u32[]{:S(2)}, u32[]{:S(2)}) collective-permute-start(bf16[160,256]{1,0:T(8,128)(2,1)S(1)} %slice.49), channel_id=1, source_target_pairs={{0,6},{1,7},{2,0},{3,1},{4,2},{5,3},{6,4},{7,5},{8,14},{9,15},{10,... | collective-permute-start | bytes 245768 | tf_op jit(solution)/shard_map/ppermute | solution.py:413
  26.1 0.5 collective-permute-start.3
  26.6 1.7 %collective-permute-done.6.refs_8_ = bf16[160,256]{1,0:T(8,128)(2,1)S(1)} collective-permute-done((bf16[160,256]{1,0:T(8,128)(2,1)S(1)}, bf16[160,256]{1,0:T(8,128)(2,1)S(1)}, u32[]{:S(2)}, u32[]{:S(2)}) %collective-permute-start.6) | collective-permute-done | bytes 81952 | tf_op jit(solution)/shard_map/ppermute | solution.py:413
  28.3 0.7 collective-permute-done.7.refs_9_
  29.2 1.4 %collective-permute-done.8.refs_10_ = bf16[320,256]{1,0:T(8,128)(2,1)S(1)} collective-permute-done((bf16[320,256]{1,0:T(8,128)(2,1)S(1)}, bf16[320,256]{1,0:T(8,128)(2,1)S(1)}, u32[]{:S(2)}, u32[]{:S(2)}) %collective-permute-start.8) | collective-permute-done | bytes 163872 | tf_op jit(solution)/shard_map/ppermute | solution.py:418
  30.5 2.4 %shard_map.78 = (bf16[32,512]{1,0:T(8,128)(2,1)S(1)}, bf16[64,256]{1,0:T(8,128)(2,1)S(1)}, bf16[1024,128]{1,0:T(8,128)(2,1)}) custom-call(bf16[27,32,128]{2,1,0:T(8,128)(2,1)S(1)} %copy-done, f32[32,512]{1,0:T(8,128)S(1)} %get-tuple-element.43.refs_1_, bf16[864,512]{1,0:T(8,128)(2,1)S(1)} %get-tuple-element.44.refs_2_, ...), custom_call_target="tpu_custom_call" | custom-call | tf_op jit(solution)/shard_map/pallas_call | solution.py:43
  33.0 3.5 %collective-permute-start.9 = (bf16[192,256]{1,0:T(8,128)(2,1)S(1)}, bf16[192,256]{1,0:T(8,128)(2,1)S(1)}, u32[]{:S(2)}, u32[]{:S(2)}) collective-permute-start(bf16[192,256]{1,0:T(8,128)(2,1)S(1)} %get-tuple-element.70), channel_id=1, source_target_pairs={{0,2},{1,3},{2,4},{3,5},{4,6},{5,7},{6,0},{7,1},{8,10},{9,11},{10,... | collective-permute-start | bytes 294920 | tf_op jit(solution)/shard_map/ppermute | solution.py:413
  36.5 0.8 %collective-permute-start.11 = (bf16[32,256]{1,0:T(8,128)(2,1)S(1)}, bf16[32,256]{1,0:T(8,128)(2,1)S(1)}, u32[]{:S(2)}, u32[]{:S(2)}) collective-permute-start(bf16[32,256]{1,0:T(8,128)(2,1)S(1)} %slice.41), channel_id=1, source_target_pairs={{0,8},{8,16},{16,24},{24,32},{32,40},{40,48},{48,56},{56,64},{64,7... | collective-permute-start | bytes 49160 | tf_op jit(solution)/shard_map/ppermute | solution.py:410
  37.3 1.4 %collective-permute-start.12 = (bf16[192,256]{1,0:T(8,128)(2,1)S(1)}, bf16[192,256]{1,0:T(8,128)(2,1)S(1)}, u32[]{:S(2)}, u32[]{:S(2)}) collective-permute-start(bf16[192,256]{1,0:T(8,128)(2,1)S(1)} %get-tuple-element.69), channel_id=1, source_target_pairs={{0,6},{1,7},{2,0},{3,1},{4,2},{5,3},{6,4},{7,5},{8,14},{9,15},{10,... | collective-permute-start | bytes 294920 | tf_op jit(solution)/shard_map/ppermute | solution.py:413
  38.7 2.3 %collective-permute-start.13 = (bf16[192,256]{1,0:T(8,128)(2,1)S(1)}, bf16[192,256]{1,0:T(8,128)(2,1)S(1)}, u32[]{:S(2)}, u32[]{:S(2)}) collective-permute-start(bf16[192,256]{1,0:T(8,128)(2,1)S(1)} %get-tuple-element.68), channel_id=1, source_target_pairs={{0,4},{1,5},{2,6},{3,7},{4,0},{5,1},{6,2},{7,3},{8,12},{9,13},{10,... | collective-permute-start | bytes 294920 | tf_op jit(solution)/shard_map/ppermute | solution.py:413
  41.0 10.1 %all-to-all-start = ((bf16[32,32,128]{2,1,0:T(8,128)(2,1)}), bf16[32,32,128]{2,1,0:T(8,128)(2,1)S(1)}, u32[]{:S(2)}, u32[]{:S(2)}) async-start(bf16[32,32,128]{2,1,0:T(8,128)(2,1)} %bitcast.3), calls=%async_computation | async-start | bytes 524288 | tf_op jit(solution)/shard_map/all_to_all | solution.py:458
  51.6 1.4 %collective-permute-done.14.refs_3_ = bf16[384,256]{1,0:T(8,128)(2,1)S(1)} collective-permute-done((bf16[384,256]{1,0:T(8,128)(2,1)S(1)}, bf16[384,256]{1,0:T(8,128)(2,1)S(1)}, u32[]{:S(2)}, u32[]{:S(2)}) %collective-permute-start.14) | collective-permute-done | bytes 196640 | tf_op jit(solution)/shard_map/ppermute | solution.py:418
  53.0 0.5 shard_map.79
  53.5 2.9 %all-to-all-done.src = bf16[32,32,128]{2,1,0:T(8,128)(2,1)S(1)} async-done(((bf16[32,32,128]{2,1,0:T(8,128)(2,1)}), bf16[32,32,128]{2,1,0:T(8,128)(2,1)S(1)}, u32[]{:S(2)}, u32[]{:S(2)}) %all-to-all-start) | async-done | bytes 262176 | tf_op jit(solution)/shard_map/all_to_all | solution.py:458
  56.4 0.8 shard_map.81
  57.1 8.1 %all-to-all-start.1 = ((bf16[32,32,128]{2,1,0:T(8,128)(2,1)}), bf16[32,32,128]{2,1,0:T(8,128)(2,1)S(1)}, u32[]{:S(2)}, u32[]{:S(2)}) async-start(bf16[32,32,128]{2,1,0:T(8,128)(2,1)} %shard_map.81), calls=%async_computation.1 | async-start | bytes 524288 | tf_op jit(solution)/shard_map/all_to_all | solution.py:485
  65.2 0.6 collective-permute-start.15
  65.9 7.8 %collective-permute-done.15.packed_ref = bf16[96,256]{1,0:T(8,128)(2,1)S(1)} collective-permute-done((bf16[96,256]{1,0:T(8,128)(2,1)S(1)}, bf16[96,256]{1,0:T(8,128)(2,1)S(1)}, u32[]{:S(2)}, u32[]{:S(2)}) %collective-permute-start.15) | collective-permute-done | bytes 49184 | tf_op jit(solution)/shard_map/ppermute | solution.py:410
  73.6 0.6 shard_map.80
  74.2 0.9 %copy.11 = f32[16,4,1024]{2,1,0:T(4,128)} copy(f32[16,4,1024]{2,0,1:T(8,128)S(1)} %bitcast.14) | data formatting | bytes 524288
  75.1 0.6 copy.10
  75.7 0.8 %shard_map.82 = (f32[27,32,128]{2,1,0:T(8,128)}, f32[27,8,32]{2,1,0:T(8,128)}) custom-call(bf16[1024,128]{1,0:T(8,128)(2,1)S(1)} %bitcast.12), custom_call_target="tpu_custom_call" | custom-call | tf_op jit(solution)/shard_map/pallas_call | solution.py:43
  (39 shorter events, 0.7 us)
Async XLA Ops:
  0.6 1.0 %copy-start.2 = (bf16[32,2,256]{2,1,0:T(2,128)(2,1)S(1)}, bf16[32,2,256]{2,1,0:T(2,128)(2,1)}, u32[]{:S(2)}) copy-start(bf16[32,2,256]{2,1,0:T(2,128)(2,1)} %param.7) | copy-start | bytes 98308
  1.6 16.1 %copy-start = (bf16[27,32,128]{2,1,0:T(8,128)(2,1)S(1)}, bf16[27,32,128]{2,1,0:T(8,128)(2,1)}, u32[]{:S(2)}) copy-start(bf16[27,32,128]{2,1,0:T(8,128)(2,1)} %refs_0_.1) | copy-start | bytes 663556
  1.7 9.5 %collective-permute-start = (bf16[96,256]{1,0:T(8,128)(2,1)S(1)}, bf16[96,256]{1,0:T(8,128)(2,1)S(1)}, u32[]{:S(2)}, u32[]{:S(2)}) collective-permute-start(bf16[96,256]{1,0:T(8,128)(2,1)S(1)} %get-tuple-element.34), channel_id=1, source_target_pairs={{0,8},{8,16},{16,24},{24,32},{32,40},{40,48},{48,56},{56,64},{64,7... | collective-permute-start | bytes 147464 | tf_op jit(solution)/shard_map/ppermute | solution.py:410
  3.2 8.0 %collective-permute-start.1 = (bf16[32,256]{1,0:T(8,128)(2,1)S(1)}, bf16[32,256]{1,0:T(8,128)(2,1)S(1)}, u32[]{:S(2)}, u32[]{:S(2)}) collective-permute-start(bf16[32,256]{1,0:T(8,128)(2,1)S(1)} %slice.37), channel_id=1, source_target_pairs={{0,248},{8,0},{16,8},{24,16},{32,24},{40,32},{48,40},{56,48},{64,5... | collective-permute-start | bytes 49160 | tf_op jit(solution)/shard_map/ppermute | solution.py:410
  11.1 7.1 %copy-start.1 = (bf16[27,32,8]{1,2,0:T(8,128)(2,1)S(1)}, bf16[27,32,8]{1,2,0:T(8,128)(2,1)}, u32[]{:S(2)}) copy-start(bf16[27,32,8]{1,2,0:T(8,128)(2,1)} %param.6) | copy-start | bytes 41476
  11.2 10.6 %collective-permute-start.2 = (bf16[320,256]{1,0:T(8,128)(2,1)S(1)}, bf16[320,256]{1,0:T(8,128)(2,1)S(1)}, u32[]{:S(2)}, u32[]{:S(2)}) collective-permute-start(bf16[320,256]{1,0:T(8,128)(2,1)S(1)} %pad_maximum_fusion.1.refs_3_), channel_id=1, source_target_pairs={{0,2},{1,3},{2,4},{3,5},{4,6},{5,7},{6,0},{7,1},{8,10},{9,11},{10,... | collective-permute-start | bytes 491528 | tf_op jit(solution)/shard_map/ppermute | solution.py:413
  14.4 9.3 %collective-permute-start.4 = (bf16[320,256]{1,0:T(8,128)(2,1)S(1)}, bf16[320,256]{1,0:T(8,128)(2,1)S(1)}, u32[]{:S(2)}, u32[]{:S(2)}) collective-permute-start(bf16[320,256]{1,0:T(8,128)(2,1)S(1)} %pad_maximum_fusion.1.refs_3_), channel_id=1, source_target_pairs={{0,6},{1,7},{2,0},{3,1},{4,2},{5,3},{6,4},{7,5},{8,14},{9,15},{10,... | collective-permute-start | bytes 491528 | tf_op jit(solution)/shard_map/ppermute | solution.py:413
  21.7 6.6 %collective-permute-start.6 = (bf16[160,256]{1,0:T(8,128)(2,1)S(1)}, bf16[160,256]{1,0:T(8,128)(2,1)S(1)}, u32[]{:S(2)}, u32[]{:S(2)}) collective-permute-start(bf16[160,256]{1,0:T(8,128)(2,1)S(1)} %slice.38), channel_id=1, source_target_pairs={{0,2},{1,3},{2,4},{3,5},{4,6},{5,7},{6,0},{7,1},{8,10},{9,11},{10,... | collective-permute-start | bytes 245768 | tf_op jit(solution)/shard_map/ppermute | solution.py:413
  23.7 5.3 %collective-permute-start.7 = (bf16[160,256]{1,0:T(8,128)(2,1)S(1)}, bf16[160,256]{1,0:T(8,128)(2,1)S(1)}, u32[]{:S(2)}, u32[]{:S(2)}) collective-permute-start(bf16[160,256]{1,0:T(8,128)(2,1)S(1)} %slice.49), channel_id=1, source_target_pairs={{0,6},{1,7},{2,0},{3,1},{4,2},{5,3},{6,4},{7,5},{8,14},{9,15},{10,... | collective-permute-start | bytes 245768 | tf_op jit(solution)/shard_map/ppermute | solution.py:413
  26.0 4.5 %collective-permute-start.5 = (bf16[640,256]{1,0:T(8,128)(2,1)S(1)}, bf16[640,256]{1,0:T(8,128)(2,1)S(1)}, u32[]{:S(2)}, u32[]{:S(2)}) collective-permute-start(bf16[640,256]{1,0:T(8,128)(2,1)S(1)} %pad_maximum_fusion), channel_id=1, source_target_pairs={{0,1},{1,0},{2,3},{3,2},{4,5},{5,4},{6,7},{7,6},{8,9},{9,8},{10,11... | collective-permute-start | bytes 983048 | tf_op jit(solution)/shard_map/ppermute | solution.py:418
  26.1 3.1 %collective-permute-start.3 = (bf16[320,256]{1,0:T(8,128)(2,1)S(1)}, bf16[320,256]{1,0:T(8,128)(2,1)S(1)}, u32[]{:S(2)}, u32[]{:S(2)}) collective-permute-start(bf16[320,256]{1,0:T(8,128)(2,1)S(1)} %pad_maximum_fusion.1.refs_3_), channel_id=1, source_target_pairs={{0,1},{1,0},{2,3},{3,2},{4,5},{5,4},{6,7},{7,6},{8,9},{9,8},{10,11... | collective-permute-start | bytes 491528 | tf_op jit(solution)/shard_map/ppermute | solution.py:418
  29.0 1.5 %collective-permute-start.8 = (bf16[320,256]{1,0:T(8,128)(2,1)S(1)}, bf16[320,256]{1,0:T(8,128)(2,1)S(1)}, u32[]{:S(2)}, u32[]{:S(2)}) collective-permute-start(bf16[320,256]{1,0:T(8,128)(2,1)S(1)} %pad_maximum_fusion.2), channel_id=1, source_target_pairs={{0,1},{1,0},{2,3},{3,2},{4,5},{5,4},{6,7},{7,6},{8,9},{9,8},{10,11... | collective-permute-start | bytes 491528 | tf_op jit(solution)/shard_map/ppermute | solution.py:418
  33.0 18.2 %collective-permute-start.9 = (bf16[192,256]{1,0:T(8,128)(2,1)S(1)}, bf16[192,256]{1,0:T(8,128)(2,1)S(1)}, u32[]{:S(2)}, u32[]{:S(2)}) collective-permute-start(bf16[192,256]{1,0:T(8,128)(2,1)S(1)} %get-tuple-element.70), channel_id=1, source_target_pairs={{0,2},{1,3},{2,4},{3,5},{4,6},{5,7},{6,0},{7,1},{8,10},{9,11},{10,... | collective-permute-start | bytes 294920 | tf_op jit(solution)/shard_map/ppermute | solution.py:413
  36.5 14.7 %collective-permute-start.10 = (bf16[128,256]{1,0:T(8,128)(2,1)S(1)}, bf16[128,256]{1,0:T(8,128)(2,1)S(1)}, u32[]{:S(2)}, u32[]{:S(2)}) collective-permute-start(bf16[128,256]{1,0:T(8,128)(2,1)S(1)} %pad_maximum_fusion.6), channel_id=1, source_target_pairs={{0,1},{1,0},{2,3},{3,2},{4,5},{5,4},{6,7},{7,6},{8,9},{9,8},{10,11... | collective-permute-start | bytes 196616 | tf_op jit(solution)/shard_map/ppermute | solution.py:418
  36.5 14.7 %collective-permute-start.11 = (bf16[32,256]{1,0:T(8,128)(2,1)S(1)}, bf16[32,256]{1,0:T(8,128)(2,1)S(1)}, u32[]{:S(2)}, u32[]{:S(2)}) collective-permute-start(bf16[32,256]{1,0:T(8,128)(2,1)S(1)} %slice.41), channel_id=1, source_target_pairs={{0,8},{8,16},{16,24},{24,32},{32,40},{40,48},{48,56},{56,64},{64,7... | collective-permute-start | bytes 49160 | tf_op jit(solution)/shard_map/ppermute | solution.py:410
  37.3 13.9 %collective-permute-start.12 = (bf16[192,256]{1,0:T(8,128)(2,1)S(1)}, bf16[192,256]{1,0:T(8,128)(2,1)S(1)}, u32[]{:S(2)}, u32[]{:S(2)}) collective-permute-start(bf16[192,256]{1,0:T(8,128)(2,1)S(1)} %get-tuple-element.69), channel_id=1, source_target_pairs={{0,6},{1,7},{2,0},{3,1},{4,2},{5,3},{6,4},{7,5},{8,14},{9,15},{10,... | collective-permute-start | bytes 294920 | tf_op jit(solution)/shard_map/ppermute | solution.py:413
  38.7 12.5 %collective-permute-start.13 = (bf16[192,256]{1,0:T(8,128)(2,1)S(1)}, bf16[192,256]{1,0:T(8,128)(2,1)S(1)}, u32[]{:S(2)}, u32[]{:S(2)}) collective-permute-start(bf16[192,256]{1,0:T(8,128)(2,1)S(1)} %get-tuple-element.68), channel_id=1, source_target_pairs={{0,4},{1,5},{2,6},{3,7},{4,0},{5,1},{6,2},{7,3},{8,12},{9,13},{10,... | collective-permute-start | bytes 294920 | tf_op jit(solution)/shard_map/ppermute | solution.py:413
  41.0 15.3 %all-to-all-start = ((bf16[32,32,128]{2,1,0:T(8,128)(2,1)}), bf16[32,32,128]{2,1,0:T(8,128)(2,1)S(1)}, u32[]{:S(2)}, u32[]{:S(2)}) async-start(bf16[32,32,128]{2,1,0:T(8,128)(2,1)} %bitcast.3), calls=%async_computation | async-start | bytes 524288 | tf_op jit(solution)/shard_map/all_to_all | solution.py:458
  51.3 1.7 %collective-permute-start.14 = (bf16[384,256]{1,0:T(8,128)(2,1)S(1)}, bf16[384,256]{1,0:T(8,128)(2,1)S(1)}, u32[]{:S(2)}, u32[]{:S(2)}) collective-permute-start(bf16[384,256]{1,0:T(8,128)(2,1)S(1)} %slice_dynamic-update-slice_fusion), channel_id=1, source_target_pairs={{0,1},{1,0},{2,3},{3,2},{4,5},{5,4},{6,7},{7,6},{8,9},{9,8},{10,11... | collective-permute-start | bytes 589832 | tf_op jit(solution)/shard_map/ppermute | solution.py:418
  57.1 18.6 %all-to-all-start.1 = ((bf16[32,32,128]{2,1,0:T(8,128)(2,1)}), bf16[32,32,128]{2,1,0:T(8,128)(2,1)S(1)}, u32[]{:S(2)}, u32[]{:S(2)}) async-start(bf16[32,32,128]{2,1,0:T(8,128)(2,1)} %shard_map.81), calls=%async_computation.1 | async-start | bytes 524288 | tf_op jit(solution)/shard_map/all_to_all | solution.py:485
  65.2 8.4 %collective-permute-start.15 = (bf16[96,256]{1,0:T(8,128)(2,1)S(1)}, bf16[96,256]{1,0:T(8,128)(2,1)S(1)}, u32[]{:S(2)}, u32[]{:S(2)}) collective-permute-start(bf16[96,256]{1,0:T(8,128)(2,1)S(1)} %get-tuple-element.57), channel_id=1, source_target_pairs={{0,248},{8,0},{16,8},{24,16},{32,24},{40,32},{48,40},{56,48},{64,5... | collective-permute-start | bytes 147464 | tf_op jit(solution)/shard_map/ppermute | solution.py:410

commit v3 on v2

--- a/solution.py
+++ b/solution.py
@@ -13,7 +13,7 @@
 TAPS = len(OFFSETS)
 BF16 = jnp.bfloat16
 F32 = jnp.float32
-VMEM_LIMIT = 48 * 1024 * 1024
+VMEM_LIMIT = 16 * 1024 * 1024
 
 
 def phase_of(row_k, col_k):
@@ -334,19 +334,19 @@
             weights, windows_ref[...], (((0,), (0,)), ((), ())), preferred_element_type=F32
         ).astype(BF16)
         for z in range(planes):
-            out_ref[z] = mixed[:, z * square : (z + 1) * square]
+            out_ref[:, z, :] = mixed[:, z * square : (z + 1) * square]
         for frame in range(in_planes - 1):
-            sum_ref[frame] = grad_ref[frame]
+            sum_ref[:, frame, :] = grad_ref[frame]
         for phase in range(4):
             at = slice(phase * square, (phase + 1) * square)
             from_above = packed_ref[phase * in_chan : (phase + 1) * in_chan, :].astype(F32)
-            sum_ref[in_planes - 1, :, at] = grad_ref[in_planes - 1, :, at] + from_above
+            sum_ref[:, in_planes - 1, at] = grad_ref[in_planes - 1, :, at] + from_above
 
     return call(
         kernel,
         (
-            jax.ShapeDtypeStruct((planes, outputs, square), BF16),
-            jax.ShapeDtypeStruct(framed_grad.shape, F32),
+            jax.ShapeDtypeStruct((outputs, planes, square), BF16),
+            jax.ShapeDtypeStruct((in_chan, in_planes, 4 * square), F32),
         ),
         low,
         active,
@@ -465,7 +465,7 @@
     far = along_chips(joined(hidden_grad, far), 2)
     block = 2 * outputs
     near = other_core(joined(hidden_grad, here[:block]))
-    up, near, act_low = lax.optimization_barrier((up, near, act_low))
+    up, near = lax.optimization_barrier((up, near))
     crossed = other_core(
         joined(*[part for ring in (up, down, far) for part in (ring[:block], ring[2 * block :])])
     )
@@ -480,7 +480,7 @@
     for ring, step in zip((up, down, far), steps):
         grads.append((ring, [(0, False, step, False), (block, True, step, False)]))
     framed_grad, lowest = input_part(grads, active, in_chan, side)
-    received, lowest = lax.optimization_barrier((received, lowest))
+    received, lowest, act_low = lax.optimization_barrier((received, lowest, act_low))
     scale = 1.0 / math.sqrt(slabs * cells)
     gathered = lax.all_to_all(
         sum_part(received, scale), "space", split_axis=0, concat_axis=0, tiled=True
@@ -491,8 +491,8 @@
         act_low, active, along_space(lowest, -1), framed_grad, group_filter, side
     )
     return (
-        jnp.transpose(mixed, (1, 0, 2)),
-        jnp.transpose(input_grad, (1, 0, 2)),
+        mixed,
+        input_grad,
         filter_grad,
         jnp.transpose(group_grad, (0, 2, 1)),
     )

time: 76.8 us -> 74.1 us (0.965)
  starting transfers between devices: 38.8 us -> 36.8 us
  local copies, waits for them, and re-layouts: 2.58 us -> 1.03 us
  Pallas kernels: 6.05 us -> 6.82 us
    ppermute x4, waiting for transfers between devices: 15.1 us -> 17.2 us  [along_space(): lax.ppermute(block, 'space', [(i, (i + step) % slabs) for i in range(slab...]
    all_to_all x1, waiting for transfers between devices: 2.88 us -> 1.17 us  [body(): lax.all_to_all(terms.reshape(slabs, rows // slabs, 128), 'space', split_a...]
    unnamed x15 -> x13, local copies, waits for them, and re-layouts: 2.55 us -> 1 us
    all_to_all x1, starting transfers between devices: 10.1 us -> 8.76 us  [body(): lax.all_to_all(terms.reshape(slabs, rows // slabs, 128), 'space', split_a...]
    pallas_call x8, Pallas kernels: 6.05 us -> 6.82 us  [call(): pl.pallas_call(kernel, out_shape=outs, in_specs=[whole] * len(args), out_...]
  transfers between devices with their start and end apart: 18 -> 18, of which waited for: 9 -> 10; matrix products, arithmetic and copies ran while one was open for 2% -> 0% of each run, Pallas kernels for 3% -> 4%
where the time goes in v3:
time: 74.1 us; the launch traced here: 73.8 us
  starting transfers between devices  36.8 us (50%)
  waiting for transfers between devices  28.1 us (38%)
  Pallas kernels  6.82 us (9%)
  local copies, waits for them, and re-layouts  1.03 us (1%)
  between operations  0.89 us (1%)
    ppermute x4, waiting for transfers between devices, along_space(): lax.ppermute(block, 'space', [(i, (i + step) % slabs) for i in range(slab...  17.2 us
    ppermute x7, starting transfers between devices, along_chips(): lax.ppermute(block, 'chan', [(i, (i + 2 * step) % blocks) for i in range(...  16.1 us
    all_to_all x1, starting transfers between devices, body(): lax.all_to_all(terms.reshape(slabs, rows // slabs, 128), 'space', split_a...  8.76 us
    all_to_all x1, starting transfers between devices, body(): lax.all_to_all(sum_part(received, scale), 'space', split_axis=0, concat_a...  8.01 us
    ppermute x7, waiting for transfers between devices, along_chips(): lax.ppermute(block, 'chan', [(i, (i + 2 * step) % blocks) for i in range(...  7.41 us
    pallas_call x8, Pallas kernels, call(): pl.pallas_call(kernel, out_shape=outs, in_specs=[whole] * len(args), out_...  6.82 us
    ppermute x4, starting transfers between devices, along_space(): lax.ppermute(block, 'space', [(i, (i + step) % slabs) for i in range(slab...  3.14 us
    ppermute x5, waiting for transfers between devices, other_core(): return lax.ppermute(block, 'chan', [(i, i ^ 1) for i in range(blocks)])  2.38 us
  transfers between devices with their start and end apart: 18, of which 10 were waited for; matrix products, arithmetic and copies ran while one was open for 0% of the time, Pallas kernels for 4%

profile of v3, /device:TPU:62, one launch (start us, length us, event | category | flops | bytes accessed | tf_op | source)
XLA Modules:
  0.0 73.8 jit_solution(10695546972280304784)
XLA Ops:
  0.6 1.0 %copy.12 = bf16[16,4,1024]{2,0,1:T(8,128)(2,1)S(1)} copy(bf16[16,4,1024]{2,1,0:T(4,128)(2,1)} %param.4) | data formatting | bytes 262144 | tf_op args[0]
  1.7 1.5 %collective-permute-start = (bf16[96,256]{1,0:T(8,128)(2,1)S(1)}, bf16[96,256]{1,0:T(8,128)(2,1)S(1)}, u32[]{:S(2)}, u32[]{:S(2)}) collective-permute-start(bf16[96,256]{1,0:T(8,128)(2,1)S(1)} %get-tuple-element.34), channel_id=1, source_target_pairs={{0,8},{8,16},{16,24},{24,32},{32,40},{40,48},{48,56},{56,64},{64,7... | collective-permute-start | bytes 147464 | tf_op jit(solution)/shard_map/ppermute | solution.py:410
  3.2 0.6 collective-permute-start.1
  3.8 7.4 %collective-permute-done.1.high_ref = bf16[32,256]{1,0:T(8,128)(2,1)S(1)} collective-permute-done((bf16[32,256]{1,0:T(8,128)(2,1)S(1)}, bf16[32,256]{1,0:T(8,128)(2,1)S(1)}, u32[]{:S(2)}, u32[]{:S(2)}) %collective-permute-start.1) | collective-permute-done | bytes 16416 | tf_op jit(solution)/shard_map/ppermute | solution.py:410
  11.2 3.2 %collective-permute-start.2 = (bf16[320,256]{1,0:T(8,128)(2,1)S(1)}, bf16[320,256]{1,0:T(8,128)(2,1)S(1)}, u32[]{:S(2)}, u32[]{:S(2)}) collective-permute-start(bf16[320,256]{1,0:T(8,128)(2,1)S(1)} %pad_maximum_fusion.1.refs_3_), channel_id=1, source_target_pairs={{0,2},{1,3},{2,4},{3,5},{4,6},{5,7},{6,0},{7,1},{8,10},{9,11},{10,... | collective-permute-start | bytes 491528 | tf_op jit(solution)/shard_map/ppermute | solution.py:413
  14.4 3.3 %collective-permute-start.4 = (bf16[320,256]{1,0:T(8,128)(2,1)S(1)}, bf16[320,256]{1,0:T(8,128)(2,1)S(1)}, u32[]{:S(2)}, u32[]{:S(2)}) collective-permute-start(bf16[320,256]{1,0:T(8,128)(2,1)S(1)} %pad_maximum_fusion.1.refs_3_), channel_id=1, source_target_pairs={{0,6},{1,7},{2,0},{3,1},{4,2},{5,3},{6,4},{7,5},{8,14},{9,15},{10,... | collective-permute-start | bytes 491528 | tf_op jit(solution)/shard_map/ppermute | solution.py:413
  17.7 0.5 shard_map.77
  18.2 0.5 shard_map.76
  18.7 3.0 %collective-permute-done.2.refs_5_ = bf16[320,256]{1,0:T(8,128)(2,1)S(1)} collective-permute-done((bf16[320,256]{1,0:T(8,128)(2,1)S(1)}, bf16[320,256]{1,0:T(8,128)(2,1)S(1)}, u32[]{:S(2)}, u32[]{:S(2)}) %collective-permute-start.2) | collective-permute-done | bytes 163872 | tf_op jit(solution)/shard_map/ppermute | solution.py:413
  21.8 1.9 %collective-permute-done.4.refs_6_ = bf16[320,256]{1,0:T(8,128)(2,1)S(1)} collective-permute-done((bf16[320,256]{1,0:T(8,128)(2,1)S(1)}, bf16[320,256]{1,0:T(8,128)(2,1)S(1)}, u32[]{:S(2)}, u32[]{:S(2)}) %collective-permute-start.4) | collective-permute-done | bytes 163872 | tf_op jit(solution)/shard_map/ppermute | solution.py:413
  23.7 2.3 %collective-permute-start.7 = (bf16[160,256]{1,0:T(8,128)(2,1)S(1)}, bf16[160,256]{1,0:T(8,128)(2,1)S(1)}, u32[]{:S(2)}, u32[]{:S(2)}) collective-permute-start(bf16[160,256]{1,0:T(8,128)(2,1)S(1)} %slice.49), channel_id=1, source_target_pairs={{0,6},{1,7},{2,0},{3,1},{4,2},{5,3},{6,4},{7,5},{8,14},{9,15},{10,... | collective-permute-start | bytes 245768 | tf_op jit(solution)/shard_map/ppermute | solution.py:413
  26.0 0.1 collective-permute-start.5
  26.1 0.5 collective-permute-start.3
  26.6 1.7 %collective-permute-done.6.refs_8_ = bf16[160,256]{1,0:T(8,128)(2,1)S(1)} collective-permute-done((bf16[160,256]{1,0:T(8,128)(2,1)S(1)}, bf16[160,256]{1,0:T(8,128)(2,1)S(1)}, u32[]{:S(2)}, u32[]{:S(2)}) %collective-permute-start.6) | collective-permute-done | bytes 81952 | tf_op jit(solution)/shard_map/ppermute | solution.py:413
  28.3 0.7 collective-permute-done.7.refs_9_
  29.2 1.4 %collective-permute-done.8.refs_10_ = bf16[320,256]{1,0:T(8,128)(2,1)S(1)} collective-permute-done((bf16[320,256]{1,0:T(8,128)(2,1)S(1)}, bf16[320,256]{1,0:T(8,128)(2,1)S(1)}, u32[]{:S(2)}, u32[]{:S(2)}) %collective-permute-start.8) | collective-permute-done | bytes 163872 | tf_op jit(solution)/shard_map/ppermute | solution.py:418
  30.5 2.4 %shard_map.78 = (bf16[32,512]{1,0:T(8,128)(2,1)S(1)}, bf16[64,256]{1,0:T(8,128)(2,1)S(1)}, bf16[1024,128]{1,0:T(8,128)(2,1)}) custom-call(bf16[27,32,128]{2,1,0:T(8,128)(2,1)S(1)} %copy-done, f32[32,512]{1,0:T(8,128)S(1)} %get-tuple-element.43.refs_1_, bf16[864,512]{1,0:T(8,128)(2,1)S(1)} %get-tuple-element.44.refs_2_, ...), custom_call_target="tpu_custom_call" | custom-call | tf_op jit(solution)/shard_map/pallas_call | solution.py:43
  33.0 3.5 %collective-permute-start.9 = (bf16[192,256]{1,0:T(8,128)(2,1)S(1)}, bf16[192,256]{1,0:T(8,128)(2,1)S(1)}, u32[]{:S(2)}, u32[]{:S(2)}) collective-permute-start(bf16[192,256]{1,0:T(8,128)(2,1)S(1)} %get-tuple-element.66), channel_id=1, source_target_pairs={{0,2},{1,3},{2,4},{3,5},{4,6},{5,7},{6,0},{7,1},{8,10},{9,11},{10,... | collective-permute-start | bytes 294920 | tf_op jit(solution)/shard_map/ppermute | solution.py:413
  36.5 0.8 %collective-permute-start.11 = (bf16[192,256]{1,0:T(8,128)(2,1)S(1)}, bf16[192,256]{1,0:T(8,128)(2,1)S(1)}, u32[]{:S(2)}, u32[]{:S(2)}) collective-permute-start(bf16[192,256]{1,0:T(8,128)(2,1)S(1)} %get-tuple-element.65), channel_id=1, source_target_pairs={{0,6},{1,7},{2,0},{3,1},{4,2},{5,3},{6,4},{7,5},{8,14},{9,15},{10,... | collective-permute-start | bytes 294920 | tf_op jit(solution)/shard_map/ppermute | solution.py:413
  37.3 3.0 %collective-permute-start.12 = (bf16[192,256]{1,0:T(8,128)(2,1)S(1)}, bf16[192,256]{1,0:T(8,128)(2,1)S(1)}, u32[]{:S(2)}, u32[]{:S(2)}) collective-permute-start(bf16[192,256]{1,0:T(8,128)(2,1)S(1)} %get-tuple-element.64), channel_id=1, source_target_pairs={{0,4},{1,5},{2,6},{3,7},{4,0},{5,1},{6,2},{7,3},{8,12},{9,13},{10,... | collective-permute-start | bytes 294920 | tf_op jit(solution)/shard_map/ppermute | solution.py:413
  40.3 8.8 %all-to-all-start = ((bf16[32,32,128]{2,1,0:T(8,128)(2,1)}), bf16[32,32,128]{2,1,0:T(8,128)(2,1)S(1)}, u32[]{:S(2)}, u32[]{:S(2)}) async-start(bf16[32,32,128]{2,1,0:T(8,128)(2,1)} %bitcast.3), calls=%async_computation | async-start | bytes 524288 | tf_op jit(solution)/shard_map/all_to_all | solution.py:458
  49.3 0.4 collective-permute-start.14
  49.7 1.0 %collective-permute-done.13.refs_3_ = bf16[384,256]{1,0:T(8,128)(2,1)S(1)} collective-permute-done((bf16[384,256]{1,0:T(8,128)(2,1)S(1)}, bf16[384,256]{1,0:T(8,128)(2,1)S(1)}, u32[]{:S(2)}, u32[]{:S(2)}) %collective-permute-start.13) | collective-permute-done | bytes 196640 | tf_op jit(solution)/shard_map/ppermute | solution.py:418
  50.7 0.5 shard_map.79
  51.2 2.1 %collective-permute-done.14.low_ref = bf16[32,256]{1,0:T(8,128)(2,1)S(1)} collective-permute-done((bf16[32,256]{1,0:T(8,128)(2,1)S(1)}, bf16[32,256]{1,0:T(8,128)(2,1)S(1)}, u32[]{:S(2)}, u32[]{:S(2)}) %collective-permute-start.14) | collective-permute-done | bytes 16416 | tf_op jit(solution)/shard_map/ppermute | solution.py:410
  53.3 1.2 %all-to-all-done.src = bf16[32,32,128]{2,1,0:T(8,128)(2,1)S(1)} async-done(((bf16[32,32,128]{2,1,0:T(8,128)(2,1)}), bf16[32,32,128]{2,1,0:T(8,128)(2,1)S(1)}, u32[]{:S(2)}, u32[]{:S(2)}) %all-to-all-start) | async-done | bytes 262176 | tf_op jit(solution)/shard_map/all_to_all | solution.py:458
  54.5 0.8 %shard_map.81 = bf16[32,32,128]{2,1,0:T(8,128)(2,1)} custom-call(bf16[32,32,128]{2,1,0:T(8,128)(2,1)S(1)} %all-to-all-done.src), custom_call_target="tpu_custom_call" | custom-call | tf_op jit(solution)/shard_map/pallas_call | solution.py:43
  55.2 8.0 %all-to-all-start.1 = ((bf16[32,32,128]{2,1,0:T(8,128)(2,1)}), bf16[32,32,128]{2,1,0:T(8,128)(2,1)S(1)}, u32[]{:S(2)}, u32[]{:S(2)}) async-start(bf16[32,32,128]{2,1,0:T(8,128)(2,1)} %shard_map.81), calls=%async_computation.1 | async-start | bytes 524288 | tf_op jit(solution)/shard_map/all_to_all | solution.py:485
  63.3 0.6 collective-permute-start.15
  63.9 7.8 %collective-permute-done.15.packed_ref = bf16[96,256]{1,0:T(8,128)(2,1)S(1)} collective-permute-done((bf16[96,256]{1,0:T(8,128)(2,1)S(1)}, bf16[96,256]{1,0:T(8,128)(2,1)S(1)}, u32[]{:S(2)}, u32[]{:S(2)}) %collective-permute-start.15) | collective-permute-done | bytes 49184 | tf_op jit(solution)/shard_map/ppermute | solution.py:410
  71.6 1.3 %shard_map.80 = (bf16[32,2,256]{2,1,0:T(2,128)(2,1)}, f32[16,4,1024]{2,1,0:T(4,128)}) custom-call(bf16[32,256]{1,0:T(8,128)(2,1)S(1)} %collective-permute-done.14.low_ref, bf16[32,512]{1,0:T(8,128)(2,1)S(1)} %get-tuple-element.47.active_ref.mid_ref, bf16[96,256]{1,0:T(8,128)(2,1)S(1)} %collective-permute-done.15.packed_ref, ...), custom_call_target="tpu_custom_call" | custom-call | tf_op jit(solution)/shard_map/pallas_call | solution.py:43
  73.0 0.8 %shard_map.82 = (f32[27,32,128]{2,1,0:T(8,128)}, f32[27,8,32]{2,1,0:T(8,128)}) custom-call(bf16[1024,128]{1,0:T(8,128)(2,1)S(1)} %bitcast.10), custom_call_target="tpu_custom_call" | custom-call | tf_op jit(solution)/shard_map/pallas_call | solution.py:43
  (37 shorter events, 0.4 us)
Async XLA Ops:
  0.6 1.0 %copy-start.2 = (bf16[32,2,256]{2,1,0:T(2,128)(2,1)S(1)}, bf16[32,2,256]{2,1,0:T(2,128)(2,1)}, u32[]{:S(2)}) copy-start(bf16[32,2,256]{2,1,0:T(2,128)(2,1)} %param.7) | copy-start | bytes 98308
  1.6 16.1 %copy-start = (bf16[27,32,128]{2,1,0:T(8,128)(2,1)S(1)}, bf16[27,32,128]{2,1,0:T(8,128)(2,1)}, u32[]{:S(2)}) copy-start(bf16[27,32,128]{2,1,0:T(8,128)(2,1)} %refs_0_.1) | copy-start | bytes 663556
  1.7 9.5 %collective-permute-start = (bf16[96,256]{1,0:T(8,128)(2,1)S(1)}, bf16[96,256]{1,0:T(8,128)(2,1)S(1)}, u32[]{:S(2)}, u32[]{:S(2)}) collective-permute-start(bf16[96,256]{1,0:T(8,128)(2,1)S(1)} %get-tuple-element.34), channel_id=1, source_target_pairs={{0,8},{8,16},{16,24},{24,32},{32,40},{40,48},{48,56},{56,64},{64,7... | collective-permute-start | bytes 147464 | tf_op jit(solution)/shard_map/ppermute | solution.py:410
  3.2 8.0 %collective-permute-start.1 = (bf16[32,256]{1,0:T(8,128)(2,1)S(1)}, bf16[32,256]{1,0:T(8,128)(2,1)S(1)}, u32[]{:S(2)}, u32[]{:S(2)}) collective-permute-start(bf16[32,256]{1,0:T(8,128)(2,1)S(1)} %slice.37), channel_id=1, source_target_pairs={{0,248},{8,0},{16,8},{24,16},{32,24},{40,32},{48,40},{56,48},{64,5... | collective-permute-start | bytes 49160 | tf_op jit(solution)/shard_map/ppermute | solution.py:410
  11.1 7.1 %copy-start.1 = (bf16[27,32,8]{1,2,0:T(8,128)(2,1)S(1)}, bf16[27,32,8]{1,2,0:T(8,128)(2,1)}, u32[]{:S(2)}) copy-start(bf16[27,32,8]{1,2,0:T(8,128)(2,1)} %param.6) | copy-start | bytes 41476
  11.2 10.6 %collective-permute-start.2 = (bf16[320,256]{1,0:T(8,128)(2,1)S(1)}, bf16[320,256]{1,0:T(8,128)(2,1)S(1)}, u32[]{:S(2)}, u32[]{:S(2)}) collective-permute-start(bf16[320,256]{1,0:T(8,128)(2,1)S(1)} %pad_maximum_fusion.1.refs_3_), channel_id=1, source_target_pairs={{0,2},{1,3},{2,4},{3,5},{4,6},{5,7},{6,0},{7,1},{8,10},{9,11},{10,... | collective-permute-start | bytes 491528 | tf_op jit(solution)/shard_map/ppermute | solution.py:413
  14.4 9.3 %collective-permute-start.4 = (bf16[320,256]{1,0:T(8,128)(2,1)S(1)}, bf16[320,256]{1,0:T(8,128)(2,1)S(1)}, u32[]{:S(2)}, u32[]{:S(2)}) collective-permute-start(bf16[320,256]{1,0:T(8,128)(2,1)S(1)} %pad_maximum_fusion.1.refs_3_), channel_id=1, source_target_pairs={{0,6},{1,7},{2,0},{3,1},{4,2},{5,3},{6,4},{7,5},{8,14},{9,15},{10,... | collective-permute-start | bytes 491528 | tf_op jit(solution)/shard_map/ppermute | solution.py:413
  21.7 6.6 %collective-permute-start.6 = (bf16[160,256]{1,0:T(8,128)(2,1)S(1)}, bf16[160,256]{1,0:T(8,128)(2,1)S(1)}, u32[]{:S(2)}, u32[]{:S(2)}) collective-permute-start(bf16[160,256]{1,0:T(8,128)(2,1)S(1)} %slice.38), channel_id=1, source_target_pairs={{0,2},{1,3},{2,4},{3,5},{4,6},{5,7},{6,0},{7,1},{8,10},{9,11},{10,... | collective-permute-start | bytes 245768 | tf_op jit(solution)/shard_map/ppermute | solution.py:413
  23.7 5.3 %collective-permute-start.7 = (bf16[160,256]{1,0:T(8,128)(2,1)S(1)}, bf16[160,256]{1,0:T(8,128)(2,1)S(1)}, u32[]{:S(2)}, u32[]{:S(2)}) collective-permute-start(bf16[160,256]{1,0:T(8,128)(2,1)S(1)} %slice.49), channel_id=1, source_target_pairs={{0,6},{1,7},{2,0},{3,1},{4,2},{5,3},{6,4},{7,5},{8,14},{9,15},{10,... | collective-permute-start | bytes 245768 | tf_op jit(solution)/shard_map/ppermute | solution.py:413
  26.0 4.5 %collective-permute-start.5 = (bf16[640,256]{1,0:T(8,128)(2,1)S(1)}, bf16[640,256]{1,0:T(8,128)(2,1)S(1)}, u32[]{:S(2)}, u32[]{:S(2)}) collective-permute-start(bf16[640,256]{1,0:T(8,128)(2,1)S(1)} %pad_maximum_fusion), channel_id=1, source_target_pairs={{0,1},{1,0},{2,3},{3,2},{4,5},{5,4},{6,7},{7,6},{8,9},{9,8},{10,11... | collective-permute-start | bytes 983048 | tf_op jit(solution)/shard_map/ppermute | solution.py:418
  26.1 3.1 %collective-permute-start.3 = (bf16[320,256]{1,0:T(8,128)(2,1)S(1)}, bf16[320,256]{1,0:T(8,128)(2,1)S(1)}, u32[]{:S(2)}, u32[]{:S(2)}) collective-permute-start(bf16[320,256]{1,0:T(8,128)(2,1)S(1)} %pad_maximum_fusion.1.refs_3_), channel_id=1, source_target_pairs={{0,1},{1,0},{2,3},{3,2},{4,5},{5,4},{6,7},{7,6},{8,9},{9,8},{10,11... | collective-permute-start | bytes 491528 | tf_op jit(solution)/shard_map/ppermute | solution.py:418
  29.0 1.5 %collective-permute-start.8 = (bf16[320,256]{1,0:T(8,128)(2,1)S(1)}, bf16[320,256]{1,0:T(8,128)(2,1)S(1)}, u32[]{:S(2)}, u32[]{:S(2)}) collective-permute-start(bf16[320,256]{1,0:T(8,128)(2,1)S(1)} %pad_maximum_fusion.2), channel_id=1, source_target_pairs={{0,1},{1,0},{2,3},{3,2},{4,5},{5,4},{6,7},{7,6},{8,9},{9,8},{10,11... | collective-permute-start | bytes 491528 | tf_op jit(solution)/shard_map/ppermute | solution.py:418
  33.0 16.1 %collective-permute-start.9 = (bf16[192,256]{1,0:T(8,128)(2,1)S(1)}, bf16[192,256]{1,0:T(8,128)(2,1)S(1)}, u32[]{:S(2)}, u32[]{:S(2)}) collective-permute-start(bf16[192,256]{1,0:T(8,128)(2,1)S(1)} %get-tuple-element.66), channel_id=1, source_target_pairs={{0,2},{1,3},{2,4},{3,5},{4,6},{5,7},{6,0},{7,1},{8,10},{9,11},{10,... | collective-permute-start | bytes 294920 | tf_op jit(solution)/shard_map/ppermute | solution.py:413
  36.5 12.6 %collective-permute-start.10 = (bf16[128,256]{1,0:T(8,128)(2,1)S(1)}, bf16[128,256]{1,0:T(8,128)(2,1)S(1)}, u32[]{:S(2)}, u32[]{:S(2)}) collective-permute-start(bf16[128,256]{1,0:T(8,128)(2,1)S(1)} %pad_maximum_fusion.6), channel_id=1, source_target_pairs={{0,1},{1,0},{2,3},{3,2},{4,5},{5,4},{6,7},{7,6},{8,9},{9,8},{10,11... | collective-permute-start | bytes 196616 | tf_op jit(solution)/shard_map/ppermute | solution.py:418
  36.5 12.6 %collective-permute-start.11 = (bf16[192,256]{1,0:T(8,128)(2,1)S(1)}, bf16[192,256]{1,0:T(8,128)(2,1)S(1)}, u32[]{:S(2)}, u32[]{:S(2)}) collective-permute-start(bf16[192,256]{1,0:T(8,128)(2,1)S(1)} %get-tuple-element.65), channel_id=1, source_target_pairs={{0,6},{1,7},{2,0},{3,1},{4,2},{5,3},{6,4},{7,5},{8,14},{9,15},{10,... | collective-permute-start | bytes 294920 | tf_op jit(solution)/shard_map/ppermute | solution.py:413
  37.3 11.9 %collective-permute-start.12 = (bf16[192,256]{1,0:T(8,128)(2,1)S(1)}, bf16[192,256]{1,0:T(8,128)(2,1)S(1)}, u32[]{:S(2)}, u32[]{:S(2)}) collective-permute-start(bf16[192,256]{1,0:T(8,128)(2,1)S(1)} %get-tuple-element.64), channel_id=1, source_target_pairs={{0,4},{1,5},{2,6},{3,7},{4,0},{5,1},{6,2},{7,3},{8,12},{9,13},{10,... | collective-permute-start | bytes 294920 | tf_op jit(solution)/shard_map/ppermute | solution.py:413
  40.3 14.2 %all-to-all-start = ((bf16[32,32,128]{2,1,0:T(8,128)(2,1)}), bf16[32,32,128]{2,1,0:T(8,128)(2,1)S(1)}, u32[]{:S(2)}, u32[]{:S(2)}) async-start(bf16[32,32,128]{2,1,0:T(8,128)(2,1)} %bitcast.3), calls=%async_computation | async-start | bytes 524288 | tf_op jit(solution)/shard_map/all_to_all | solution.py:458
  49.2 1.5 %collective-permute-start.13 = (bf16[384,256]{1,0:T(8,128)(2,1)S(1)}, bf16[384,256]{1,0:T(8,128)(2,1)S(1)}, u32[]{:S(2)}, u32[]{:S(2)}) collective-permute-start(bf16[384,256]{1,0:T(8,128)(2,1)S(1)} %slice_dynamic-update-slice_fusion), channel_id=1, source_target_pairs={{0,1},{1,0},{2,3},{3,2},{4,5},{5,4},{6,7},{7,6},{8,9},{9,8},{10,11... | collective-permute-start | bytes 589832 | tf_op jit(solution)/shard_map/ppermute | solution.py:418
  49.3 4.0 %collective-permute-start.14 = (bf16[32,256]{1,0:T(8,128)(2,1)S(1)}, bf16[32,256]{1,0:T(8,128)(2,1)S(1)}, u32[]{:S(2)}, u32[]{:S(2)}) collective-permute-start(bf16[32,256]{1,0:T(8,128)(2,1)S(1)} %slice.47), channel_id=1, source_target_pairs={{0,8},{8,16},{16,24},{24,32},{32,40},{40,48},{48,56},{56,64},{64,7... | collective-permute-start | bytes 49160 | tf_op jit(solution)/shard_map/ppermute | solution.py:410
  55.2 17.7 %all-to-all-start.1 = ((bf16[32,32,128]{2,1,0:T(8,128)(2,1)}), bf16[32,32,128]{2,1,0:T(8,128)(2,1)S(1)}, u32[]{:S(2)}, u32[]{:S(2)}) async-start(bf16[32,32,128]{2,1,0:T(8,128)(2,1)} %shard_map.81), calls=%async_computation.1 | async-start | bytes 524288 | tf_op jit(solution)/shard_map/all_to_all | solution.py:485
  63.3 8.4 %collective-permute-start.15 = (bf16[96,256]{1,0:T(8,128)(2,1)S(1)}, bf16[96,256]{1,0:T(8,128)(2,1)S(1)}, u32[]{:S(2)}, u32[]{:S(2)}) collective-permute-start(bf16[96,256]{1,0:T(8,128)(2,1)S(1)} %get-tuple-element.57), channel_id=1, source_target_pairs={{0,248},{8,0},{16,8},{24,16},{32,24},{40,32},{48,40},{56,48},{64,5... | collective-permute-start | bytes 147464 | tf_op jit(solution)/shard_map/ppermute | solution.py:410

commit v4 on v3

--- a/solution.py
+++ b/solution.py
@@ -157,6 +157,7 @@
         cotangent,
         high,
         group_filter,
+        flops=10**10,
     )
 
 
@@ -431,11 +432,10 @@
     slots = list(range(4 * (in_planes + 1)))
     length = len(slots) * in_chan
     cut = len(slots) // 2
-    own, up_high = lax.optimization_barrier((own, up_high))
     framed = joined(packed[:frame], own)
     from_low = along_chips(framed, 1)
     from_high = along_chips(framed, -1)
-    from_low, act_grad, sent = lax.optimization_barrier((from_low, act_grad, sent))
+    from_low, sent = lax.optimization_barrier((from_low, sent))
     far_low = along_chips(from_low[: cut * in_chan], 1)
     far_high = along_chips(from_high[cut * in_chan :], -1)
     near_other = other_core(joined(from_low, from_high))

time: 74.1 us -> 71.9 us (0.970)
  waiting for transfers between devices: 28.1 us -> 22.6 us
  starting transfers between devices: 36.8 us -> 40.2 us
    ppermute x4, waiting for transfers between devices: 17.2 us -> 12.5 us  [along_space(): lax.ppermute(block, 'space', [(i, (i + step) % slabs) for i in range(slab...]
    ppermute x7, starting transfers between devices: 16.1 us -> 18 us  [along_chips(): lax.ppermute(block, 'chan', [(i, (i + 2 * step) % blocks) for i in range(...]
    ppermute x4, starting transfers between devices: 3.14 us -> 4.71 us  [along_space(): lax.ppermute(block, 'space', [(i, (i + step) % slabs) for i in range(slab...]
    ppermute x5, waiting for transfers between devices: 2.38 us -> 1.61 us  [other_core(): return lax.ppermute(block, 'chan', [(i, i ^ 1) for i in range(blocks)])]
  transfers between devices with their start and end apart: 18 -> 18, of which waited for: 10 -> 9; matrix products, arithmetic and copies ran while one was open for 0% -> 0% of each run, Pallas kernels for 4% -> 4%
where the time goes in v4:
time: 71.9 us; the launch traced here: 71.6 us
  starting transfers between devices  40.2 us (56%)
  waiting for transfers between devices  22.6 us (31%)
  Pallas kernels  6.82 us (9%)
  local copies, waits for them, and re-layouts  1.04 us (1%)
  between operations  0.91 us (1%)
    ppermute x7, starting transfers between devices, along_chips(): lax.ppermute(block, 'chan', [(i, (i + 2 * step) % blocks) for i in range(...  18 us
    ppermute x4, waiting for transfers between devices, along_space(): lax.ppermute(block, 'space', [(i, (i + step) % slabs) for i in range(slab...  12.5 us
    all_to_all x1, starting transfers between devices, body(): lax.all_to_all(terms.reshape(slabs, rows // slabs, 128), 'space', split_a...  9.04 us
    all_to_all x1, starting transfers between devices, body(): lax.all_to_all(sum_part(received, scale), 'space', split_axis=0, concat_a...  8.14 us
    ppermute x7, waiting for transfers between devices, along_chips(): lax.ppermute(block, 'chan', [(i, (i + 2 * step) % blocks) for i in range(...  7.31 us
    pallas_call x8, Pallas kernels, call(): pl.pallas_call(kernel, out_shape=outs, in_specs=[whole] * len(args), out_...  6.82 us
    ppermute x4, starting transfers between devices, along_space(): lax.ppermute(block, 'space', [(i, (i + step) % slabs) for i in range(slab...  4.71 us
    ppermute x5, waiting for transfers between devices, other_core(): return lax.ppermute(block, 'chan', [(i, i ^ 1) for i in range(blocks)])  1.61 us
  transfers between devices with their start and end apart: 18, of which 9 were waited for; matrix products, arithmetic and copies ran while one was open for 0% of the time, Pallas kernels for 4%

profile of v4, /device:TPU:62, one launch (start us, length us, event | category | flops | bytes accessed | tf_op | source)
XLA Modules:
  0.0 71.6 jit_solution(7794905668949570217)
XLA Ops:
  0.6 1.0 %copy.12 = bf16[16,4,1024]{2,0,1:T(8,128)(2,1)S(1)} copy(bf16[16,4,1024]{2,1,0:T(4,128)(2,1)} %param.4) | data formatting | bytes 262144 | tf_op args[0]
  1.7 1.5 %collective-permute-start = (bf16[96,256]{1,0:T(8,128)(2,1)S(1)}, bf16[96,256]{1,0:T(8,128)(2,1)S(1)}, u32[]{:S(2)}, u32[]{:S(2)}) collective-permute-start(bf16[96,256]{1,0:T(8,128)(2,1)S(1)} %get-tuple-element.32), channel_id=1, source_target_pairs={{0,8},{8,16},{16,24},{24,32},{32,40},{40,48},{48,56},{56,64},{64,7... | collective-permute-start | bytes 147464 | tf_op jit(solution)/shard_map/ppermute | solution.py:411
  3.2 2.7 %collective-permute-done.low_ref = bf16[96,256]{1,0:T(8,128)(2,1)S(1)} collective-permute-done((bf16[96,256]{1,0:T(8,128)(2,1)S(1)}, bf16[96,256]{1,0:T(8,128)(2,1)S(1)}, u32[]{:S(2)}, u32[]{:S(2)}) %collective-permute-start) | collective-permute-done | bytes 49184 | tf_op jit(solution)/shard_map/ppermute | solution.py:411
  5.8 3.3 %collective-permute-start.3 = (bf16[320,256]{1,0:T(8,128)(2,1)S(1)}, bf16[320,256]{1,0:T(8,128)(2,1)S(1)}, u32[]{:S(2)}, u32[]{:S(2)}) collective-permute-start(bf16[320,256]{1,0:T(8,128)(2,1)S(1)} %pad_maximum_fusion.1.refs_3_), channel_id=1, source_target_pairs={{0,2},{1,3},{2,4},{3,5},{4,6},{5,7},{6,0},{7,1},{8,10},{9,11},{10,... | collective-permute-start | bytes 491528 | tf_op jit(solution)/shard_map/ppermute | solution.py:414
  9.2 2.2 %collective-permute-start.4 = (bf16[320,256]{1,0:T(8,128)(2,1)S(1)}, bf16[320,256]{1,0:T(8,128)(2,1)S(1)}, u32[]{:S(2)}, u32[]{:S(2)}) collective-permute-start(bf16[320,256]{1,0:T(8,128)(2,1)S(1)} %pad_maximum_fusion.1.refs_3_), channel_id=1, source_target_pairs={{0,6},{1,7},{2,0},{3,1},{4,2},{5,3},{6,4},{7,5},{8,14},{9,15},{10,... | collective-permute-start | bytes 491528 | tf_op jit(solution)/shard_map/ppermute | solution.py:414
  11.4 1.9 %collective-permute-start.1 = (bf16[32,256]{1,0:T(8,128)(2,1)S(1)}, bf16[32,256]{1,0:T(8,128)(2,1)S(1)}, u32[]{:S(2)}, u32[]{:S(2)}) collective-permute-start(bf16[32,256]{1,0:T(8,128)(2,1)S(1)} %slice.36), channel_id=1, source_target_pairs={{0,248},{8,0},{16,8},{24,16},{32,24},{40,32},{48,40},{56,48},{64,5... | collective-permute-start | bytes 49160 | tf_op jit(solution)/shard_map/ppermute | solution.py:411
  13.3 0.5 shard_map.77
  13.8 0.1 collective-permute-start.2
  13.9 2.3 %collective-permute-done.3.refs_5_ = bf16[320,256]{1,0:T(8,128)(2,1)S(1)} collective-permute-done((bf16[320,256]{1,0:T(8,128)(2,1)S(1)}, bf16[320,256]{1,0:T(8,128)(2,1)S(1)}, u32[]{:S(2)}, u32[]{:S(2)}) %collective-permute-start.3) | collective-permute-done | bytes 163872 | tf_op jit(solution)/shard_map/ppermute | solution.py:414
  16.2 0.9 %collective-permute-start.6 = (bf16[160,256]{1,0:T(8,128)(2,1)S(1)}, bf16[160,256]{1,0:T(8,128)(2,1)S(1)}, u32[]{:S(2)}, u32[]{:S(2)}) collective-permute-start(bf16[160,256]{1,0:T(8,128)(2,1)S(1)} %slice.38), channel_id=1, source_target_pairs={{0,2},{1,3},{2,4},{3,5},{4,6},{5,7},{6,0},{7,1},{8,10},{9,11},{10,... | collective-permute-start | bytes 245768 | tf_op jit(solution)/shard_map/ppermute | solution.py:414
  17.1 3.3 %collective-permute-start.7 = (bf16[160,256]{1,0:T(8,128)(2,1)S(1)}, bf16[160,256]{1,0:T(8,128)(2,1)S(1)}, u32[]{:S(2)}, u32[]{:S(2)}) collective-permute-start(bf16[160,256]{1,0:T(8,128)(2,1)S(1)} %slice.49), channel_id=1, source_target_pairs={{0,6},{1,7},{2,0},{3,1},{4,2},{5,3},{6,4},{7,5},{8,14},{9,15},{10,... | collective-permute-start | bytes 245768 | tf_op jit(solution)/shard_map/ppermute | solution.py:414
  20.5 0.1 collective-permute-start.5
  20.6 2.3 %collective-permute-done.6.refs_8_ = bf16[160,256]{1,0:T(8,128)(2,1)S(1)} collective-permute-done((bf16[160,256]{1,0:T(8,128)(2,1)S(1)}, bf16[160,256]{1,0:T(8,128)(2,1)S(1)}, u32[]{:S(2)}, u32[]{:S(2)}) %collective-permute-start.6) | collective-permute-done | bytes 81952 | tf_op jit(solution)/shard_map/ppermute | solution.py:414
  22.8 2.8 %collective-permute-done.7.refs_9_ = bf16[160,256]{1,0:T(8,128)(2,1)S(1)} collective-permute-done((bf16[160,256]{1,0:T(8,128)(2,1)S(1)}, bf16[160,256]{1,0:T(8,128)(2,1)S(1)}, u32[]{:S(2)}, u32[]{:S(2)}) %collective-permute-start.7) | collective-permute-done | bytes 81952 | tf_op jit(solution)/shard_map/ppermute | solution.py:414
  25.7 0.5 shard_map.76
  26.2 0.9 %collective-permute-done.8.refs_10_ = bf16[320,256]{1,0:T(8,128)(2,1)S(1)} collective-permute-done((bf16[320,256]{1,0:T(8,128)(2,1)S(1)}, bf16[320,256]{1,0:T(8,128)(2,1)S(1)}, u32[]{:S(2)}, u32[]{:S(2)}) %collective-permute-start.8) | collective-permute-done | bytes 163872 | tf_op jit(solution)/shard_map/ppermute | solution.py:419
  27.1 2.4 %shard_map.78 = (bf16[32,512]{1,0:T(8,128)(2,1)S(1)}, bf16[64,256]{1,0:T(8,128)(2,1)S(1)}, bf16[1024,128]{1,0:T(8,128)(2,1)}) custom-call(bf16[27,32,128]{2,1,0:T(8,128)(2,1)S(1)} %copy-done, f32[32,512]{1,0:T(8,128)S(1)} %get-tuple-element.34.refs_1_, bf16[864,512]{1,0:T(8,128)(2,1)S(1)} %get-tuple-element.35.refs_2_, ...), custom_call_target="tpu_custom_call" | custom-call | tf_op jit(solution)/shard_map/pallas_call | solution.py:43
  29.6 4.4 %collective-permute-start.9 = (bf16[192,256]{1,0:T(8,128)(2,1)S(1)}, bf16[192,256]{1,0:T(8,128)(2,1)S(1)}, u32[]{:S(2)}, u32[]{:S(2)}) collective-permute-start(bf16[192,256]{1,0:T(8,128)(2,1)S(1)} %get-tuple-element.62), channel_id=1, source_target_pairs={{0,2},{1,3},{2,4},{3,5},{4,6},{5,7},{6,0},{7,1},{8,10},{9,11},{10,... | collective-permute-start | bytes 294920 | tf_op jit(solution)/shard_map/ppermute | solution.py:414
  34.0 3.7 %collective-permute-start.12 = (bf16[192,256]{1,0:T(8,128)(2,1)S(1)}, bf16[192,256]{1,0:T(8,128)(2,1)S(1)}, u32[]{:S(2)}, u32[]{:S(2)}) collective-permute-start(bf16[192,256]{1,0:T(8,128)(2,1)S(1)} %get-tuple-element.60), channel_id=1, source_target_pairs={{0,4},{1,5},{2,6},{3,7},{4,0},{5,1},{6,2},{7,3},{8,12},{9,13},{10,... | collective-permute-start | bytes 294920 | tf_op jit(solution)/shard_map/ppermute | solution.py:414
  37.8 9.0 %all-to-all-start = ((bf16[32,32,128]{2,1,0:T(8,128)(2,1)}), bf16[32,32,128]{2,1,0:T(8,128)(2,1)S(1)}, u32[]{:S(2)}, u32[]{:S(2)}) async-start(bf16[32,32,128]{2,1,0:T(8,128)(2,1)} %bitcast.3), calls=%async_computation | async-start | bytes 524288 | tf_op jit(solution)/shard_map/all_to_all | solution.py:458
  46.9 0.1 collective-permute-start.13
  47.0 0.7 collective-permute-start.14
  47.7 0.7 %collective-permute-done.13.refs_3_ = bf16[384,256]{1,0:T(8,128)(2,1)S(1)} collective-permute-done((bf16[384,256]{1,0:T(8,128)(2,1)S(1)}, bf16[384,256]{1,0:T(8,128)(2,1)S(1)}, u32[]{:S(2)}, u32[]{:S(2)}) %collective-permute-start.13) | collective-permute-done | bytes 196640 | tf_op jit(solution)/shard_map/ppermute | solution.py:419
  48.5 0.5 shard_map.79
  49.0 2.1 %collective-permute-done.14.low_ref = bf16[32,256]{1,0:T(8,128)(2,1)S(1)} collective-permute-done((bf16[32,256]{1,0:T(8,128)(2,1)S(1)}, bf16[32,256]{1,0:T(8,128)(2,1)S(1)}, u32[]{:S(2)}, u32[]{:S(2)}) %collective-permute-start.14) | collective-permute-done | bytes 16416 | tf_op jit(solution)/shard_map/ppermute | solution.py:411
  51.0 1.2 %all-to-all-done.src = bf16[32,32,128]{2,1,0:T(8,128)(2,1)S(1)} async-done(((bf16[32,32,128]{2,1,0:T(8,128)(2,1)}), bf16[32,32,128]{2,1,0:T(8,128)(2,1)S(1)}, u32[]{:S(2)}, u32[]{:S(2)}) %all-to-all-start) | async-done | bytes 262176 | tf_op jit(solution)/shard_map/all_to_all | solution.py:458
  52.2 0.8 %shard_map.81 = bf16[32,32,128]{2,1,0:T(8,128)(2,1)} custom-call(bf16[32,32,128]{2,1,0:T(8,128)(2,1)S(1)} %all-to-all-done.src), custom_call_target="tpu_custom_call" | custom-call | tf_op jit(solution)/shard_map/pallas_call | solution.py:43
  53.0 8.1 %all-to-all-start.1 = ((bf16[32,32,128]{2,1,0:T(8,128)(2,1)}), bf16[32,32,128]{2,1,0:T(8,128)(2,1)S(1)}, u32[]{:S(2)}, u32[]{:S(2)}) async-start(bf16[32,32,128]{2,1,0:T(8,128)(2,1)} %shard_map.81), calls=%async_computation.1 | async-start | bytes 524288 | tf_op jit(solution)/shard_map/all_to_all | solution.py:485
  61.1 0.6 collective-permute-start.15
  61.7 7.8 %collective-permute-done.15.packed_ref = bf16[96,256]{1,0:T(8,128)(2,1)S(1)} collective-permute-done((bf16[96,256]{1,0:T(8,128)(2,1)S(1)}, bf16[96,256]{1,0:T(8,128)(2,1)S(1)}, u32[]{:S(2)}, u32[]{:S(2)}) %collective-permute-start.15) | collective-permute-done | bytes 49184 | tf_op jit(solution)/shard_map/ppermute | solution.py:411
  69.5 1.3 %shard_map.80 = (bf16[32,2,256]{2,1,0:T(2,128)(2,1)}, f32[16,4,1024]{2,1,0:T(4,128)}) custom-call(bf16[32,256]{1,0:T(8,128)(2,1)S(1)} %collective-permute-done.14.low_ref, bf16[32,512]{1,0:T(8,128)(2,1)S(1)} %get-tuple-element.43.active_ref.mid_ref, bf16[96,256]{1,0:T(8,128)(2,1)S(1)} %collective-permute-done.15.packed_ref, ...), custom_call_target="tpu_custom_call" | custom-call | tf_op jit(solution)/shard_map/pallas_call | solution.py:43
  70.8 0.8 %shard_map.82 = (f32[27,32,128]{2,1,0:T(8,128)}, f32[27,8,32]{2,1,0:T(8,128)}) custom-call(bf16[1024,128]{1,0:T(8,128)(2,1)S(1)} %bitcast.10), custom_call_target="tpu_custom_call" | custom-call | tf_op jit(solution)/shard_map/pallas_call | solution.py:43
  (37 shorter events, 0.4 us)
Async XLA Ops:
  0.6 1.0 %copy-start.2 = (bf16[32,2,256]{2,1,0:T(2,128)(2,1)S(1)}, bf16[32,2,256]{2,1,0:T(2,128)(2,1)}, u32[]{:S(2)}) copy-start(bf16[32,2,256]{2,1,0:T(2,128)(2,1)} %param.7) | copy-start | bytes 98308
  1.6 11.7 %copy-start = (bf16[27,32,128]{2,1,0:T(8,128)(2,1)S(1)}, bf16[27,32,128]{2,1,0:T(8,128)(2,1)}, u32[]{:S(2)}) copy-start(bf16[27,32,128]{2,1,0:T(8,128)(2,1)} %refs_0_.1) | copy-start | bytes 663556
  1.7 4.2 %collective-permute-start = (bf16[96,256]{1,0:T(8,128)(2,1)S(1)}, bf16[96,256]{1,0:T(8,128)(2,1)S(1)}, u32[]{:S(2)}, u32[]{:S(2)}) collective-permute-start(bf16[96,256]{1,0:T(8,128)(2,1)S(1)} %get-tuple-element.32), channel_id=1, source_target_pairs={{0,8},{8,16},{16,24},{24,32},{32,40},{40,48},{48,56},{56,64},{64,7... | collective-permute-start | bytes 147464 | tf_op jit(solution)/shard_map/ppermute | solution.py:411
  5.8 10.4 %collective-permute-start.3 = (bf16[320,256]{1,0:T(8,128)(2,1)S(1)}, bf16[320,256]{1,0:T(8,128)(2,1)S(1)}, u32[]{:S(2)}, u32[]{:S(2)}) collective-permute-start(bf16[320,256]{1,0:T(8,128)(2,1)S(1)} %pad_maximum_fusion.1.refs_3_), channel_id=1, source_target_pairs={{0,2},{1,3},{2,4},{3,5},{4,6},{5,7},{6,0},{7,1},{8,10},{9,11},{10,... | collective-permute-start | bytes 491528 | tf_op jit(solution)/shard_map/ppermute | solution.py:414
  9.2 7.9 %collective-permute-start.4 = (bf16[320,256]{1,0:T(8,128)(2,1)S(1)}, bf16[320,256]{1,0:T(8,128)(2,1)S(1)}, u32[]{:S(2)}, u32[]{:S(2)}) collective-permute-start(bf16[320,256]{1,0:T(8,128)(2,1)S(1)} %pad_maximum_fusion.1.refs_3_), channel_id=1, source_target_pairs={{0,6},{1,7},{2,0},{3,1},{4,2},{5,3},{6,4},{7,5},{8,14},{9,15},{10,... | collective-permute-start | bytes 491528 | tf_op jit(solution)/shard_map/ppermute | solution.py:414
  11.4 14.3 %collective-permute-start.1 = (bf16[32,256]{1,0:T(8,128)(2,1)S(1)}, bf16[32,256]{1,0:T(8,128)(2,1)S(1)}, u32[]{:S(2)}, u32[]{:S(2)}) collective-permute-start(bf16[32,256]{1,0:T(8,128)(2,1)S(1)} %slice.36), channel_id=1, source_target_pairs={{0,248},{8,0},{16,8},{24,16},{32,24},{40,32},{48,40},{56,48},{64,5... | collective-permute-start | bytes 49160 | tf_op jit(solution)/shard_map/ppermute | solution.py:411
  13.8 12.4 %collective-permute-start.2 = (bf16[320,256]{1,0:T(8,128)(2,1)S(1)}, bf16[320,256]{1,0:T(8,128)(2,1)S(1)}, u32[]{:S(2)}, u32[]{:S(2)}) collective-permute-start(bf16[320,256]{1,0:T(8,128)(2,1)S(1)} %pad_maximum_fusion.1.refs_3_), channel_id=1, source_target_pairs={{0,1},{1,0},{2,3},{3,2},{4,5},{5,4},{6,7},{7,6},{8,9},{9,8},{10,11... | collective-permute-start | bytes 491528 | tf_op jit(solution)/shard_map/ppermute | solution.py:419
  16.2 6.6 %collective-permute-start.6 = (bf16[160,256]{1,0:T(8,128)(2,1)S(1)}, bf16[160,256]{1,0:T(8,128)(2,1)S(1)}, u32[]{:S(2)}, u32[]{:S(2)}) collective-permute-start(bf16[160,256]{1,0:T(8,128)(2,1)S(1)} %slice.38), channel_id=1, source_target_pairs={{0,2},{1,3},{2,4},{3,5},{4,6},{5,7},{6,0},{7,1},{8,10},{9,11},{10,... | collective-permute-start | bytes 245768 | tf_op jit(solution)/shard_map/ppermute | solution.py:414
  17.1 8.5 %collective-permute-start.7 = (bf16[160,256]{1,0:T(8,128)(2,1)S(1)}, bf16[160,256]{1,0:T(8,128)(2,1)S(1)}, u32[]{:S(2)}, u32[]{:S(2)}) collective-permute-start(bf16[160,256]{1,0:T(8,128)(2,1)S(1)} %slice.49), channel_id=1, source_target_pairs={{0,6},{1,7},{2,0},{3,1},{4,2},{5,3},{6,4},{7,5},{8,14},{9,15},{10,... | collective-permute-start | bytes 245768 | tf_op jit(solution)/shard_map/ppermute | solution.py:414
  20.5 5.3 %copy-start.1 = (bf16[27,32,8]{1,2,0:T(8,128)(2,1)S(1)}, bf16[27,32,8]{1,2,0:T(8,128)(2,1)}, u32[]{:S(2)}) copy-start(bf16[27,32,8]{1,2,0:T(8,128)(2,1)} %param.6) | copy-start | bytes 41476
  20.5 6.6 %collective-permute-start.5 = (bf16[640,256]{1,0:T(8,128)(2,1)S(1)}, bf16[640,256]{1,0:T(8,128)(2,1)S(1)}, u32[]{:S(2)}, u32[]{:S(2)}) collective-permute-start(bf16[640,256]{1,0:T(8,128)(2,1)S(1)} %pad_maximum_fusion), channel_id=1, source_target_pairs={{0,1},{1,0},{2,3},{3,2},{4,5},{5,4},{6,7},{7,6},{8,9},{9,8},{10,11... | collective-permute-start | bytes 983048 | tf_op jit(solution)/shard_map/ppermute | solution.py:419
  25.6 1.5 %collective-permute-start.8 = (bf16[320,256]{1,0:T(8,128)(2,1)S(1)}, bf16[320,256]{1,0:T(8,128)(2,1)S(1)}, u32[]{:S(2)}, u32[]{:S(2)}) collective-permute-start(bf16[320,256]{1,0:T(8,128)(2,1)S(1)} %pad_maximum_fusion.2), channel_id=1, source_target_pairs={{0,1},{1,0},{2,3},{3,2},{4,5},{5,4},{6,7},{7,6},{8,9},{9,8},{10,11... | collective-permute-start | bytes 491528 | tf_op jit(solution)/shard_map/ppermute | solution.py:419
  29.6 17.3 %collective-permute-start.9 = (bf16[192,256]{1,0:T(8,128)(2,1)S(1)}, bf16[192,256]{1,0:T(8,128)(2,1)S(1)}, u32[]{:S(2)}, u32[]{:S(2)}) collective-permute-start(bf16[192,256]{1,0:T(8,128)(2,1)S(1)} %get-tuple-element.62), channel_id=1, source_target_pairs={{0,2},{1,3},{2,4},{3,5},{4,6},{5,7},{6,0},{7,1},{8,10},{9,11},{10,... | collective-permute-start | bytes 294920 | tf_op jit(solution)/shard_map/ppermute | solution.py:414
  33.9 12.9 %collective-permute-start.10 = (bf16[128,256]{1,0:T(8,128)(2,1)S(1)}, bf16[128,256]{1,0:T(8,128)(2,1)S(1)}, u32[]{:S(2)}, u32[]{:S(2)}) collective-permute-start(bf16[128,256]{1,0:T(8,128)(2,1)S(1)} %pad_maximum_fusion.6), channel_id=1, source_target_pairs={{0,1},{1,0},{2,3},{3,2},{4,5},{5,4},{6,7},{7,6},{8,9},{9,8},{10,11... | collective-permute-start | bytes 196616 | tf_op jit(solution)/shard_map/ppermute | solution.py:419
  33.9 12.9 %collective-permute-start.11 = (bf16[192,256]{1,0:T(8,128)(2,1)S(1)}, bf16[192,256]{1,0:T(8,128)(2,1)S(1)}, u32[]{:S(2)}, u32[]{:S(2)}) collective-permute-start(bf16[192,256]{1,0:T(8,128)(2,1)S(1)} %get-tuple-element.61), channel_id=1, source_target_pairs={{0,6},{1,7},{2,0},{3,1},{4,2},{5,3},{6,4},{7,5},{8,14},{9,15},{10,... | collective-permute-start | bytes 294920 | tf_op jit(solution)/shard_map/ppermute | solution.py:414
  34.0 12.9 %collective-permute-start.12 = (bf16[192,256]{1,0:T(8,128)(2,1)S(1)}, bf16[192,256]{1,0:T(8,128)(2,1)S(1)}, u32[]{:S(2)}, u32[]{:S(2)}) collective-permute-start(bf16[192,256]{1,0:T(8,128)(2,1)S(1)} %get-tuple-element.60), channel_id=1, source_target_pairs={{0,4},{1,5},{2,6},{3,7},{4,0},{5,1},{6,2},{7,3},{8,12},{9,13},{10,... | collective-permute-start | bytes 294920 | tf_op jit(solution)/shard_map/ppermute | solution.py:414
  37.8 14.4 %all-to-all-start = ((bf16[32,32,128]{2,1,0:T(8,128)(2,1)}), bf16[32,32,128]{2,1,0:T(8,128)(2,1)S(1)}, u32[]{:S(2)}, u32[]{:S(2)}) async-start(bf16[32,32,128]{2,1,0:T(8,128)(2,1)} %bitcast.3), calls=%async_computation | async-start | bytes 524288 | tf_op jit(solution)/shard_map/all_to_all | solution.py:458
  46.9 1.5 %collective-permute-start.13 = (bf16[384,256]{1,0:T(8,128)(2,1)S(1)}, bf16[384,256]{1,0:T(8,128)(2,1)S(1)}, u32[]{:S(2)}, u32[]{:S(2)}) collective-permute-start(bf16[384,256]{1,0:T(8,128)(2,1)S(1)} %slice_dynamic-update-slice_fusion), channel_id=1, source_target_pairs={{0,1},{1,0},{2,3},{3,2},{4,5},{5,4},{6,7},{7,6},{8,9},{9,8},{10,11... | collective-permute-start | bytes 589832 | tf_op jit(solution)/shard_map/ppermute | solution.py:419
  47.0 4.0 %collective-permute-start.14 = (bf16[32,256]{1,0:T(8,128)(2,1)S(1)}, bf16[32,256]{1,0:T(8,128)(2,1)S(1)}, u32[]{:S(2)}, u32[]{:S(2)}) collective-permute-start(bf16[32,256]{1,0:T(8,128)(2,1)S(1)} %slice.47), channel_id=1, source_target_pairs={{0,8},{8,16},{16,24},{24,32},{32,40},{40,48},{48,56},{56,64},{64,7... | collective-permute-start | bytes 49160 | tf_op jit(solution)/shard_map/ppermute | solution.py:411
  53.0 17.9 %all-to-all-start.1 = ((bf16[32,32,128]{2,1,0:T(8,128)(2,1)}), bf16[32,32,128]{2,1,0:T(8,128)(2,1)S(1)}, u32[]{:S(2)}, u32[]{:S(2)}) async-start(bf16[32,32,128]{2,1,0:T(8,128)(2,1)} %shard_map.81), calls=%async_computation.1 | async-start | bytes 524288 | tf_op jit(solution)/shard_map/all_to_all | solution.py:485
  61.1 8.4 %collective-permute-start.15 = (bf16[96,256]{1,0:T(8,128)(2,1)S(1)}, bf16[96,256]{1,0:T(8,128)(2,1)S(1)}, u32[]{:S(2)}, u32[]{:S(2)}) collective-permute-start(bf16[96,256]{1,0:T(8,128)(2,1)S(1)} %get-tuple-element.53), channel_id=1, source_target_pairs={{0,248},{8,0},{16,8},{24,16},{32,24},{40,32},{48,40},{56,48},{64,5... | collective-permute-start | bytes 147464 | tf_op jit(solution)/shard_map/ppermute | solution.py:411

commit v5 on v4

--- a/solution.py
+++ b/solution.py
@@ -439,7 +439,7 @@
     far_low = along_chips(from_low[: cut * in_chan], 1)
     far_high = along_chips(from_high[cut * in_chan :], -1)
     near_other = other_core(joined(from_low, from_high))
-    far_other = other_core(joined(far_low, far_high))
+    low_other, high_other = other_core(far_low), other_core(far_high)
     pieces = [
         (framed, [(0, slots, 0, False)]),
         (other_core(framed), [(0, slots, 0, True)]),
@@ -448,7 +448,8 @@
         (near_other, [(0, slots, -1, True), (length, slots, 1, True)]),
         (far_low, [(0, slots[:cut], 2, False)]),
         (far_high, [(0, slots[cut:], 2, False)]),
-        (far_other, [(0, slots, 2, True)]),
+        (low_other, [(0, slots[:cut], 2, True)]),
+        (high_other, [(0, slots[cut:], 2, True)]),
     ]
 
     rows = -(-(taps * outputs + 64) // (slabs * 32)) * slabs * 32

time: 71.9 us -> 71.8 us (level)
    ppermute x5 -> x6, waiting for transfers between devices: 1.61 us -> 1.65 us  [other_core(): return lax.ppermute(block, 'chan', [(i, i ^ 1) for i in range(blocks)])]
  transfers between devices with their start and end apart: 18 -> 19, of which waited for: 9 -> 9; matrix products, arithmetic and copies ran while one was open for 0% -> 0% of each run, Pallas kernels for 4% -> 4%
where the time goes in v5:
time: 71.8 us; the launch traced here: 71.5 us
  starting transfers between devices  40.3 us (56%)
  waiting for transfers between devices  22.3 us (31%)
  Pallas kernels  6.83 us (10%)
  local copies, waits for them, and re-layouts  1.04 us (1%)
  between operations  0.89 us (1%)
    ppermute x7, starting transfers between devices, along_chips(): lax.ppermute(block, 'chan', [(i, (i + 2 * step) % blocks) for i in range(...  17.9 us
    ppermute x4, waiting for transfers between devices, along_space(): lax.ppermute(block, 'space', [(i, (i + step) % slabs) for i in range(slab...  12.3 us
    all_to_all x1, starting transfers between devices, body(): lax.all_to_all(terms.reshape(slabs, rows // slabs, 128), 'space', split_a...  9.06 us
    all_to_all x1, starting transfers between devices, body(): lax.all_to_all(sum_part(received, scale), 'space', split_axis=0, concat_a...  8.31 us
    ppermute x7, waiting for transfers between devices, along_chips(): lax.ppermute(block, 'chan', [(i, (i + 2 * step) % blocks) for i in range(...  7.35 us
    pallas_call x8, Pallas kernels, call(): pl.pallas_call(kernel, out_shape=outs, in_specs=[whole] * len(args), out_...  6.83 us
    ppermute x4, starting transfers between devices, along_space(): lax.ppermute(block, 'space', [(i, (i + step) % slabs) for i in range(slab...  4.56 us
    ppermute x6, waiting for transfers between devices, other_core(): return lax.ppermute(block, 'chan', [(i, i ^ 1) for i in range(blocks)])  1.65 us
  transfers between devices with their start and end apart: 19, of which 9 were waited for; matrix products, arithmetic and copies ran while one was open for 0% of the time, Pallas kernels for 4%

profile of v5, /device:TPU:62, one launch (start us, length us, event | category | flops | bytes accessed | tf_op | source)
XLA Modules:
  0.0 71.5 jit_solution(12227054626140271002)
XLA Ops:
  0.6 1.0 %copy.12 = bf16[16,4,1024]{2,0,1:T(8,128)(2,1)S(1)} copy(bf16[16,4,1024]{2,1,0:T(4,128)(2,1)} %param.4) | data formatting | bytes 262144 | tf_op args[0]
  1.7 1.5 %collective-permute-start = (bf16[96,256]{1,0:T(8,128)(2,1)S(1)}, bf16[96,256]{1,0:T(8,128)(2,1)S(1)}, u32[]{:S(2)}, u32[]{:S(2)}) collective-permute-start(bf16[96,256]{1,0:T(8,128)(2,1)S(1)} %get-tuple-element.32), channel_id=1, source_target_pairs={{0,8},{8,16},{16,24},{24,32},{32,40},{40,48},{48,56},{56,64},{64,7... | collective-permute-start | bytes 147464 | tf_op jit(solution)/shard_map/ppermute | solution.py:411
  3.2 2.7 %collective-permute-done.low_ref = bf16[96,256]{1,0:T(8,128)(2,1)S(1)} collective-permute-done((bf16[96,256]{1,0:T(8,128)(2,1)S(1)}, bf16[96,256]{1,0:T(8,128)(2,1)S(1)}, u32[]{:S(2)}, u32[]{:S(2)}) %collective-permute-start) | collective-permute-done | bytes 49184 | tf_op jit(solution)/shard_map/ppermute | solution.py:411
  5.8 3.3 %collective-permute-start.3 = (bf16[320,256]{1,0:T(8,128)(2,1)S(1)}, bf16[320,256]{1,0:T(8,128)(2,1)S(1)}, u32[]{:S(2)}, u32[]{:S(2)}) collective-permute-start(bf16[320,256]{1,0:T(8,128)(2,1)S(1)} %pad_maximum_fusion.1.refs_3_), channel_id=1, source_target_pairs={{0,2},{1,3},{2,4},{3,5},{4,6},{5,7},{6,0},{7,1},{8,10},{9,11},{10,... | collective-permute-start | bytes 491528 | tf_op jit(solution)/shard_map/ppermute | solution.py:414
  9.2 2.2 %collective-permute-start.4 = (bf16[320,256]{1,0:T(8,128)(2,1)S(1)}, bf16[320,256]{1,0:T(8,128)(2,1)S(1)}, u32[]{:S(2)}, u32[]{:S(2)}) collective-permute-start(bf16[320,256]{1,0:T(8,128)(2,1)S(1)} %pad_maximum_fusion.1.refs_3_), channel_id=1, source_target_pairs={{0,6},{1,7},{2,0},{3,1},{4,2},{5,3},{6,4},{7,5},{8,14},{9,15},{10,... | collective-permute-start | bytes 491528 | tf_op jit(solution)/shard_map/ppermute | solution.py:414
  11.4 1.9 %collective-permute-start.1 = (bf16[32,256]{1,0:T(8,128)(2,1)S(1)}, bf16[32,256]{1,0:T(8,128)(2,1)S(1)}, u32[]{:S(2)}, u32[]{:S(2)}) collective-permute-start(bf16[32,256]{1,0:T(8,128)(2,1)S(1)} %slice.36), channel_id=1, source_target_pairs={{0,248},{8,0},{16,8},{24,16},{32,24},{40,32},{48,40},{56,48},{64,5... | collective-permute-start | bytes 49160 | tf_op jit(solution)/shard_map/ppermute | solution.py:411
  13.3 0.5 shard_map.77
  13.8 0.1 collective-permute-start.2
  13.9 2.3 %collective-permute-done.3.refs_5_ = bf16[320,256]{1,0:T(8,128)(2,1)S(1)} collective-permute-done((bf16[320,256]{1,0:T(8,128)(2,1)S(1)}, bf16[320,256]{1,0:T(8,128)(2,1)S(1)}, u32[]{:S(2)}, u32[]{:S(2)}) %collective-permute-start.3) | collective-permute-done | bytes 163872 | tf_op jit(solution)/shard_map/ppermute | solution.py:414
  16.2 0.9 %collective-permute-start.6 = (bf16[160,256]{1,0:T(8,128)(2,1)S(1)}, bf16[160,256]{1,0:T(8,128)(2,1)S(1)}, u32[]{:S(2)}, u32[]{:S(2)}) collective-permute-start(bf16[160,256]{1,0:T(8,128)(2,1)S(1)} %slice.38), channel_id=1, source_target_pairs={{0,2},{1,3},{2,4},{3,5},{4,6},{5,7},{6,0},{7,1},{8,10},{9,11},{10,... | collective-permute-start | bytes 245768 | tf_op jit(solution)/shard_map/ppermute | solution.py:414
  17.1 3.3 %collective-permute-start.7 = (bf16[160,256]{1,0:T(8,128)(2,1)S(1)}, bf16[160,256]{1,0:T(8,128)(2,1)S(1)}, u32[]{:S(2)}, u32[]{:S(2)}) collective-permute-start(bf16[160,256]{1,0:T(8,128)(2,1)S(1)} %slice.49), channel_id=1, source_target_pairs={{0,6},{1,7},{2,0},{3,1},{4,2},{5,3},{6,4},{7,5},{8,14},{9,15},{10,... | collective-permute-start | bytes 245768 | tf_op jit(solution)/shard_map/ppermute | solution.py:414
  20.5 0.1 collective-permute-start.5
  20.6 2.3 %collective-permute-done.6.refs_8_ = bf16[160,256]{1,0:T(8,128)(2,1)S(1)} collective-permute-done((bf16[160,256]{1,0:T(8,128)(2,1)S(1)}, bf16[160,256]{1,0:T(8,128)(2,1)S(1)}, u32[]{:S(2)}, u32[]{:S(2)}) %collective-permute-start.6) | collective-permute-done | bytes 81952 | tf_op jit(solution)/shard_map/ppermute | solution.py:414
  22.8 2.8 %collective-permute-done.7.refs_9_ = bf16[160,256]{1,0:T(8,128)(2,1)S(1)} collective-permute-done((bf16[160,256]{1,0:T(8,128)(2,1)S(1)}, bf16[160,256]{1,0:T(8,128)(2,1)S(1)}, u32[]{:S(2)}, u32[]{:S(2)}) %collective-permute-start.7) | collective-permute-done | bytes 81952 | tf_op jit(solution)/shard_map/ppermute | solution.py:414
  25.6 0.5 shard_map.76
  26.2 0.7 %collective-permute-done.9.refs_11_ = bf16[160,256]{1,0:T(8,128)(2,1)S(1)} collective-permute-done((bf16[160,256]{1,0:T(8,128)(2,1)S(1)}, bf16[160,256]{1,0:T(8,128)(2,1)S(1)}, u32[]{:S(2)}, u32[]{:S(2)}) %collective-permute-start.9) | collective-permute-done | bytes 81952 | tf_op jit(solution)/shard_map/ppermute | solution.py:419
  26.9 2.4 %shard_map.78 = (bf16[32,512]{1,0:T(8,128)(2,1)S(1)}, bf16[64,256]{1,0:T(8,128)(2,1)S(1)}, bf16[1024,128]{1,0:T(8,128)(2,1)}) custom-call(bf16[27,32,128]{2,1,0:T(8,128)(2,1)S(1)} %copy-done, f32[32,512]{1,0:T(8,128)S(1)} %get-tuple-element.34.refs_1_, bf16[864,512]{1,0:T(8,128)(2,1)S(1)} %get-tuple-element.35.refs_2_, ...), custom_call_target="tpu_custom_call" | custom-call | tf_op jit(solution)/shard_map/pallas_call | solution.py:43
  29.4 4.3 %collective-permute-start.10 = (bf16[192,256]{1,0:T(8,128)(2,1)S(1)}, bf16[192,256]{1,0:T(8,128)(2,1)S(1)}, u32[]{:S(2)}, u32[]{:S(2)}) collective-permute-start(bf16[192,256]{1,0:T(8,128)(2,1)S(1)} %get-tuple-element.62), channel_id=1, source_target_pairs={{0,2},{1,3},{2,4},{3,5},{4,6},{5,7},{6,0},{7,1},{8,10},{9,11},{10,... | collective-permute-start | bytes 294920 | tf_op jit(solution)/shard_map/ppermute | solution.py:414
  33.8 3.7 %collective-permute-start.13 = (bf16[192,256]{1,0:T(8,128)(2,1)S(1)}, bf16[192,256]{1,0:T(8,128)(2,1)S(1)}, u32[]{:S(2)}, u32[]{:S(2)}) collective-permute-start(bf16[192,256]{1,0:T(8,128)(2,1)S(1)} %get-tuple-element.60), channel_id=1, source_target_pairs={{0,4},{1,5},{2,6},{3,7},{4,0},{5,1},{6,2},{7,3},{8,12},{9,13},{10,... | collective-permute-start | bytes 294920 | tf_op jit(solution)/shard_map/ppermute | solution.py:414
  37.5 9.1 %all-to-all-start = ((bf16[32,32,128]{2,1,0:T(8,128)(2,1)}), bf16[32,32,128]{2,1,0:T(8,128)(2,1)S(1)}, u32[]{:S(2)}, u32[]{:S(2)}) async-start(bf16[32,32,128]{2,1,0:T(8,128)(2,1)} %bitcast.3), calls=%async_computation | async-start | bytes 524288 | tf_op jit(solution)/shard_map/all_to_all | solution.py:459
  46.7 0.3 collective-permute-start.14
  47.0 0.5 collective-permute-start.15
  47.6 0.9 %collective-permute-done.14.refs_3_ = bf16[384,256]{1,0:T(8,128)(2,1)S(1)} collective-permute-done((bf16[384,256]{1,0:T(8,128)(2,1)S(1)}, bf16[384,256]{1,0:T(8,128)(2,1)S(1)}, u32[]{:S(2)}, u32[]{:S(2)}) %collective-permute-start.14) | collective-permute-done | bytes 196640 | tf_op jit(solution)/shard_map/ppermute | solution.py:419
  48.4 0.5 shard_map.79
  49.0 1.9 %collective-permute-done.15.low_ref = bf16[32,256]{1,0:T(8,128)(2,1)S(1)} collective-permute-done((bf16[32,256]{1,0:T(8,128)(2,1)S(1)}, bf16[32,256]{1,0:T(8,128)(2,1)S(1)}, u32[]{:S(2)}, u32[]{:S(2)}) %collective-permute-start.15) | collective-permute-done | bytes 16416 | tf_op jit(solution)/shard_map/ppermute | solution.py:411
  50.8 1.0 %all-to-all-done.src = bf16[32,32,128]{2,1,0:T(8,128)(2,1)S(1)} async-done(((bf16[32,32,128]{2,1,0:T(8,128)(2,1)}), bf16[32,32,128]{2,1,0:T(8,128)(2,1)S(1)}, u32[]{:S(2)}, u32[]{:S(2)}) %all-to-all-start) | async-done | bytes 262176 | tf_op jit(solution)/shard_map/all_to_all | solution.py:459
  51.8 0.8 %shard_map.81 = bf16[32,32,128]{2,1,0:T(8,128)(2,1)} custom-call(bf16[32,32,128]{2,1,0:T(8,128)(2,1)S(1)} %all-to-all-done.src), custom_call_target="tpu_custom_call" | custom-call | tf_op jit(solution)/shard_map/pallas_call | solution.py:43
  52.6 8.3 %all-to-all-start.1 = ((bf16[32,32,128]{2,1,0:T(8,128)(2,1)}), bf16[32,32,128]{2,1,0:T(8,128)(2,1)S(1)}, u32[]{:S(2)}, u32[]{:S(2)}) async-start(bf16[32,32,128]{2,1,0:T(8,128)(2,1)} %shard_map.81), calls=%async_computation.1 | async-start | bytes 524288 | tf_op jit(solution)/shard_map/all_to_all | solution.py:486
  60.9 0.6 collective-permute-start.16
  61.6 7.8 %collective-permute-done.16.packed_ref = bf16[96,256]{1,0:T(8,128)(2,1)S(1)} collective-permute-done((bf16[96,256]{1,0:T(8,128)(2,1)S(1)}, bf16[96,256]{1,0:T(8,128)(2,1)S(1)}, u32[]{:S(2)}, u32[]{:S(2)}) %collective-permute-start.16) | collective-permute-done | bytes 49184 | tf_op jit(solution)/shard_map/ppermute | solution.py:411
  69.3 1.3 %shard_map.80 = (bf16[32,2,256]{2,1,0:T(2,128)(2,1)}, f32[16,4,1024]{2,1,0:T(4,128)}) custom-call(bf16[32,256]{1,0:T(8,128)(2,1)S(1)} %collective-permute-done.15.low_ref, bf16[32,512]{1,0:T(8,128)(2,1)S(1)} %get-tuple-element.43.active_ref.mid_ref, bf16[96,256]{1,0:T(8,128)(2,1)S(1)} %collective-permute-done.16.packed_ref, ...), custom_call_target="tpu_custom_call" | custom-call | tf_op jit(solution)/shard_map/pallas_call | solution.py:43
  70.6 0.8 %shard_map.82 = (f32[27,32,128]{2,1,0:T(8,128)}, f32[27,8,32]{2,1,0:T(8,128)}) custom-call(bf16[1024,128]{1,0:T(8,128)(2,1)S(1)} %bitcast.10), custom_call_target="tpu_custom_call" | custom-call | tf_op jit(solution)/shard_map/pallas_call | solution.py:43
  (38 shorter events, 0.3 us)
Async XLA Ops:
  0.6 1.0 %copy-start.2 = (bf16[32,2,256]{2,1,0:T(2,128)(2,1)S(1)}, bf16[32,2,256]{2,1,0:T(2,128)(2,1)}, u32[]{:S(2)}) copy-start(bf16[32,2,256]{2,1,0:T(2,128)(2,1)} %param.7) | copy-start | bytes 98308
  1.6 11.7 %copy-start = (bf16[27,32,128]{2,1,0:T(8,128)(2,1)S(1)}, bf16[27,32,128]{2,1,0:T(8,128)(2,1)}, u32[]{:S(2)}) copy-start(bf16[27,32,128]{2,1,0:T(8,128)(2,1)} %refs_0_.1) | copy-start | bytes 663556
  1.7 4.2 %collective-permute-start = (bf16[96,256]{1,0:T(8,128)(2,1)S(1)}, bf16[96,256]{1,0:T(8,128)(2,1)S(1)}, u32[]{:S(2)}, u32[]{:S(2)}) collective-permute-start(bf16[96,256]{1,0:T(8,128)(2,1)S(1)} %get-tuple-element.32), channel_id=1, source_target_pairs={{0,8},{8,16},{16,24},{24,32},{32,40},{40,48},{48,56},{56,64},{64,7... | collective-permute-start | bytes 147464 | tf_op jit(solution)/shard_map/ppermute | solution.py:411
  5.8 10.4 %collective-permute-start.3 = (bf16[320,256]{1,0:T(8,128)(2,1)S(1)}, bf16[320,256]{1,0:T(8,128)(2,1)S(1)}, u32[]{:S(2)}, u32[]{:S(2)}) collective-permute-start(bf16[320,256]{1,0:T(8,128)(2,1)S(1)} %pad_maximum_fusion.1.refs_3_), channel_id=1, source_target_pairs={{0,2},{1,3},{2,4},{3,5},{4,6},{5,7},{6,0},{7,1},{8,10},{9,11},{10,... | collective-permute-start | bytes 491528 | tf_op jit(solution)/shard_map/ppermute | solution.py:414
  9.2 7.9 %collective-permute-start.4 = (bf16[320,256]{1,0:T(8,128)(2,1)S(1)}, bf16[320,256]{1,0:T(8,128)(2,1)S(1)}, u32[]{:S(2)}, u32[]{:S(2)}) collective-permute-start(bf16[320,256]{1,0:T(8,128)(2,1)S(1)} %pad_maximum_fusion.1.refs_3_), channel_id=1, source_target_pairs={{0,6},{1,7},{2,0},{3,1},{4,2},{5,3},{6,4},{7,5},{8,14},{9,15},{10,... | collective-permute-start | bytes 491528 | tf_op jit(solution)/shard_map/ppermute | solution.py:414
  11.4 14.2 %collective-permute-start.1 = (bf16[32,256]{1,0:T(8,128)(2,1)S(1)}, bf16[32,256]{1,0:T(8,128)(2,1)S(1)}, u32[]{:S(2)}, u32[]{:S(2)}) collective-permute-start(bf16[32,256]{1,0:T(8,128)(2,1)S(1)} %slice.36), channel_id=1, source_target_pairs={{0,248},{8,0},{16,8},{24,16},{32,24},{40,32},{48,40},{56,48},{64,5... | collective-permute-start | bytes 49160 | tf_op jit(solution)/shard_map/ppermute | solution.py:411
  13.8 12.3 %collective-permute-start.2 = (bf16[320,256]{1,0:T(8,128)(2,1)S(1)}, bf16[320,256]{1,0:T(8,128)(2,1)S(1)}, u32[]{:S(2)}, u32[]{:S(2)}) collective-permute-start(bf16[320,256]{1,0:T(8,128)(2,1)S(1)} %pad_maximum_fusion.1.refs_3_), channel_id=1, source_target_pairs={{0,1},{1,0},{2,3},{3,2},{4,5},{5,4},{6,7},{7,6},{8,9},{9,8},{10,11... | collective-permute-start | bytes 491528 | tf_op jit(solution)/shard_map/ppermute | solution.py:419
  16.2 6.6 %collective-permute-start.6 = (bf16[160,256]{1,0:T(8,128)(2,1)S(1)}, bf16[160,256]{1,0:T(8,128)(2,1)S(1)}, u32[]{:S(2)}, u32[]{:S(2)}) collective-permute-start(bf16[160,256]{1,0:T(8,128)(2,1)S(1)} %slice.38), channel_id=1, source_target_pairs={{0,2},{1,3},{2,4},{3,5},{4,6},{5,7},{6,0},{7,1},{8,10},{9,11},{10,... | collective-permute-start | bytes 245768 | tf_op jit(solution)/shard_map/ppermute | solution.py:414
  17.1 8.5 %copy-start.1 = (bf16[27,32,8]{1,2,0:T(8,128)(2,1)S(1)}, bf16[27,32,8]{1,2,0:T(8,128)(2,1)}, u32[]{:S(2)}) copy-start(bf16[27,32,8]{1,2,0:T(8,128)(2,1)} %param.6) | copy-start | bytes 41476
  17.1 8.5 %collective-permute-start.7 = (bf16[160,256]{1,0:T(8,128)(2,1)S(1)}, bf16[160,256]{1,0:T(8,128)(2,1)S(1)}, u32[]{:S(2)}, u32[]{:S(2)}) collective-permute-start(bf16[160,256]{1,0:T(8,128)(2,1)S(1)} %slice.49), channel_id=1, source_target_pairs={{0,6},{1,7},{2,0},{3,1},{4,2},{5,3},{6,4},{7,5},{8,14},{9,15},{10,... | collective-permute-start | bytes 245768 | tf_op jit(solution)/shard_map/ppermute | solution.py:414
  20.5 6.4 %collective-permute-start.5 = (bf16[640,256]{1,0:T(8,128)(2,1)S(1)}, bf16[640,256]{1,0:T(8,128)(2,1)S(1)}, u32[]{:S(2)}, u32[]{:S(2)}) collective-permute-start(bf16[640,256]{1,0:T(8,128)(2,1)S(1)} %pad_maximum_fusion), channel_id=1, source_target_pairs={{0,1},{1,0},{2,3},{3,2},{4,5},{5,4},{6,7},{7,6},{8,9},{9,8},{10,11... | collective-permute-start | bytes 983048 | tf_op jit(solution)/shard_map/ppermute | solution.py:419
  22.8 3.3 %collective-permute-start.8 = (bf16[160,256]{1,0:T(8,128)(2,1)S(1)}, bf16[160,256]{1,0:T(8,128)(2,1)S(1)}, u32[]{:S(2)}, u32[]{:S(2)}) collective-permute-start(bf16[160,256]{1,0:T(8,128)(2,1)S(1)} %collective-permute-done.6.refs_8_), channel_id=1, source_target_pairs={{0,1},{1,0},{2,3},{3,2},{4,5},{5,4},{6,7},{7,6},{8,9},{9,8},{10,11... | collective-permute-start | bytes 245768 | tf_op jit(solution)/shard_map/ppermute | solution.py:419
  25.6 1.3 %collective-permute-start.9 = (bf16[160,256]{1,0:T(8,128)(2,1)S(1)}, bf16[160,256]{1,0:T(8,128)(2,1)S(1)}, u32[]{:S(2)}, u32[]{:S(2)}) collective-permute-start(bf16[160,256]{1,0:T(8,128)(2,1)S(1)} %collective-permute-done.7.refs_9_), channel_id=1, source_target_pairs={{0,1},{1,0},{2,3},{3,2},{4,5},{5,4},{6,7},{7,6},{8,9},{9,8},{10,11... | collective-permute-start | bytes 245768 | tf_op jit(solution)/shard_map/ppermute | solution.py:419
  29.4 17.3 %collective-permute-start.10 = (bf16[192,256]{1,0:T(8,128)(2,1)S(1)}, bf16[192,256]{1,0:T(8,128)(2,1)S(1)}, u32[]{:S(2)}, u32[]{:S(2)}) collective-permute-start(bf16[192,256]{1,0:T(8,128)(2,1)S(1)} %get-tuple-element.62), channel_id=1, source_target_pairs={{0,2},{1,3},{2,4},{3,5},{4,6},{5,7},{6,0},{7,1},{8,10},{9,11},{10,... | collective-permute-start | bytes 294920 | tf_op jit(solution)/shard_map/ppermute | solution.py:414
  33.7 12.9 %collective-permute-start.11 = (bf16[128,256]{1,0:T(8,128)(2,1)S(1)}, bf16[128,256]{1,0:T(8,128)(2,1)S(1)}, u32[]{:S(2)}, u32[]{:S(2)}) collective-permute-start(bf16[128,256]{1,0:T(8,128)(2,1)S(1)} %pad_maximum_fusion.5), channel_id=1, source_target_pairs={{0,1},{1,0},{2,3},{3,2},{4,5},{5,4},{6,7},{7,6},{8,9},{9,8},{10,11... | collective-permute-start | bytes 196616 | tf_op jit(solution)/shard_map/ppermute | solution.py:419
  33.7 12.9 %collective-permute-start.12 = (bf16[192,256]{1,0:T(8,128)(2,1)S(1)}, bf16[192,256]{1,0:T(8,128)(2,1)S(1)}, u32[]{:S(2)}, u32[]{:S(2)}) collective-permute-start(bf16[192,256]{1,0:T(8,128)(2,1)S(1)} %get-tuple-element.61), channel_id=1, source_target_pairs={{0,6},{1,7},{2,0},{3,1},{4,2},{5,3},{6,4},{7,5},{8,14},{9,15},{10,... | collective-permute-start | bytes 294920 | tf_op jit(solution)/shard_map/ppermute | solution.py:414
  33.8 12.9 %collective-permute-start.13 = (bf16[192,256]{1,0:T(8,128)(2,1)S(1)}, bf16[192,256]{1,0:T(8,128)(2,1)S(1)}, u32[]{:S(2)}, u32[]{:S(2)}) collective-permute-start(bf16[192,256]{1,0:T(8,128)(2,1)S(1)} %get-tuple-element.60), channel_id=1, source_target_pairs={{0,4},{1,5},{2,6},{3,7},{4,0},{5,1},{6,2},{7,3},{8,12},{9,13},{10,... | collective-permute-start | bytes 294920 | tf_op jit(solution)/shard_map/ppermute | solution.py:414
  37.5 14.3 %all-to-all-start = ((bf16[32,32,128]{2,1,0:T(8,128)(2,1)}), bf16[32,32,128]{2,1,0:T(8,128)(2,1)S(1)}, u32[]{:S(2)}, u32[]{:S(2)}) async-start(bf16[32,32,128]{2,1,0:T(8,128)(2,1)} %bitcast.3), calls=%async_computation | async-start | bytes 524288 | tf_op jit(solution)/shard_map/all_to_all | solution.py:459
  46.7 1.7 %collective-permute-start.14 = (bf16[384,256]{1,0:T(8,128)(2,1)S(1)}, bf16[384,256]{1,0:T(8,128)(2,1)S(1)}, u32[]{:S(2)}, u32[]{:S(2)}) collective-permute-start(bf16[384,256]{1,0:T(8,128)(2,1)S(1)} %slice_dynamic-update-slice_fusion), channel_id=1, source_target_pairs={{0,1},{1,0},{2,3},{3,2},{4,5},{5,4},{6,7},{7,6},{8,9},{9,8},{10,11... | collective-permute-start | bytes 589832 | tf_op jit(solution)/shard_map/ppermute | solution.py:419
  47.0 3.8 %collective-permute-start.15 = (bf16[32,256]{1,0:T(8,128)(2,1)S(1)}, bf16[32,256]{1,0:T(8,128)(2,1)S(1)}, u32[]{:S(2)}, u32[]{:S(2)}) collective-permute-start(bf16[32,256]{1,0:T(8,128)(2,1)S(1)} %slice.47), channel_id=1, source_target_pairs={{0,8},{8,16},{16,24},{24,32},{32,40},{40,48},{48,56},{56,64},{64,7... | collective-permute-start | bytes 49160 | tf_op jit(solution)/shard_map/ppermute | solution.py:411
  52.6 18.0 %all-to-all-start.1 = ((bf16[32,32,128]{2,1,0:T(8,128)(2,1)}), bf16[32,32,128]{2,1,0:T(8,128)(2,1)S(1)}, u32[]{:S(2)}, u32[]{:S(2)}) async-start(bf16[32,32,128]{2,1,0:T(8,128)(2,1)} %shard_map.81), calls=%async_computation.1 | async-start | bytes 524288 | tf_op jit(solution)/shard_map/all_to_all | solution.py:486
  60.9 8.4 %collective-permute-start.16 = (bf16[96,256]{1,0:T(8,128)(2,1)S(1)}, bf16[96,256]{1,0:T(8,128)(2,1)S(1)}, u32[]{:S(2)}, u32[]{:S(2)}) collective-permute-start(bf16[96,256]{1,0:T(8,128)(2,1)S(1)} %get-tuple-element.53), channel_id=1, source_target_pairs={{0,248},{8,0},{16,8},{24,16},{32,24},{40,32},{48,40},{56,48},{64,5... | collective-permute-start | bytes 147464 | tf_op jit(solution)/shard_map/ppermute | solution.py:411

commit v6 on v4

--- a/solution.py
+++ b/solution.py
@@ -464,8 +464,8 @@
     down = along_chips(joined(hidden_grad, down), -1)
     far = along_chips(joined(hidden_grad, far), 2)
     block = 2 * outputs
-    near = other_core(joined(hidden_grad, here[:block]))
-    up, near = lax.optimization_barrier((up, near))
+    up, lent = lax.optimization_barrier((up, joined(hidden_grad, here[:block])))
+    near = other_core(lent)
     crossed = other_core(
         joined(*[part for ring in (up, down, far) for part in (ring[:block], ring[2 * block :])])
     )

time: 71.9 us -> 71.8 us (level)
  no operation moved by 1% of the time
where the time goes in v6:
time: 71.8 us; the launch traced here: 71.5 us
  starting transfers between devices  40.1 us (56%)
  waiting for transfers between devices  22.5 us (31%)
  Pallas kernels  6.82 us (9%)
  local copies, waits for them, and re-layouts  1.04 us (1%)
  between operations  0.89 us (1%)
    ppermute x7, starting transfers between devices, along_chips(): lax.ppermute(block, 'chan', [(i, (i + 2 * step) % blocks) for i in range(...  17.8 us
    ppermute x4, waiting for transfers between devices, along_space(): lax.ppermute(block, 'space', [(i, (i + step) % slabs) for i in range(slab...  12.6 us
    all_to_all x1, starting transfers between devices, body(): lax.all_to_all(terms.reshape(slabs, rows // slabs, 128), 'space', split_a...  9.05 us
    all_to_all x1, starting transfers between devices, body(): lax.all_to_all(sum_part(received, scale), 'space', split_axis=0, concat_a...  8.25 us
    ppermute x7, waiting for transfers between devices, along_chips(): lax.ppermute(block, 'chan', [(i, (i + 2 * step) % blocks) for i in range(...  7.31 us
    pallas_call x8, Pallas kernels, call(): pl.pallas_call(kernel, out_shape=outs, in_specs=[whole] * len(args), out_...  6.82 us
    ppermute x4, starting transfers between devices, along_space(): lax.ppermute(block, 'space', [(i, (i + step) % slabs) for i in range(slab...  4.18 us
    ppermute x5, waiting for transfers between devices, other_core(): return lax.ppermute(block, 'chan', [(i, i ^ 1) for i in range(blocks)])  1.74 us
  transfers between devices with their start and end apart: 18, of which 9 were waited for; matrix products, arithmetic and copies ran while one was open for 0% of the time, Pallas kernels for 4%

profile of v6, /device:TPU:62, one launch (start us, length us, event | category | flops | bytes accessed | tf_op | source)
XLA Modules:
  0.0 71.5 jit_solution(8885349085695470943)
XLA Ops:
  0.6 1.0 %copy.12 = bf16[16,4,1024]{2,0,1:T(8,128)(2,1)S(1)} copy(bf16[16,4,1024]{2,1,0:T(4,128)(2,1)} %param.4) | data formatting | bytes 262144 | tf_op args[0]
  1.7 1.5 %collective-permute-start = (bf16[96,256]{1,0:T(8,128)(2,1)S(1)}, bf16[96,256]{1,0:T(8,128)(2,1)S(1)}, u32[]{:S(2)}, u32[]{:S(2)}) collective-permute-start(bf16[96,256]{1,0:T(8,128)(2,1)S(1)} %get-tuple-element.32), channel_id=1, source_target_pairs={{0,8},{8,16},{16,24},{24,32},{32,40},{40,48},{48,56},{56,64},{64,7... | collective-permute-start | bytes 147464 | tf_op jit(solution)/shard_map/ppermute | solution.py:411
  3.2 2.7 %collective-permute-done.low_ref = bf16[96,256]{1,0:T(8,128)(2,1)S(1)} collective-permute-done((bf16[96,256]{1,0:T(8,128)(2,1)S(1)}, bf16[96,256]{1,0:T(8,128)(2,1)S(1)}, u32[]{:S(2)}, u32[]{:S(2)}) %collective-permute-start) | collective-permute-done | bytes 49184 | tf_op jit(solution)/shard_map/ppermute | solution.py:411
  5.8 3.3 %collective-permute-start.3 = (bf16[320,256]{1,0:T(8,128)(2,1)S(1)}, bf16[320,256]{1,0:T(8,128)(2,1)S(1)}, u32[]{:S(2)}, u32[]{:S(2)}) collective-permute-start(bf16[320,256]{1,0:T(8,128)(2,1)S(1)} %pad_maximum_fusion.1.refs_3_), channel_id=1, source_target_pairs={{0,2},{1,3},{2,4},{3,5},{4,6},{5,7},{6,0},{7,1},{8,10},{9,11},{10,... | collective-permute-start | bytes 491528 | tf_op jit(solution)/shard_map/ppermute | solution.py:414
  9.2 2.2 %collective-permute-start.4 = (bf16[320,256]{1,0:T(8,128)(2,1)S(1)}, bf16[320,256]{1,0:T(8,128)(2,1)S(1)}, u32[]{:S(2)}, u32[]{:S(2)}) collective-permute-start(bf16[320,256]{1,0:T(8,128)(2,1)S(1)} %pad_maximum_fusion.1.refs_3_), channel_id=1, source_target_pairs={{0,6},{1,7},{2,0},{3,1},{4,2},{5,3},{6,4},{7,5},{8,14},{9,15},{10,... | collective-permute-start | bytes 491528 | tf_op jit(solution)/shard_map/ppermute | solution.py:414
  11.4 1.9 %collective-permute-start.1 = (bf16[32,256]{1,0:T(8,128)(2,1)S(1)}, bf16[32,256]{1,0:T(8,128)(2,1)S(1)}, u32[]{:S(2)}, u32[]{:S(2)}) collective-permute-start(bf16[32,256]{1,0:T(8,128)(2,1)S(1)} %slice.36), channel_id=1, source_target_pairs={{0,248},{8,0},{16,8},{24,16},{32,24},{40,32},{48,40},{56,48},{64,5... | collective-permute-start | bytes 49160 | tf_op jit(solution)/shard_map/ppermute | solution.py:411
  13.3 0.5 shard_map.77
  13.8 0.1 collective-permute-start.2
  13.9 2.3 %collective-permute-done.3.refs_5_ = bf16[320,256]{1,0:T(8,128)(2,1)S(1)} collective-permute-done((bf16[320,256]{1,0:T(8,128)(2,1)S(1)}, bf16[320,256]{1,0:T(8,128)(2,1)S(1)}, u32[]{:S(2)}, u32[]{:S(2)}) %collective-permute-start.3) | collective-permute-done | bytes 163872 | tf_op jit(solution)/shard_map/ppermute | solution.py:414
  16.2 0.9 %collective-permute-start.6 = (bf16[160,256]{1,0:T(8,128)(2,1)S(1)}, bf16[160,256]{1,0:T(8,128)(2,1)S(1)}, u32[]{:S(2)}, u32[]{:S(2)}) collective-permute-start(bf16[160,256]{1,0:T(8,128)(2,1)S(1)} %slice.38), channel_id=1, source_target_pairs={{0,2},{1,3},{2,4},{3,5},{4,6},{5,7},{6,0},{7,1},{8,10},{9,11},{10,... | collective-permute-start | bytes 245768 | tf_op jit(solution)/shard_map/ppermute | solution.py:414
  17.1 3.3 %collective-permute-start.7 = (bf16[160,256]{1,0:T(8,128)(2,1)S(1)}, bf16[160,256]{1,0:T(8,128)(2,1)S(1)}, u32[]{:S(2)}, u32[]{:S(2)}) collective-permute-start(bf16[160,256]{1,0:T(8,128)(2,1)S(1)} %slice.49), channel_id=1, source_target_pairs={{0,6},{1,7},{2,0},{3,1},{4,2},{5,3},{6,4},{7,5},{8,14},{9,15},{10,... | collective-permute-start | bytes 245768 | tf_op jit(solution)/shard_map/ppermute | solution.py:414
  20.6 2.3 %collective-permute-done.6.refs_8_ = bf16[160,256]{1,0:T(8,128)(2,1)S(1)} collective-permute-done((bf16[160,256]{1,0:T(8,128)(2,1)S(1)}, bf16[160,256]{1,0:T(8,128)(2,1)S(1)}, u32[]{:S(2)}, u32[]{:S(2)}) %collective-permute-start.6) | collective-permute-done | bytes 81952 | tf_op jit(solution)/shard_map/ppermute | solution.py:414
  22.8 2.8 %collective-permute-done.7.refs_9_ = bf16[160,256]{1,0:T(8,128)(2,1)S(1)} collective-permute-done((bf16[160,256]{1,0:T(8,128)(2,1)S(1)}, bf16[160,256]{1,0:T(8,128)(2,1)S(1)}, u32[]{:S(2)}, u32[]{:S(2)}) %collective-permute-start.7) | collective-permute-done | bytes 81952 | tf_op jit(solution)/shard_map/ppermute | solution.py:414
  25.6 0.1 collective-permute-start.8
  25.7 0.5 shard_map.76
  26.2 0.9 %collective-permute-done.8.refs_10_ = bf16[320,256]{1,0:T(8,128)(2,1)S(1)} collective-permute-done((bf16[320,256]{1,0:T(8,128)(2,1)S(1)}, bf16[320,256]{1,0:T(8,128)(2,1)S(1)}, u32[]{:S(2)}, u32[]{:S(2)}) %collective-permute-start.8) | collective-permute-done | bytes 163872 | tf_op jit(solution)/shard_map/ppermute | solution.py:419
  27.1 2.4 %shard_map.78 = (bf16[32,512]{1,0:T(8,128)(2,1)S(1)}, bf16[64,256]{1,0:T(8,128)(2,1)S(1)}, bf16[1024,128]{1,0:T(8,128)(2,1)}) custom-call(bf16[27,32,128]{2,1,0:T(8,128)(2,1)S(1)} %copy-done, f32[32,512]{1,0:T(8,128)S(1)} %get-tuple-element.34.refs_1_, bf16[864,512]{1,0:T(8,128)(2,1)S(1)} %get-tuple-element.35.refs_2_, ...), custom_call_target="tpu_custom_call" | custom-call | tf_op jit(solution)/shard_map/pallas_call | solution.py:43
  29.6 4.4 %collective-permute-start.9 = (bf16[192,256]{1,0:T(8,128)(2,1)S(1)}, bf16[192,256]{1,0:T(8,128)(2,1)S(1)}, u32[]{:S(2)}, u32[]{:S(2)}) collective-permute-start(bf16[192,256]{1,0:T(8,128)(2,1)S(1)} %get-tuple-element.62), channel_id=1, source_target_pairs={{0,2},{1,3},{2,4},{3,5},{4,6},{5,7},{6,0},{7,1},{8,10},{9,11},{10,... | collective-permute-start | bytes 294920 | tf_op jit(solution)/shard_map/ppermute | solution.py:414
  33.9 3.7 %collective-permute-start.12 = (bf16[192,256]{1,0:T(8,128)(2,1)S(1)}, bf16[192,256]{1,0:T(8,128)(2,1)S(1)}, u32[]{:S(2)}, u32[]{:S(2)}) collective-permute-start(bf16[192,256]{1,0:T(8,128)(2,1)S(1)} %get-tuple-element.60), channel_id=1, source_target_pairs={{0,4},{1,5},{2,6},{3,7},{4,0},{5,1},{6,2},{7,3},{8,12},{9,13},{10,... | collective-permute-start | bytes 294920 | tf_op jit(solution)/shard_map/ppermute | solution.py:414
  37.6 9.0 %all-to-all-start = ((bf16[32,32,128]{2,1,0:T(8,128)(2,1)}), bf16[32,32,128]{2,1,0:T(8,128)(2,1)S(1)}, u32[]{:S(2)}, u32[]{:S(2)}) async-start(bf16[32,32,128]{2,1,0:T(8,128)(2,1)} %bitcast.3), calls=%async_computation | async-start | bytes 524288 | tf_op jit(solution)/shard_map/all_to_all | solution.py:458
  46.8 0.5 collective-permute-start.10
  47.3 0.1 collective-permute-start.14
  47.5 0.9 %collective-permute-done.10.refs_2_ = bf16[128,256]{1,0:T(8,128)(2,1)S(1)} collective-permute-done((bf16[128,256]{1,0:T(8,128)(2,1)S(1)}, bf16[128,256]{1,0:T(8,128)(2,1)S(1)}, u32[]{:S(2)}, u32[]{:S(2)}) %collective-permute-start.10) | collective-permute-done | bytes 65568 | tf_op jit(solution)/shard_map/ppermute | solution.py:419
  48.4 0.5 shard_map.79
  48.9 2.2 %collective-permute-done.14.low_ref = bf16[32,256]{1,0:T(8,128)(2,1)S(1)} collective-permute-done((bf16[32,256]{1,0:T(8,128)(2,1)S(1)}, bf16[32,256]{1,0:T(8,128)(2,1)S(1)}, u32[]{:S(2)}, u32[]{:S(2)}) %collective-permute-start.14) | collective-permute-done | bytes 16416 | tf_op jit(solution)/shard_map/ppermute | solution.py:411
  51.1 0.8 %all-to-all-done.src = bf16[32,32,128]{2,1,0:T(8,128)(2,1)S(1)} async-done(((bf16[32,32,128]{2,1,0:T(8,128)(2,1)}), bf16[32,32,128]{2,1,0:T(8,128)(2,1)S(1)}, u32[]{:S(2)}, u32[]{:S(2)}) %all-to-all-start) | async-done | bytes 262176 | tf_op jit(solution)/shard_map/all_to_all | solution.py:458
  51.9 0.8 %shard_map.81 = bf16[32,32,128]{2,1,0:T(8,128)(2,1)} custom-call(bf16[32,32,128]{2,1,0:T(8,128)(2,1)S(1)} %all-to-all-done.src), custom_call_target="tpu_custom_call" | custom-call | tf_op jit(solution)/shard_map/pallas_call | solution.py:43
  52.7 8.3 %all-to-all-start.1 = ((bf16[32,32,128]{2,1,0:T(8,128)(2,1)}), bf16[32,32,128]{2,1,0:T(8,128)(2,1)S(1)}, u32[]{:S(2)}, u32[]{:S(2)}) async-start(bf16[32,32,128]{2,1,0:T(8,128)(2,1)} %shard_map.81), calls=%async_computation.1 | async-start | bytes 524288 | tf_op jit(solution)/shard_map/all_to_all | solution.py:485
  60.9 0.6 collective-permute-start.15
  61.6 7.8 %collective-permute-done.15.packed_ref = bf16[96,256]{1,0:T(8,128)(2,1)S(1)} collective-permute-done((bf16[96,256]{1,0:T(8,128)(2,1)S(1)}, bf16[96,256]{1,0:T(8,128)(2,1)S(1)}, u32[]{:S(2)}, u32[]{:S(2)}) %collective-permute-start.15) | collective-permute-done | bytes 49184 | tf_op jit(solution)/shard_map/ppermute | solution.py:411
  69.3 1.3 %shard_map.80 = (bf16[32,2,256]{2,1,0:T(2,128)(2,1)}, f32[16,4,1024]{2,1,0:T(4,128)}) custom-call(bf16[32,256]{1,0:T(8,128)(2,1)S(1)} %collective-permute-done.14.low_ref, bf16[32,512]{1,0:T(8,128)(2,1)S(1)} %get-tuple-element.43.active_ref.mid_ref, bf16[96,256]{1,0:T(8,128)(2,1)S(1)} %collective-permute-done.15.packed_ref, ...), custom_call_target="tpu_custom_call" | custom-call | tf_op jit(solution)/shard_map/pallas_call | solution.py:43
  70.6 0.8 %shard_map.82 = (f32[27,32,128]{2,1,0:T(8,128)}, f32[27,8,32]{2,1,0:T(8,128)}) custom-call(bf16[1024,128]{1,0:T(8,128)(2,1)S(1)} %bitcast.10), custom_call_target="tpu_custom_call" | custom-call | tf_op jit(solution)/shard_map/pallas_call | solution.py:43
  (37 shorter events, 0.4 us)
Async XLA Ops:
  0.6 1.0 %copy-start.2 = (bf16[32,2,256]{2,1,0:T(2,128)(2,1)S(1)}, bf16[32,2,256]{2,1,0:T(2,128)(2,1)}, u32[]{:S(2)}) copy-start(bf16[32,2,256]{2,1,0:T(2,128)(2,1)} %param.7) | copy-start | bytes 98308
  1.6 11.7 %copy-start = (bf16[27,32,128]{2,1,0:T(8,128)(2,1)S(1)}, bf16[27,32,128]{2,1,0:T(8,128)(2,1)}, u32[]{:S(2)}) copy-start(bf16[27,32,128]{2,1,0:T(8,128)(2,1)} %refs_0_.1) | copy-start | bytes 663556
  1.7 4.2 %collective-permute-start = (bf16[96,256]{1,0:T(8,128)(2,1)S(1)}, bf16[96,256]{1,0:T(8,128)(2,1)S(1)}, u32[]{:S(2)}, u32[]{:S(2)}) collective-permute-start(bf16[96,256]{1,0:T(8,128)(2,1)S(1)} %get-tuple-element.32), channel_id=1, source_target_pairs={{0,8},{8,16},{16,24},{24,32},{32,40},{40,48},{48,56},{56,64},{64,7... | collective-permute-start | bytes 147464 | tf_op jit(solution)/shard_map/ppermute | solution.py:411
  5.8 10.4 %collective-permute-start.3 = (bf16[320,256]{1,0:T(8,128)(2,1)S(1)}, bf16[320,256]{1,0:T(8,128)(2,1)S(1)}, u32[]{:S(2)}, u32[]{:S(2)}) collective-permute-start(bf16[320,256]{1,0:T(8,128)(2,1)S(1)} %pad_maximum_fusion.1.refs_3_), channel_id=1, source_target_pairs={{0,2},{1,3},{2,4},{3,5},{4,6},{5,7},{6,0},{7,1},{8,10},{9,11},{10,... | collective-permute-start | bytes 491528 | tf_op jit(solution)/shard_map/ppermute | solution.py:414
  9.2 7.9 %collective-permute-start.4 = (bf16[320,256]{1,0:T(8,128)(2,1)S(1)}, bf16[320,256]{1,0:T(8,128)(2,1)S(1)}, u32[]{:S(2)}, u32[]{:S(2)}) collective-permute-start(bf16[320,256]{1,0:T(8,128)(2,1)S(1)} %pad_maximum_fusion.1.refs_3_), channel_id=1, source_target_pairs={{0,6},{1,7},{2,0},{3,1},{4,2},{5,3},{6,4},{7,5},{8,14},{9,15},{10,... | collective-permute-start | bytes 491528 | tf_op jit(solution)/shard_map/ppermute | solution.py:414
  11.4 14.3 %collective-permute-start.1 = (bf16[32,256]{1,0:T(8,128)(2,1)S(1)}, bf16[32,256]{1,0:T(8,128)(2,1)S(1)}, u32[]{:S(2)}, u32[]{:S(2)}) collective-permute-start(bf16[32,256]{1,0:T(8,128)(2,1)S(1)} %slice.36), channel_id=1, source_target_pairs={{0,248},{8,0},{16,8},{24,16},{32,24},{40,32},{48,40},{56,48},{64,5... | collective-permute-start | bytes 49160 | tf_op jit(solution)/shard_map/ppermute | solution.py:411
  13.8 12.4 %collective-permute-start.2 = (bf16[320,256]{1,0:T(8,128)(2,1)S(1)}, bf16[320,256]{1,0:T(8,128)(2,1)S(1)}, u32[]{:S(2)}, u32[]{:S(2)}) collective-permute-start(bf16[320,256]{1,0:T(8,128)(2,1)S(1)} %pad_maximum_fusion.1.refs_3_), channel_id=1, source_target_pairs={{0,1},{1,0},{2,3},{3,2},{4,5},{5,4},{6,7},{7,6},{8,9},{9,8},{10,11... | collective-permute-start | bytes 491528 | tf_op jit(solution)/shard_map/ppermute | solution.py:419
  16.2 6.6 %collective-permute-start.6 = (bf16[160,256]{1,0:T(8,128)(2,1)S(1)}, bf16[160,256]{1,0:T(8,128)(2,1)S(1)}, u32[]{:S(2)}, u32[]{:S(2)}) collective-permute-start(bf16[160,256]{1,0:T(8,128)(2,1)S(1)} %slice.38), channel_id=1, source_target_pairs={{0,2},{1,3},{2,4},{3,5},{4,6},{5,7},{6,0},{7,1},{8,10},{9,11},{10,... | collective-permute-start | bytes 245768 | tf_op jit(solution)/shard_map/ppermute | solution.py:414
  17.1 8.5 %collective-permute-start.7 = (bf16[160,256]{1,0:T(8,128)(2,1)S(1)}, bf16[160,256]{1,0:T(8,128)(2,1)S(1)}, u32[]{:S(2)}, u32[]{:S(2)}) collective-permute-start(bf16[160,256]{1,0:T(8,128)(2,1)S(1)} %slice.49), channel_id=1, source_target_pairs={{0,6},{1,7},{2,0},{3,1},{4,2},{5,3},{6,4},{7,5},{8,14},{9,15},{10,... | collective-permute-start | bytes 245768 | tf_op jit(solution)/shard_map/ppermute | solution.py:414
  20.5 5.3 %copy-start.1 = (bf16[27,32,8]{1,2,0:T(8,128)(2,1)S(1)}, bf16[27,32,8]{1,2,0:T(8,128)(2,1)}, u32[]{:S(2)}) copy-start(bf16[27,32,8]{1,2,0:T(8,128)(2,1)} %param.6) | copy-start | bytes 41476
  20.5 6.6 %collective-permute-start.5 = (bf16[640,256]{1,0:T(8,128)(2,1)S(1)}, bf16[640,256]{1,0:T(8,128)(2,1)S(1)}, u32[]{:S(2)}, u32[]{:S(2)}) collective-permute-start(bf16[640,256]{1,0:T(8,128)(2,1)S(1)} %pad_maximum_fusion), channel_id=1, source_target_pairs={{0,1},{1,0},{2,3},{3,2},{4,5},{5,4},{6,7},{7,6},{8,9},{9,8},{10,11... | collective-permute-start | bytes 983048 | tf_op jit(solution)/shard_map/ppermute | solution.py:419
  25.6 1.5 %collective-permute-start.8 = (bf16[320,256]{1,0:T(8,128)(2,1)S(1)}, bf16[320,256]{1,0:T(8,128)(2,1)S(1)}, u32[]{:S(2)}, u32[]{:S(2)}) collective-permute-start(bf16[320,256]{1,0:T(8,128)(2,1)S(1)} %pad_maximum_fusion.2), channel_id=1, source_target_pairs={{0,1},{1,0},{2,3},{3,2},{4,5},{5,4},{6,7},{7,6},{8,9},{9,8},{10,11... | collective-permute-start | bytes 491528 | tf_op jit(solution)/shard_map/ppermute | solution.py:419
  29.6 17.1 %collective-permute-start.9 = (bf16[192,256]{1,0:T(8,128)(2,1)S(1)}, bf16[192,256]{1,0:T(8,128)(2,1)S(1)}, u32[]{:S(2)}, u32[]{:S(2)}) collective-permute-start(bf16[192,256]{1,0:T(8,128)(2,1)S(1)} %get-tuple-element.62), channel_id=1, source_target_pairs={{0,2},{1,3},{2,4},{3,5},{4,6},{5,7},{6,0},{7,1},{8,10},{9,11},{10,... | collective-permute-start | bytes 294920 | tf_op jit(solution)/shard_map/ppermute | solution.py:414
  33.9 12.8 %collective-permute-start.11 = (bf16[192,256]{1,0:T(8,128)(2,1)S(1)}, bf16[192,256]{1,0:T(8,128)(2,1)S(1)}, u32[]{:S(2)}, u32[]{:S(2)}) collective-permute-start(bf16[192,256]{1,0:T(8,128)(2,1)S(1)} %get-tuple-element.61), channel_id=1, source_target_pairs={{0,6},{1,7},{2,0},{3,1},{4,2},{5,3},{6,4},{7,5},{8,14},{9,15},{10,... | collective-permute-start | bytes 294920 | tf_op jit(solution)/shard_map/ppermute | solution.py:414
  33.9 12.8 %collective-permute-start.12 = (bf16[192,256]{1,0:T(8,128)(2,1)S(1)}, bf16[192,256]{1,0:T(8,128)(2,1)S(1)}, u32[]{:S(2)}, u32[]{:S(2)}) collective-permute-start(bf16[192,256]{1,0:T(8,128)(2,1)S(1)} %get-tuple-element.60), channel_id=1, source_target_pairs={{0,4},{1,5},{2,6},{3,7},{4,0},{5,1},{6,2},{7,3},{8,12},{9,13},{10,... | collective-permute-start | bytes 294920 | tf_op jit(solution)/shard_map/ppermute | solution.py:414
  37.6 14.3 %all-to-all-start = ((bf16[32,32,128]{2,1,0:T(8,128)(2,1)}), bf16[32,32,128]{2,1,0:T(8,128)(2,1)S(1)}, u32[]{:S(2)}, u32[]{:S(2)}) async-start(bf16[32,32,128]{2,1,0:T(8,128)(2,1)} %bitcast.3), calls=%async_computation | async-start | bytes 524288 | tf_op jit(solution)/shard_map/all_to_all | solution.py:458
  46.7 1.6 %collective-permute-start.13 = (bf16[384,256]{1,0:T(8,128)(2,1)S(1)}, bf16[384,256]{1,0:T(8,128)(2,1)S(1)}, u32[]{:S(2)}, u32[]{:S(2)}) collective-permute-start(bf16[384,256]{1,0:T(8,128)(2,1)S(1)} %slice_dynamic-update-slice_fusion), channel_id=1, source_target_pairs={{0,1},{1,0},{2,3},{3,2},{4,5},{5,4},{6,7},{7,6},{8,9},{9,8},{10,11... | collective-permute-start | bytes 589832 | tf_op jit(solution)/shard_map/ppermute | solution.py:419
  46.8 1.5 %collective-permute-start.10 = (bf16[128,256]{1,0:T(8,128)(2,1)S(1)}, bf16[128,256]{1,0:T(8,128)(2,1)S(1)}, u32[]{:S(2)}, u32[]{:S(2)}) collective-permute-start(bf16[128,256]{1,0:T(8,128)(2,1)S(1)} %pad_maximum_fusion.6), channel_id=1, source_target_pairs={{0,1},{1,0},{2,3},{3,2},{4,5},{5,4},{6,7},{7,6},{8,9},{9,8},{10,11... | collective-permute-start | bytes 196616 | tf_op jit(solution)/shard_map/ppermute | solution.py:419
  47.3 3.7 %collective-permute-start.14 = (bf16[32,256]{1,0:T(8,128)(2,1)S(1)}, bf16[32,256]{1,0:T(8,128)(2,1)S(1)}, u32[]{:S(2)}, u32[]{:S(2)}) collective-permute-start(bf16[32,256]{1,0:T(8,128)(2,1)S(1)} %slice.47), channel_id=1, source_target_pairs={{0,8},{8,16},{16,24},{24,32},{32,40},{40,48},{48,56},{56,64},{64,7... | collective-permute-start | bytes 49160 | tf_op jit(solution)/shard_map/ppermute | solution.py:411
  52.7 18.0 %all-to-all-start.1 = ((bf16[32,32,128]{2,1,0:T(8,128)(2,1)}), bf16[32,32,128]{2,1,0:T(8,128)(2,1)S(1)}, u32[]{:S(2)}, u32[]{:S(2)}) async-start(bf16[32,32,128]{2,1,0:T(8,128)(2,1)} %shard_map.81), calls=%async_computation.1 | async-start | bytes 524288 | tf_op jit(solution)/shard_map/all_to_all | solution.py:485
  60.9 8.4 %collective-permute-start.15 = (bf16[96,256]{1,0:T(8,128)(2,1)S(1)}, bf16[96,256]{1,0:T(8,128)(2,1)S(1)}, u32[]{:S(2)}, u32[]{:S(2)}) collective-permute-start(bf16[96,256]{1,0:T(8,128)(2,1)S(1)} %get-tuple-element.53), channel_id=1, source_target_pairs={{0,248},{8,0},{16,8},{24,16},{32,24},{40,32},{48,40},{56,48},{64,5... | collective-permute-start | bytes 147464 | tf_op jit(solution)/shard_map/ppermute | solution.py:411
